TPU v7x, 32 devices: a whole 2x2x4 slice. The times are simulated.
32 devices in a mesh: groups: 2 (over y), gx: 4 (over x, core), gy: 4 (over z).
Axes of the slice: x: 2, y: 2, z: 4, core: 2. Of those that a mesh axis runs over, the one named last changes fastest.
Arguments:
- layer_class: int32 [64, 64, 128], P(('groups', 'gx'), 'gy'), parts along dimension 0, may hold values from 0 to 5
- permittivity: float32 [6], replicated, may hold values from 2 to 8
- mobility: float32 [6], replicated, may hold values from 0.1 to 10
- capture: float32 [6], replicated, may hold values from 0.02 to 0.4
- potential: float32 [64, 64, 128], P(('groups', 'gx'), 'gy'), parts along dimension 0, may hold values from -2.4 to 2.4
- rhs_psi: float32 [64, 64, 128], P(('groups', 'gx'), 'gy'), parts along dimension 0, may hold values from -48 to 48
- rhs_n: float32 [64, 64, 128], P(('groups', 'gx'), 'gy'), parts along dimension 0, may hold values from -24 to 24
Outputs:
- potential_update: float32 [64, 64, 128], P(('groups', 'gx'), 'gy'), parts along dimension 0
- density_update: float32 [64, 64, 128], P(('groups', 'gx'), 'gy'), parts along dimension 0
There are 2 independent parts, one for each index of `groups`. A program takes and returns all parts, laid end to end along the dimension named above; an argument that names none is the same for every part. Nothing has to cross between parts.
All inputs are finite; a program needn't handle non-finite values.
Results may differ from a plain program's by a relative error of at most 0.0003.
Values sent between devices are 32-bit elements; how exact they have to be, the bound alone decides.
No kernel may reach another device: no remote copies, remote signals or barrier semaphores. Data moves between devices by JAX's collectives and lax.ppermute only.
A program may use at most 64 MiB of HBM per device.

v0:
```python
import jax
import jax.numpy as jnp
from jax import lax
from jax.sharding import PartitionSpec as P

LEVELS = 4
COARSE_ITERS = 20


OMEGA = 0.8


def extended(shard, sides, width):
    for axis, dim in sides:
        count, length = (lax.axis_size(axis), shard.shape[dim])
        up = [(i, (i + 1) % count) for i in range(count - 1)]
        down = [(j, i) for i, j in up]
        last = lax.slice_in_dim(shard, length - width, length, axis=dim)
        leading = lax.slice_in_dim(shard, 0, width, axis=dim)
        before = lax.ppermute(last, axis, up)
        after = lax.ppermute(leading, axis, down)
        shard = jnp.concatenate([before, shard, after], axis=dim)
    return shard


def bernoulli(values):
    nearly_zero = jnp.abs(values) < 0.001
    guarded = jnp.where(nearly_zero, 1.0, values)
    return jnp.where(
        nearly_zero, 1.0 - 0.5 * values + values * values / 12.0, guarded / jnp.expm1(guarded)
    )


def neighbours(array):
    center = array[..., 1:-1, 1:-1, :]
    pad_widths = [(0, 0)] * (array.ndim - 1) + [(1, 1)]
    vertical = jnp.pad(center, pad_widths)
    return (
        center,
        [
            array[..., 2:, 1:-1, :],
            array[..., :-2, 1:-1, :],
            array[..., 1:-1, 2:, :],
            array[..., 1:-1, :-2, :],
            vertical[..., 2:],
            vertical[..., :-2],
        ],
    )


def assemble_operator(coefficients, factor):
    center, beside = neighbours(coefficients)
    diag_poisson = jnp.zeros_like(center[0])
    diag_density = center[3]
    couplings = []
    for other in beside:
        conduct = 0.5 * (center[0] + other[0]) * factor
        motion = 0.5 * (center[1] + other[1]) * factor
        gradient = other[2] - center[2]
        diag_poisson = diag_poisson + conduct
        diag_density = diag_density + motion * bernoulli(-gradient)
        couplings.append(jnp.stack([conduct, motion * bernoulli(gradient)]))
    return (jnp.stack([diag_poisson, diag_density]), jnp.stack(couplings))


def apply_operator(operator, field):
    diagonal, couplings = operator
    center, beside = neighbours(field)
    result = diagonal * center
    for position in range(6):
        result = result - couplings[position] * beside[position]
    return result


def jacobi_sweep(operator, field, source):
    center = field[..., 1:-1, 1:-1, :]
    return center + OMEGA * (source - apply_operator(operator, field)) / operator[0]


def pad_lateral(array):
    return jnp.pad(array, [(0, 0)] * (array.ndim - 3) + [(1, 1), (1, 1), (0, 0)])


def restrict_mean(array):
    leading = array.shape[:-3]
    rows, columns, layers = (array.shape[-3], array.shape[-2], array.shape[-1])
    blocks = array.reshape(leading + (rows // 2, 2, columns // 2, 2, layers // 2, 2))
    return jnp.sum(blocks, axis=(-5, -3, -1)) * 0.125


def prolong(array):
    return jnp.repeat(jnp.repeat(jnp.repeat(array, 2, axis=-3), 2, axis=-2), 2, axis=-1)


def material_fields(layer_class, permittivity, mobility, capture, potential):
    classes = jnp.arange(permittivity.shape[0], dtype=jnp.int32)
    same_class = layer_class[None] == classes[:, None, None, None]

    def select_table(table):
        return jnp.sum(jnp.where(same_class, table[:, None, None, None], 0.0), axis=0)

    return jnp.stack(
        [select_table(permittivity), select_table(mobility), potential, select_table(capture)]
    )


def exchange_rims(field):
    return extended(field, (("gx", 1), ("gy", 2)), 1)


def gather_blocks(gathered):
    devices_x = lax.axis_size("gx")
    devices_y = lax.axis_size("gy")
    count, channels, rows, columns, layers = gathered.shape
    arranged = gathered.reshape(devices_x, devices_y, channels, rows, columns, layers)
    arranged = jnp.transpose(arranged, (2, 0, 3, 1, 4, 5))
    return arranged.reshape(channels, devices_x * rows, devices_y * columns, layers)


def coarse_solve(local, source, factor):
    whole = gather_blocks(lax.all_gather(local[None], ("gx", "gy"), axis=0, tiled=True))
    whole_source = gather_blocks(lax.all_gather(source[None], ("gx", "gy"), axis=0, tiled=True))
    operator = assemble_operator(pad_lateral(whole), factor)
    iterate = OMEGA * whole_source / operator[0]
    iterate = lax.fori_loop(
        0,
        COARSE_ITERS - 1,
        lambda counter, current: jacobi_sweep(operator, pad_lateral(current), whole_source),
        iterate,
    )
    rows, columns = (source.shape[1], source.shape[2])
    return lax.dynamic_slice(
        iterate, (0, lax.axis_index("gx") * rows, lax.axis_index("gy") * columns, 0), source.shape
    )


def per_device(layer_class, permittivity, mobility, capture, potential, rhs_psi, rhs_n):
    hierarchy = [material_fields(layer_class, permittivity, mobility, capture, potential)]
    for grid_level in range(1, LEVELS):
        hierarchy.append(restrict_mean(hierarchy[-1]))

    def descend(grid_level, source):
        factor = 0.25**grid_level
        local = hierarchy[grid_level]
        if grid_level == LEVELS - 1:
            return coarse_solve(local, source, factor)
        coef_rim = extended(local, (("gx", 1), ("gy", 2)), 1)
        operator = assemble_operator(coef_rim, factor)
        iterate = OMEGA * source / operator[0]
        iterate = jacobi_sweep(operator, exchange_rims(iterate), source)
        residual = source - apply_operator(operator, exchange_rims(iterate))
        iterate = iterate + prolong(descend(grid_level + 1, restrict_mean(residual)))
        for iteration in range(2):
            iterate = jacobi_sweep(operator, exchange_rims(iterate), source)
        return iterate

    result = descend(0, jnp.stack([rhs_psi, rhs_n]))
    return (result[0], result[1])


def solution(mesh):
    in_specs = (
        P(("groups", "gx"), "gy", None),
        P(),
        P(),
        P(),
        P(("groups", "gx"), "gy", None),
        P(("groups", "gx"), "gy", None),
        P(("groups", "gx"), "gy", None),
    )
    out_specs = (P(("groups", "gx"), "gy", None), P(("groups", "gx"), "gy", None))
    return jax.shard_map(
        per_device, mesh=mesh, in_specs=in_specs, out_specs=out_specs, check_vma=False
    )
```

profile of v0, /device:TPU:1, one launch (start us, length us, event | category | flops | bytes accessed | tf_op | source)
XLA Modules:
  0.0 324.5 jit_solution(7951785363222572838)
XLA Ops:
  1.7 5.7 %stack.208 = f32[1,4,2,8,2,64,2]{6,5,4,3,2,1,0:T(8,128)} reshape(f32[8,16,128]{2,1,0:T(8,128)S(1)} %get-tuple-element.140) | data formatting | bytes 131072 | tf_op jit(solution)/shard_map/stack | solution.py:102
  7.4 5.5 %stack.207 = f32[1,4,2,8,2,64,2]{6,5,4,3,2,1,0:T(8,128)} reshape(f32[8,16,128]{2,1,0:T(8,128)S(1)} %get-tuple-element.138) | data formatting | bytes 131072 | tf_op jit(solution)/shard_map/stack | solution.py:102
  12.9 5.6 %stack.210 = f32[1,4,2,8,2,64,2]{6,5,4,3,2,1,0:T(8,128)} reshape(f32[8,16,128]{2,1,0:T(8,128)S(1)} %get-tuple-element.139) | data formatting | bytes 131072 | tf_op jit(solution)/shard_map/stack | solution.py:102
  18.4 5.6 %stack.209 = f32[1,4,2,8,2,64,2]{6,5,4,3,2,1,0:T(8,128)} reshape(f32[8,16,128]{2,1,0:T(8,128)S(1)} %copy-done) | data formatting | bytes 131072 | tf_op jit(solution)/shard_map/stack | solution.py:102
  24.0 6.7 %maximum_reduce_fusion = f32[4,4,8,64]{3,2,1,0:T(8,128)S(1)} fusion(f32[1,4,2,8,2,64,2]{6,5,4,3,2,1,0:T(8,128)} %stack.210, f32[1,4,2,8,2,64,2]{6,5,4,3,2,1,0:T(8,128)} %stack.209, f32[1,4,2,8,2,64,2]{6,5,4,3,2,1,0:T(8,128)} %stack.208, f32[1,4,2,8,2,64,2]{6,5,4,3,2,1,0:T(8,128)} %stack.207), kind=kLoop, calls=%fused_computation.18 | loop fusion | flops 253952 | bytes 294912 | tf_op jit(solution)/shard_map/reduce_sum | solution.py:88
  46.3 28.9 %all-gather.1 = f32[64,2,16]{2,1,0:T(2,128)S(1)} all-gather(f32[4,2,16]{2,1,0:T(2,128)S(1)} %copy.725), channel_id=3, replica_groups=mesh['groups'=2,'gx'=4,'gy'=4] {'gx','gy'}, dimensions={0}, use_global_device_ids=true | all-gather | bytes 8704 | tf_op jit(solution)/shard_map/all_gather | solution.py:121
  75.6 6.8 %collective-permute-start.1 = (f32[4,1,16,128]{3,2,1,0:T(8,128)S(1)}, f32[4,1,16,128]{3,2,1,0:T(8,128)S(1)}, u32[]{:S(2)}, u32[]{:S(2)}) collective-permute-start(f32[4,1,16,128]{3,2,1,0:T(8,128)S(1)} %get-tuple-element.230), channel_id=1, source_target_pairs={{0,4},{4,8},{8,12},{1,5},{5,9},{9,13},{2,6},{6,10},{10,14},{3,7},{... | collective-permute-start | bytes 98312 | tf_op jit(solution)/shard_map/ppermute | solution.py:20
  85.1 4.6 %collective-permute-start.27 = (f32[4,4,1,32]{3,2,1,0:T(1,128)S(1)}, f32[4,4,1,32]{3,2,1,0:T(1,128)S(1)}, u32[]{:S(2)}, u32[]{:S(2)}) collective-permute-start(f32[4,4,1,32]{3,2,1,0:T(1,128)S(1)} %get-tuple-element.296), channel_id=1, source_target_pairs={{0,1},{1,2},{2,3},{4,5},{5,6},{6,7},{8,9},{9,10},{10,11},{12,13},{... | collective-permute-start | bytes 6152 | tf_op jit(solution)/shard_map/ppermute | solution.py:20
  108.4 4.6 %collective-permute-start.7 = (f32[2,10,1,128]{3,0,2,1:T(2,128)S(1)}, f32[2,10,1,128]{3,0,2,1:T(2,128)S(1)}, u32[]{:S(2)}, u32[]{:S(2)}) collective-permute-start(f32[2,10,1,128]{3,0,2,1:T(2,128)S(1)} %copy.707), channel_id=1, source_target_pairs={{0,1},{1,2},{2,3},{4,5},{5,6},{6,7},{8,9},{9,10},{10,11},{12,13},{... | collective-permute-start | bytes 30728 | tf_op jit(solution)/shard_map/ppermute | solution.py:20
  115.9 5.1 %collective-permute-start.9 = (f32[2,1,16,128]{3,2,1,0:T(8,128)S(1)}, f32[2,1,16,128]{3,2,1,0:T(8,128)S(1)}, u32[]{:S(2)}, u32[]{:S(2)}) collective-permute-start(f32[2,1,16,128]{3,2,1,0:T(8,128)S(1)} %get-tuple-element.246), channel_id=1, source_target_pairs={{0,4},{4,8},{8,12},{1,5},{5,9},{9,13},{2,6},{6,10},{10,14},{3,7},{... | collective-permute-start | bytes 49160 | tf_op jit(solution)/shard_map/ppermute | solution.py:20
  123.1 4.7 %collective-permute-start.11 = (f32[2,10,1,128]{3,0,2,1:T(2,128)S(1)}, f32[2,10,1,128]{3,0,2,1:T(2,128)S(1)}, u32[]{:S(2)}, u32[]{:S(2)}) collective-permute-start(f32[2,10,1,128]{3,0,2,1:T(2,128)S(1)} %copy.711), channel_id=1, source_target_pairs={{0,1},{1,2},{2,3},{4,5},{5,6},{6,7},{8,9},{9,10},{10,11},{12,13},{... | collective-permute-start | bytes 30728 | tf_op jit(solution)/shard_map/ppermute | solution.py:20
  128.7 9.8 %reshape.131 = f32[2,4,2,8,2,64,2]{6,5,4,3,2,1,0:T(8,128)} reshape(f32[2,8,16,128]{3,2,1,0:T(8,128)S(1)} %fusion.25) | data formatting | bytes 262144 | tf_op jit(solution)/shard_map/reshape | solution.py:87
  144.4 5.1 %collective-permute-start.17 = (f32[2,1,8,64]{3,2,1,0:T(8,128)S(1)}, f32[2,1,8,64]{3,2,1,0:T(8,128)S(1)}, u32[]{:S(2)}, u32[]{:S(2)}) collective-permute-start(f32[2,1,8,64]{3,2,1,0:T(8,128)S(1)} %get-tuple-element.299), channel_id=1, source_target_pairs={{0,4},{4,8},{8,12},{1,5},{5,9},{9,13},{2,6},{6,10},{10,14},{3,7},{... | collective-permute-start | bytes 12296 | tf_op jit(solution)/shard_map/ppermute | solution.py:20
  151.6 4.5 %collective-permute-start.19 = (f32[2,6,1,64]{3,2,1,0:T(1,128)S(1)}, f32[2,6,1,64]{3,2,1,0:T(1,128)S(1)}, u32[]{:S(2)}, u32[]{:S(2)}) collective-permute-start(f32[2,6,1,64]{3,2,1,0:T(1,128)S(1)} %get-tuple-element.288), channel_id=1, source_target_pairs={{0,1},{1,2},{2,3},{4,5},{5,6},{6,7},{8,9},{9,10},{10,11},{12,13},{... | collective-permute-start | bytes 9224 | tf_op jit(solution)/shard_map/ppermute | solution.py:20
  158.9 5.0 %collective-permute-start.21 = (f32[2,1,8,64]{3,2,1,0:T(8,128)S(1)}, f32[2,1,8,64]{3,2,1,0:T(8,128)S(1)}, u32[]{:S(2)}, u32[]{:S(2)}) collective-permute-start(f32[2,1,8,64]{3,2,1,0:T(8,128)S(1)} %get-tuple-element.297), channel_id=1, source_target_pairs={{0,4},{4,8},{8,12},{1,5},{5,9},{9,13},{2,6},{6,10},{10,14},{3,7},{... | collective-permute-start | bytes 12296 | tf_op jit(solution)/shard_map/ppermute | solution.py:20
  166.0 4.5 %collective-permute-start.23 = (f32[2,6,1,64]{3,2,1,0:T(1,128)S(1)}, f32[2,6,1,64]{3,2,1,0:T(1,128)S(1)}, u32[]{:S(2)}, u32[]{:S(2)}) collective-permute-start(f32[2,6,1,64]{3,2,1,0:T(1,128)S(1)} %get-tuple-element.286), channel_id=1, source_target_pairs={{0,1},{1,2},{2,3},{4,5},{5,6},{6,7},{8,9},{9,10},{10,11},{12,13},{... | collective-permute-start | bytes 9224 | tf_op jit(solution)/shard_map/ppermute | solution.py:20
  174.6 5.0 %collective-permute-start.29 = (f32[2,1,4,32]{3,2,1,0:T(4,128)S(1)}, f32[2,1,4,32]{3,2,1,0:T(4,128)S(1)}, u32[]{:S(2)}, u32[]{:S(2)}) collective-permute-start(f32[2,1,4,32]{3,2,1,0:T(4,128)S(1)} %get-tuple-element.327), channel_id=1, source_target_pairs={{0,4},{4,8},{8,12},{1,5},{5,9},{9,13},{2,6},{6,10},{10,14},{3,7},{... | collective-permute-start | bytes 3080 | tf_op jit(solution)/shard_map/ppermute | solution.py:20
  181.7 4.5 %collective-permute-start.31 = (f32[2,4,1,32]{3,2,1,0:T(1,128)S(1)}, f32[2,4,1,32]{3,2,1,0:T(1,128)S(1)}, u32[]{:S(2)}, u32[]{:S(2)}) collective-permute-start(f32[2,4,1,32]{3,2,1,0:T(1,128)S(1)} %get-tuple-element.318), channel_id=1, source_target_pairs={{0,1},{1,2},{2,3},{4,5},{5,6},{6,7},{8,9},{9,10},{10,11},{12,13},{... | collective-permute-start | bytes 3080 | tf_op jit(solution)/shard_map/ppermute | solution.py:20
  189.0 5.0 %collective-permute-start.33 = (f32[2,1,4,32]{3,2,1,0:T(4,128)S(1)}, f32[2,1,4,32]{3,2,1,0:T(4,128)S(1)}, u32[]{:S(2)}, u32[]{:S(2)}) collective-permute-start(f32[2,1,4,32]{3,2,1,0:T(4,128)S(1)} %get-tuple-element.325), channel_id=1, source_target_pairs={{0,4},{4,8},{8,12},{1,5},{5,9},{9,13},{2,6},{6,10},{10,14},{3,7},{... | collective-permute-start | bytes 3080 | tf_op jit(solution)/shard_map/ppermute | solution.py:20
  196.1 4.5 %collective-permute-start.35 = (f32[2,4,1,32]{3,2,1,0:T(1,128)S(1)}, f32[2,4,1,32]{3,2,1,0:T(1,128)S(1)}, u32[]{:S(2)}, u32[]{:S(2)}) collective-permute-start(f32[2,4,1,32]{3,2,1,0:T(1,128)S(1)} %get-tuple-element.314), channel_id=1, source_target_pairs={{0,1},{1,2},{2,3},{4,5},{5,6},{6,7},{8,9},{9,10},{10,11},{12,13},{... | collective-permute-start | bytes 3080 | tf_op jit(solution)/shard_map/ppermute | solution.py:20
  201.8 30.1 %all-gather = f32[32,2,16]{2,1,0:T(2,128)S(1)} all-gather(f32[2,2,16]{2,1,0:T(2,128)S(1)} %broadcast_multiply_fusion.3), channel_id=2, replica_groups=mesh['groups'=2,'gx'=4,'gy'=4] {'gx','gy'}, dimensions={0}, use_global_device_ids=true | all-gather | bytes 4352 | tf_op jit(solution)/shard_map/all_gather | solution.py:122
  234.6 5.4 %collective-permute-start.36 = (f32[2,1,4,32]{3,2,1,0:T(4,128)S(1)}, f32[2,1,4,32]{3,2,1,0:T(4,128)S(1)}, u32[]{:S(2)}, u32[]{:S(2)}) collective-permute-start(f32[2,1,4,32]{3,2,1,0:T(4,128)S(1)} %get-tuple-element.324), channel_id=1, source_target_pairs={{4,0},{8,4},{12,8},{5,1},{9,5},{13,9},{6,2},{10,6},{14,10},{7,3},{... | collective-permute-start | bytes 3080 | tf_op jit(solution)/shard_map/ppermute | solution.py:21
  252.4 4.5 %collective-permute-start.41 = (f32[2,1,4,32]{3,2,1,0:T(4,128)S(1)}, f32[2,1,4,32]{3,2,1,0:T(4,128)S(1)}, u32[]{:S(2)}, u32[]{:S(2)}) collective-permute-start(f32[2,1,4,32]{3,2,1,0:T(4,128)S(1)} %get-tuple-element.321), channel_id=1, source_target_pairs={{0,4},{4,8},{8,12},{1,5},{5,9},{9,13},{2,6},{6,10},{10,14},{3,7},{... | collective-permute-start | bytes 3080 | tf_op jit(solution)/shard_map/ppermute | solution.py:20
  258.9 4.5 %collective-permute-start.43 = (f32[2,4,1,32]{3,2,1,0:T(1,128)S(1)}, f32[2,4,1,32]{3,2,1,0:T(1,128)S(1)}, u32[]{:S(2)}, u32[]{:S(2)}) collective-permute-start(f32[2,4,1,32]{3,2,1,0:T(1,128)S(1)} %get-tuple-element.308), channel_id=1, source_target_pairs={{0,1},{1,2},{2,3},{4,5},{5,6},{6,7},{8,9},{9,10},{10,11},{12,13},{... | collective-permute-start | bytes 3080 | tf_op jit(solution)/shard_map/ppermute | solution.py:20
  266.5 5.0 %collective-permute-start.45 = (f32[2,1,8,64]{3,2,1,0:T(8,128)S(1)}, f32[2,1,8,64]{3,2,1,0:T(8,128)S(1)}, u32[]{:S(2)}, u32[]{:S(2)}) collective-permute-start(f32[2,1,8,64]{3,2,1,0:T(8,128)S(1)} %get-tuple-element.291), channel_id=1, source_target_pairs={{0,4},{4,8},{8,12},{1,5},{5,9},{9,13},{2,6},{6,10},{10,14},{3,7},{... | collective-permute-start | bytes 12296 | tf_op jit(solution)/shard_map/ppermute | solution.py:20
  273.7 4.5 %collective-permute-start.47 = (f32[2,6,1,64]{3,2,1,0:T(1,128)S(1)}, f32[2,6,1,64]{3,2,1,0:T(1,128)S(1)}, u32[]{:S(2)}, u32[]{:S(2)}) collective-permute-start(f32[2,6,1,64]{3,2,1,0:T(1,128)S(1)} %get-tuple-element.284), channel_id=1, source_target_pairs={{0,1},{1,2},{2,3},{4,5},{5,6},{6,7},{8,9},{9,10},{10,11},{12,13},{... | collective-permute-start | bytes 9224 | tf_op jit(solution)/shard_map/ppermute | solution.py:20
  281.0 5.0 %collective-permute-start.49 = (f32[2,1,8,64]{3,2,1,0:T(8,128)S(1)}, f32[2,1,8,64]{3,2,1,0:T(8,128)S(1)}, u32[]{:S(2)}, u32[]{:S(2)}) collective-permute-start(f32[2,1,8,64]{3,2,1,0:T(8,128)S(1)} %get-tuple-element.289), channel_id=1, source_target_pairs={{0,4},{4,8},{8,12},{1,5},{5,9},{9,13},{2,6},{6,10},{10,14},{3,7},{... | collective-permute-start | bytes 12296 | tf_op jit(solution)/shard_map/ppermute | solution.py:20
  288.2 4.5 %collective-permute-start.51 = (f32[2,6,1,64]{3,2,1,0:T(1,128)S(1)}, f32[2,6,1,64]{3,2,1,0:T(1,128)S(1)}, u32[]{:S(2)}, u32[]{:S(2)}) collective-permute-start(f32[2,6,1,64]{3,2,1,0:T(1,128)S(1)} %get-tuple-element.282), channel_id=1, source_target_pairs={{0,1},{1,2},{2,3},{4,5},{5,6},{6,7},{8,9},{9,10},{10,11},{12,13},{... | collective-permute-start | bytes 9224 | tf_op jit(solution)/shard_map/ppermute | solution.py:20
  296.4 5.0 %collective-permute-start.53 = (f32[2,1,16,128]{3,2,1,0:T(8,128)S(1)}, f32[2,1,16,128]{3,2,1,0:T(8,128)S(1)}, u32[]{:S(2)}, u32[]{:S(2)}) collective-permute-start(f32[2,1,16,128]{3,2,1,0:T(8,128)S(1)} %get-tuple-element.244), channel_id=1, source_target_pairs={{0,4},{4,8},{8,12},{1,5},{5,9},{9,13},{2,6},{6,10},{10,14},{3,7},{... | collective-permute-start | bytes 49160 | tf_op jit(solution)/shard_map/ppermute | solution.py:20
  303.6 4.5 %collective-permute-start.55 = (f32[2,10,1,128]{3,0,2,1:T(2,128)S(1)}, f32[2,10,1,128]{3,0,2,1:T(2,128)S(1)}, u32[]{:S(2)}, u32[]{:S(2)}) collective-permute-start(f32[2,10,1,128]{3,0,2,1:T(2,128)S(1)} %copy.741), channel_id=1, source_target_pairs={{0,1},{1,2},{2,3},{4,5},{5,6},{6,7},{8,9},{9,10},{10,11},{12,13},{... | collective-permute-start | bytes 30728 | tf_op jit(solution)/shard_map/ppermute | solution.py:20
  311.1 5.1 %collective-permute-start.57 = (f32[2,1,16,128]{3,2,1,0:T(8,128)S(1)}, f32[2,1,16,128]{3,2,1,0:T(8,128)S(1)}, u32[]{:S(2)}, u32[]{:S(2)}) collective-permute-start(f32[2,1,16,128]{3,2,1,0:T(8,128)S(1)} %get-tuple-element.242), channel_id=1, source_target_pairs={{0,4},{4,8},{8,12},{1,5},{5,9},{9,13},{2,6},{6,10},{10,14},{3,7},{... | collective-permute-start | bytes 49160 | tf_op jit(solution)/shard_map/ppermute | solution.py:20
  318.4 4.5 %collective-permute-start.59 = (f32[2,10,1,128]{3,0,2,1:T(2,128)S(1)}, f32[2,10,1,128]{3,0,2,1:T(2,128)S(1)}, u32[]{:S(2)}, u32[]{:S(2)}) collective-permute-start(f32[2,10,1,128]{3,0,2,1:T(2,128)S(1)} %copy.745), channel_id=1, source_target_pairs={{0,1},{1,2},{2,3},{4,5},{5,6},{6,7},{8,9},{9,10},{10,11},{12,13},{... | collective-permute-start | bytes 30728 | tf_op jit(solution)/shard_map/ppermute | solution.py:20
  (276 shorter events, 109.8 us)
Async XLA Ops:
  32.0 51.7 %collective-permute-start.24 = (f32[4,1,4,32]{3,2,1,0:T(4,128)S(1)}, f32[4,1,4,32]{3,2,1,0:T(4,128)S(1)}, u32[]{:S(2)}, u32[]{:S(2)}) collective-permute-start(f32[4,1,4,32]{3,2,1,0:T(4,128)S(1)} %get-tuple-element.320), channel_id=1, source_target_pairs={{4,0},{8,4},{12,8},{5,1},{9,5},{13,9},{6,2},{10,6},{14,10},{7,3},{... | collective-permute-start | bytes 6152 | tf_op jit(solution)/shard_map/ppermute | solution.py:21
  34.0 49.8 %collective-permute-start.25 = (f32[4,1,4,32]{3,2,1,0:T(4,128)S(1)}, f32[4,1,4,32]{3,2,1,0:T(4,128)S(1)}, u32[]{:S(2)}, u32[]{:S(2)}) collective-permute-start(f32[4,1,4,32]{3,2,1,0:T(4,128)S(1)} %get-tuple-element.319), channel_id=1, source_target_pairs={{0,4},{4,8},{8,12},{1,5},{5,9},{9,13},{2,6},{6,10},{10,14},{3,7},{... | collective-permute-start | bytes 6152 | tf_op jit(solution)/shard_map/ppermute | solution.py:20
  38.5 37.1 %collective-permute-start.12 = (f32[4,1,8,64]{3,2,1,0:T(8,128)S(1)}, f32[4,1,8,64]{3,2,1,0:T(8,128)S(1)}, u32[]{:S(2)}, u32[]{:S(2)}) collective-permute-start(f32[4,1,8,64]{3,2,1,0:T(8,128)S(1)} %get-tuple-element.280), channel_id=1, source_target_pairs={{4,0},{8,4},{12,8},{5,1},{9,5},{13,9},{6,2},{10,6},{14,10},{7,3},{... | collective-permute-start | bytes 24584 | tf_op jit(solution)/shard_map/ppermute | solution.py:21
  40.4 42.0 %collective-permute-start.13 = (f32[4,1,8,64]{3,2,1,0:T(8,128)S(1)}, f32[4,1,8,64]{3,2,1,0:T(8,128)S(1)}, u32[]{:S(2)}, u32[]{:S(2)}) collective-permute-start(f32[4,1,8,64]{3,2,1,0:T(8,128)S(1)} %get-tuple-element.279), channel_id=1, source_target_pairs={{0,4},{4,8},{8,12},{1,5},{5,9},{9,13},{2,6},{6,10},{10,14},{3,7},{... | collective-permute-start | bytes 24584 | tf_op jit(solution)/shard_map/ppermute | solution.py:20
  44.1 49.0 %collective-permute-start = (f32[4,1,16,128]{3,2,1,0:T(8,128)S(1)}, f32[4,1,16,128]{3,2,1,0:T(8,128)S(1)}, u32[]{:S(2)}, u32[]{:S(2)}) collective-permute-start(f32[4,1,16,128]{3,2,1,0:T(8,128)S(1)} %get-tuple-element.231), channel_id=1, source_target_pairs={{4,0},{8,4},{12,8},{5,1},{9,5},{13,9},{6,2},{10,6},{14,10},{7,3},{... | collective-permute-start | bytes 98312 | tf_op jit(solution)/shard_map/ppermute | solution.py:21
  75.6 17.5 %collective-permute-start.1 = (f32[4,1,16,128]{3,2,1,0:T(8,128)S(1)}, f32[4,1,16,128]{3,2,1,0:T(8,128)S(1)}, u32[]{:S(2)}, u32[]{:S(2)}) collective-permute-start(f32[4,1,16,128]{3,2,1,0:T(8,128)S(1)} %get-tuple-element.230), channel_id=1, source_target_pairs={{0,4},{4,8},{8,12},{1,5},{5,9},{9,13},{2,6},{6,10},{10,14},{3,7},{... | collective-permute-start | bytes 98312 | tf_op jit(solution)/shard_map/ppermute | solution.py:20
  82.4 7.3 %collective-permute-start.14 = (f32[4,6,1,64]{3,0,2,1:T(4,128)S(1)}, f32[4,6,1,64]{3,0,2,1:T(4,128)S(1)}, u32[]{:S(2)}, u32[]{:S(2)}) collective-permute-start(f32[4,6,1,64]{3,0,2,1:T(4,128)S(1)} %copy.752), channel_id=1, source_target_pairs={{1,0},{2,1},{3,2},{5,4},{6,5},{7,6},{9,8},{10,9},{11,10},{13,12},{... | collective-permute-start | bytes 18440 | tf_op jit(solution)/shard_map/ppermute | solution.py:21
  83.8 65.7 %collective-permute-start.26 = (f32[4,4,1,32]{3,2,1,0:T(1,128)S(1)}, f32[4,4,1,32]{3,2,1,0:T(1,128)S(1)}, u32[]{:S(2)}, u32[]{:S(2)}) collective-permute-start(f32[4,4,1,32]{3,2,1,0:T(1,128)S(1)} %get-tuple-element.295), channel_id=1, source_target_pairs={{1,0},{2,1},{3,2},{5,4},{6,5},{7,6},{9,8},{10,9},{11,10},{13,12},{... | collective-permute-start | bytes 6152 | tf_op jit(solution)/shard_map/ppermute | solution.py:21
  85.1 71.1 %collective-permute-start.27 = (f32[4,4,1,32]{3,2,1,0:T(1,128)S(1)}, f32[4,4,1,32]{3,2,1,0:T(1,128)S(1)}, u32[]{:S(2)}, u32[]{:S(2)}) collective-permute-start(f32[4,4,1,32]{3,2,1,0:T(1,128)S(1)} %get-tuple-element.296), channel_id=1, source_target_pairs={{0,1},{1,2},{2,3},{4,5},{5,6},{6,7},{8,9},{9,10},{10,11},{12,13},{... | collective-permute-start | bytes 6152 | tf_op jit(solution)/shard_map/ppermute | solution.py:20
  89.7 16.6 %collective-permute-start.15 = (f32[4,6,1,64]{3,0,2,1:T(4,128)S(1)}, f32[4,6,1,64]{3,0,2,1:T(4,128)S(1)}, u32[]{:S(2)}, u32[]{:S(2)}) collective-permute-start(f32[4,6,1,64]{3,0,2,1:T(4,128)S(1)} %copy.753), channel_id=1, source_target_pairs={{0,1},{1,2},{2,3},{4,5},{5,6},{6,7},{8,9},{9,10},{10,11},{12,13},{... | collective-permute-start | bytes 18440 | tf_op jit(solution)/shard_map/ppermute | solution.py:20
  100.1 6.2 %collective-permute-start.4 = (f32[2,1,16,128]{3,2,1,0:T(8,128)S(1)}, f32[2,1,16,128]{3,2,1,0:T(8,128)S(1)}, u32[]{:S(2)}, u32[]{:S(2)}) collective-permute-start(f32[2,1,16,128]{3,2,1,0:T(8,128)S(1)} %get-tuple-element.249), channel_id=1, source_target_pairs={{4,0},{8,4},{12,8},{5,1},{9,5},{13,9},{6,2},{10,6},{14,10},{7,3},{... | collective-permute-start | bytes 49160 | tf_op jit(solution)/shard_map/ppermute | solution.py:21
  107.1 5.9 %collective-permute-start.6 = (f32[2,10,1,128]{3,0,2,1:T(2,128)S(1)}, f32[2,10,1,128]{3,0,2,1:T(2,128)S(1)}, u32[]{:S(2)}, u32[]{:S(2)}) collective-permute-start(f32[2,10,1,128]{3,0,2,1:T(2,128)S(1)} %copy.705), channel_id=1, source_target_pairs={{1,0},{2,1},{3,2},{5,4},{6,5},{7,6},{9,8},{10,9},{11,10},{13,12},{... | collective-permute-start | bytes 30728 | tf_op jit(solution)/shard_map/ppermute | solution.py:21
  114.0 7.1 %collective-permute-start.8 = (f32[2,1,16,128]{3,2,1,0:T(8,128)S(1)}, f32[2,1,16,128]{3,2,1,0:T(8,128)S(1)}, u32[]{:S(2)}, u32[]{:S(2)}) collective-permute-start(f32[2,1,16,128]{3,2,1,0:T(8,128)S(1)} %get-tuple-element.247), channel_id=1, source_target_pairs={{4,0},{8,4},{12,8},{5,1},{9,5},{13,9},{6,2},{10,6},{14,10},{7,3},{... | collective-permute-start | bytes 49160 | tf_op jit(solution)/shard_map/ppermute | solution.py:21
  115.9 5.9 %collective-permute-start.9 = (f32[2,1,16,128]{3,2,1,0:T(8,128)S(1)}, f32[2,1,16,128]{3,2,1,0:T(8,128)S(1)}, u32[]{:S(2)}, u32[]{:S(2)}) collective-permute-start(f32[2,1,16,128]{3,2,1,0:T(8,128)S(1)} %get-tuple-element.246), channel_id=1, source_target_pairs={{0,4},{4,8},{8,12},{1,5},{5,9},{9,13},{2,6},{6,10},{10,14},{3,7},{... | collective-permute-start | bytes 49160 | tf_op jit(solution)/shard_map/ppermute | solution.py:20
  121.8 6.1 %collective-permute-start.10 = (f32[2,10,1,128]{3,0,2,1:T(2,128)S(1)}, f32[2,10,1,128]{3,0,2,1:T(2,128)S(1)}, u32[]{:S(2)}, u32[]{:S(2)}) collective-permute-start(f32[2,10,1,128]{3,0,2,1:T(2,128)S(1)} %copy.709), channel_id=1, source_target_pairs={{1,0},{2,1},{3,2},{5,4},{6,5},{7,6},{9,8},{10,9},{11,10},{13,12},{... | collective-permute-start | bytes 30728 | tf_op jit(solution)/shard_map/ppermute | solution.py:21
  142.5 7.1 %collective-permute-start.16 = (f32[2,1,8,64]{3,2,1,0:T(8,128)S(1)}, f32[2,1,8,64]{3,2,1,0:T(8,128)S(1)}, u32[]{:S(2)}, u32[]{:S(2)}) collective-permute-start(f32[2,1,8,64]{3,2,1,0:T(8,128)S(1)} %get-tuple-element.300), channel_id=1, source_target_pairs={{4,0},{8,4},{12,8},{5,1},{9,5},{13,9},{6,2},{10,6},{14,10},{7,3},{... | collective-permute-start | bytes 12296 | tf_op jit(solution)/shard_map/ppermute | solution.py:21
  150.3 6.0 %collective-permute-start.18 = (f32[2,6,1,64]{3,2,1,0:T(1,128)S(1)}, f32[2,6,1,64]{3,2,1,0:T(1,128)S(1)}, u32[]{:S(2)}, u32[]{:S(2)}) collective-permute-start(f32[2,6,1,64]{3,2,1,0:T(1,128)S(1)} %get-tuple-element.287), channel_id=1, source_target_pairs={{1,0},{2,1},{3,2},{5,4},{6,5},{7,6},{9,8},{10,9},{11,10},{13,12},{... | collective-permute-start | bytes 9224 | tf_op jit(solution)/shard_map/ppermute | solution.py:21
  157.0 7.1 %collective-permute-start.20 = (f32[2,1,8,64]{3,2,1,0:T(8,128)S(1)}, f32[2,1,8,64]{3,2,1,0:T(8,128)S(1)}, u32[]{:S(2)}, u32[]{:S(2)}) collective-permute-start(f32[2,1,8,64]{3,2,1,0:T(8,128)S(1)} %get-tuple-element.298), channel_id=1, source_target_pairs={{4,0},{8,4},{12,8},{5,1},{9,5},{13,9},{6,2},{10,6},{14,10},{7,3},{... | collective-permute-start | bytes 12296 | tf_op jit(solution)/shard_map/ppermute | solution.py:21
  164.7 5.9 %collective-permute-start.22 = (f32[2,6,1,64]{3,2,1,0:T(1,128)S(1)}, f32[2,6,1,64]{3,2,1,0:T(1,128)S(1)}, u32[]{:S(2)}, u32[]{:S(2)}) collective-permute-start(f32[2,6,1,64]{3,2,1,0:T(1,128)S(1)} %get-tuple-element.285), channel_id=1, source_target_pairs={{1,0},{2,1},{3,2},{5,4},{6,5},{7,6},{9,8},{10,9},{11,10},{13,12},{... | collective-permute-start | bytes 9224 | tf_op jit(solution)/shard_map/ppermute | solution.py:21
  172.7 7.0 %collective-permute-start.28 = (f32[2,1,4,32]{3,2,1,0:T(4,128)S(1)}, f32[2,1,4,32]{3,2,1,0:T(4,128)S(1)}, u32[]{:S(2)}, u32[]{:S(2)}) collective-permute-start(f32[2,1,4,32]{3,2,1,0:T(4,128)S(1)} %get-tuple-element.328), channel_id=1, source_target_pairs={{4,0},{8,4},{12,8},{5,1},{9,5},{13,9},{6,2},{10,6},{14,10},{7,3},{... | collective-permute-start | bytes 3080 | tf_op jit(solution)/shard_map/ppermute | solution.py:21
  180.4 5.9 %collective-permute-start.30 = (f32[2,4,1,32]{3,2,1,0:T(1,128)S(1)}, f32[2,4,1,32]{3,2,1,0:T(1,128)S(1)}, u32[]{:S(2)}, u32[]{:S(2)}) collective-permute-start(f32[2,4,1,32]{3,2,1,0:T(1,128)S(1)} %get-tuple-element.317), channel_id=1, source_target_pairs={{1,0},{2,1},{3,2},{5,4},{6,5},{7,6},{9,8},{10,9},{11,10},{13,12},{... | collective-permute-start | bytes 3080 | tf_op jit(solution)/shard_map/ppermute | solution.py:21
  187.1 7.0 %collective-permute-start.32 = (f32[2,1,4,32]{3,2,1,0:T(4,128)S(1)}, f32[2,1,4,32]{3,2,1,0:T(4,128)S(1)}, u32[]{:S(2)}, u32[]{:S(2)}) collective-permute-start(f32[2,1,4,32]{3,2,1,0:T(4,128)S(1)} %get-tuple-element.326), channel_id=1, source_target_pairs={{4,0},{8,4},{12,8},{5,1},{9,5},{13,9},{6,2},{10,6},{14,10},{7,3},{... | collective-permute-start | bytes 3080 | tf_op jit(solution)/shard_map/ppermute | solution.py:21
  234.6 8.2 %collective-permute-start.36 = (f32[2,1,4,32]{3,2,1,0:T(4,128)S(1)}, f32[2,1,4,32]{3,2,1,0:T(4,128)S(1)}, u32[]{:S(2)}, u32[]{:S(2)}) collective-permute-start(f32[2,1,4,32]{3,2,1,0:T(4,128)S(1)} %get-tuple-element.324), channel_id=1, source_target_pairs={{4,0},{8,4},{12,8},{5,1},{9,5},{13,9},{6,2},{10,6},{14,10},{7,3},{... | collective-permute-start | bytes 3080 | tf_op jit(solution)/shard_map/ppermute | solution.py:21
  249.6 7.3 %collective-permute-start.40 = (f32[2,1,4,32]{3,2,1,0:T(4,128)S(1)}, f32[2,1,4,32]{3,2,1,0:T(4,128)S(1)}, u32[]{:S(2)}, u32[]{:S(2)}) collective-permute-start(f32[2,1,4,32]{3,2,1,0:T(4,128)S(1)} %get-tuple-element.322), channel_id=1, source_target_pairs={{4,0},{8,4},{12,8},{5,1},{9,5},{13,9},{6,2},{10,6},{14,10},{7,3},{... | collective-permute-start | bytes 3080 | tf_op jit(solution)/shard_map/ppermute | solution.py:21
  264.6 7.0 %collective-permute-start.44 = (f32[2,1,8,64]{3,2,1,0:T(8,128)S(1)}, f32[2,1,8,64]{3,2,1,0:T(8,128)S(1)}, u32[]{:S(2)}, u32[]{:S(2)}) collective-permute-start(f32[2,1,8,64]{3,2,1,0:T(8,128)S(1)} %get-tuple-element.292), channel_id=1, source_target_pairs={{4,0},{8,4},{12,8},{5,1},{9,5},{13,9},{6,2},{10,6},{14,10},{7,3},{... | collective-permute-start | bytes 12296 | tf_op jit(solution)/shard_map/ppermute | solution.py:21
  279.1 7.0 %collective-permute-start.48 = (f32[2,1,8,64]{3,2,1,0:T(8,128)S(1)}, f32[2,1,8,64]{3,2,1,0:T(8,128)S(1)}, u32[]{:S(2)}, u32[]{:S(2)}) collective-permute-start(f32[2,1,8,64]{3,2,1,0:T(8,128)S(1)} %get-tuple-element.290), channel_id=1, source_target_pairs={{4,0},{8,4},{12,8},{5,1},{9,5},{13,9},{6,2},{10,6},{14,10},{7,3},{... | collective-permute-start | bytes 12296 | tf_op jit(solution)/shard_map/ppermute | solution.py:21
  294.5 7.0 %collective-permute-start.52 = (f32[2,1,16,128]{3,2,1,0:T(8,128)S(1)}, f32[2,1,16,128]{3,2,1,0:T(8,128)S(1)}, u32[]{:S(2)}, u32[]{:S(2)}) collective-permute-start(f32[2,1,16,128]{3,2,1,0:T(8,128)S(1)} %get-tuple-element.245), channel_id=1, source_target_pairs={{4,0},{8,4},{12,8},{5,1},{9,5},{13,9},{6,2},{10,6},{14,10},{7,3},{... | collective-permute-start | bytes 49160 | tf_op jit(solution)/shard_map/ppermute | solution.py:21
  296.4 5.9 %collective-permute-start.53 = (f32[2,1,16,128]{3,2,1,0:T(8,128)S(1)}, f32[2,1,16,128]{3,2,1,0:T(8,128)S(1)}, u32[]{:S(2)}, u32[]{:S(2)}) collective-permute-start(f32[2,1,16,128]{3,2,1,0:T(8,128)S(1)} %get-tuple-element.244), channel_id=1, source_target_pairs={{0,4},{4,8},{8,12},{1,5},{5,9},{9,13},{2,6},{6,10},{10,14},{3,7},{... | collective-permute-start | bytes 49160 | tf_op jit(solution)/shard_map/ppermute | solution.py:20
  302.3 5.9 %collective-permute-start.54 = (f32[2,10,1,128]{3,0,2,1:T(2,128)S(1)}, f32[2,10,1,128]{3,0,2,1:T(2,128)S(1)}, u32[]{:S(2)}, u32[]{:S(2)}) collective-permute-start(f32[2,10,1,128]{3,0,2,1:T(2,128)S(1)} %copy.739), channel_id=1, source_target_pairs={{1,0},{2,1},{3,2},{5,4},{6,5},{7,6},{9,8},{10,9},{11,10},{13,12},{... | collective-permute-start | bytes 30728 | tf_op jit(solution)/shard_map/ppermute | solution.py:21
  309.2 7.0 %collective-permute-start.56 = (f32[2,1,16,128]{3,2,1,0:T(8,128)S(1)}, f32[2,1,16,128]{3,2,1,0:T(8,128)S(1)}, u32[]{:S(2)}, u32[]{:S(2)}) collective-permute-start(f32[2,1,16,128]{3,2,1,0:T(8,128)S(1)} %get-tuple-element.243), channel_id=1, source_target_pairs={{4,0},{8,4},{12,8},{5,1},{9,5},{13,9},{6,2},{10,6},{14,10},{7,3},{... | collective-permute-start | bytes 49160 | tf_op jit(solution)/shard_map/ppermute | solution.py:21
  311.1 5.9 %collective-permute-start.57 = (f32[2,1,16,128]{3,2,1,0:T(8,128)S(1)}, f32[2,1,16,128]{3,2,1,0:T(8,128)S(1)}, u32[]{:S(2)}, u32[]{:S(2)}) collective-permute-start(f32[2,1,16,128]{3,2,1,0:T(8,128)S(1)} %get-tuple-element.242), channel_id=1, source_target_pairs={{0,4},{4,8},{8,12},{1,5},{5,9},{9,13},{2,6},{6,10},{10,14},{3,7},{... | collective-permute-start | bytes 49160 | tf_op jit(solution)/shard_map/ppermute | solution.py:20
  317.0 5.9 %collective-permute-start.58 = (f32[2,10,1,128]{3,0,2,1:T(2,128)S(1)}, f32[2,10,1,128]{3,0,2,1:T(2,128)S(1)}, u32[]{:S(2)}, u32[]{:S(2)}) collective-permute-start(f32[2,10,1,128]{3,0,2,1:T(2,128)S(1)} %copy.743), channel_id=1, source_target_pairs={{1,0},{2,1},{3,2},{5,4},{6,5},{7,6},{9,8},{10,9},{11,10},{13,12},{... | collective-permute-start | bytes 30728 | tf_op jit(solution)/shard_map/ppermute | solution.py:21
  (31 other events, 307.0 us)
where the time goes:
time: 328 us; the launch traced here: 325 us
  starting transfers between devices  190 us (58%)
  blocking collectives  58.9 us (18%)
  local copies, waits for them, and re-layouts  36.5 us (11%)
  other arithmetic  18.2 us (6%)
  waiting for transfers between devices  18 us (5%)
    ppermute x30, starting transfers between devices, extended(): before = lax.ppermute(last, axis, up)  137 us
    ppermute x30, starting transfers between devices, extended(): after = lax.ppermute(leading, axis, down)  52.8 us
    all_gather x1, blocking collectives, coarse_solve(): lax.all_gather(source[None], ('gx', 'gy'), axis=0, tiled=True)  30.1 us
    all_gather x1, blocking collectives, coarse_solve(): lax.all_gather(local[None], ('gx', 'gy'), axis=0, tiled=True)  28.9 us
    another operation x4, local copies, waits for them, and re-layouts, material_fields(): jnp.stack([select_table(permittivity), select_table(mobility), potential,...  22.3 us
    ppermute x30, waiting for transfers between devices, extended(): before = lax.ppermute(last, axis, up)  17.9 us
    reduce_sum x8, other arithmetic, restrict_mean(): return jnp.sum(blocks, axis=(-5, -3, -1)) * 0.125  11.8 us
    reshape x2, local copies, waits for them, and re-layouts, restrict_mean(): array.reshape(leading + (rows // 2, 2, columns // 2, 2, layers // 2, 2))  10.9 us
  transfers between devices with their start and end apart: 60, of which 25 were waited for; matrix products, arithmetic and copies ran while one was open for 5% of the time, Pallas kernels for 0%

commit v1 on v0

v1 whole, which is shorter than its diff:
```python
import functools
import jax
import jax.numpy as jnp
from jax import lax
from jax.experimental import pallas as pl
from jax.experimental.pallas import tpu as pltpu
from jax.sharding import PartitionSpec as P

OMEGA = 0.8
COARSE_ITERS = 20
RIM = 4
LANES = 128
VMEM = pl.BlockSpec(memory_space=pltpu.VMEM)
SMEM = pl.BlockSpec(memory_space=pltpu.SMEM)


def params(mib):
    return pltpu.CompilerParams(vmem_limit_bytes=mib * 1024 * 1024)


def bernoulli(x):
    t = x * x
    series = 1.0 - 0.5 * x + t * (1 / 12 + t * (-1 / 720 + t * (1 / 30240)))
    near = t < 0.25
    guarded = jnp.where(near, 1.0, x)
    return jnp.where(near, series, guarded / (jnp.exp(guarded) - 1.0))


def iota(shape, dim):
    return lax.broadcasted_iota(jnp.int32, shape, dim)


def up(v, step, dim):
    return pltpu.roll(v, v.shape[dim] - step, dim)


def down(v, step, dim):
    return pltpu.roll(v, step, dim)


def rim_y_kernel(cls, pot, fp, fn, out_a, out_b):
    even = lax.axis_index("gy") % 2 == 0
    length = cls.shape[1]
    for pair, (first, second) in enumerate(((cls, pot), (fp, fn))):
        lo, hi = (
            jnp.concatenate(
                [r[:, at : at + RIM, :].astype(jnp.float32) for r in (first, second)], axis=1
            )
            for at in (0, length - RIM)
        )
        out_a[pair] = jnp.where(even, hi, lo)
        out_b[pair] = jnp.where(even, lo, hi)


def rim_x_kernel(cls, pot, fp, fn, in_a, in_b, out, out_a, out_b):
    y, ny = lax.axis_index("gy"), lax.axis_size("gy")
    even_x, even_y = lax.axis_index("gx") % 2 == 0, y % 2 == 0
    planes, length = cls.shape[0], cls.shape[1]
    row = iota((planes, 2 * RIM, LANES), 1)
    for pair, refs in enumerate(((cls, pot), (fp, fn))):
        a, b = in_a[pair], in_b[pair]
        hi, lo = jnp.where(even_y, a, b), jnp.where(even_y, b, a)
        for slot, ref in enumerate(refs):
            field = 2 * pair + slot
            outside = -1.0 if field == 0 else 0.0
            h, l = jnp.where(y == ny - 1, outside, hi), jnp.where(y == 0, outside, lo)
            if slot == 0:
                l = down(l, RIM, 1)
            else:
                h = down(h, RIM, 1)
            out[field, :, 0:length, :] = ref[...].astype(jnp.float32)
            out[field, :, length : length + 2 * RIM, :] = jnp.where(row < RIM, h, l)
        for slot in range(2):
            field = 2 * pair + slot
            lo_x, hi_x = out[field, 0:RIM], out[field, planes - RIM : planes]
            out_a[field] = jnp.where(even_x, hi_x, lo_x)
            out_b[field] = jnp.where(even_x, lo_x, hi_x)


W_P, GX, GY, GZ, W_N, XP, XM, YP, YM, ZP, ZM, WF_P, WF_N, U_P, U_N = range(15)
KEPT = 15


def coupled_fine(kept, u, i, poisson):
    v = u(i)
    if poisson:
        xp, xm, yp, ym, zp, zm = GX, GX, GY, GY, GZ, GZ
    else:
        xp, xm, yp, ym, zp, zm = XP, XM, YP, YM, ZP, ZM
    s = kept[xp, i] * u(i + 1) + kept[xm, i - 1] * u(i - 1)
    s = s + (kept[yp, i] * up(v, 1, 0) + down(kept[ym, i] * v, 1, 0))
    return s + (kept[zp, i] * up(v, 1, 1) + down(kept[zm, i] * v, 1, 1))


def halve_lanes(a, b):
    lane = iota(a.shape, 1)
    at = (2 * lane) % LANES
    a = jnp.take_along_axis(a + up(a, 1, 1), at, axis=1)
    b = jnp.take_along_axis(b + up(b, 1, 1), at, axis=1)
    return jnp.where(lane < LANES // 2, a, b)


def first_kernel(eps_t, mob_t, cap_t, mid, in_a, in_b, kept, block, fld, work, tmp):
    x, nx = lax.axis_index("gx"), lax.axis_size("gx")
    even = x % 2 == 0
    planes = mid.shape[1]
    rows = mid.shape[2]
    own = rows - 2 * RIM
    total = planes + 2 * RIM
    EPS, MOB, POT, CAP, F_P, F_N, D_P, D_N = range(8)
    classes = eps_t.shape[0]

    def materials(i, c, pot, fp, fn):
        eps, mob, cap = jnp.zeros_like(c), jnp.zeros_like(c), jnp.zeros_like(c)
        for k in range(classes):
            same = c == float(k)
            eps = jnp.where(same, eps_t[k], eps)
            mob = jnp.where(same, mob_t[k], mob)
            cap = jnp.where(same, cap_t[k], cap)
        fld[EPS, i], fld[MOB, i], fld[POT, i], fld[CAP, i] = eps, mob, pot, cap
        fld[F_P, i], fld[F_N, i] = fp, fn

    def low(i, _):
        v = [jnp.where(even, in_b[f, i], in_a[f, i]) for f in range(4)]
        materials(i, *[jnp.where(x == 0, -1.0 if f == 0 else 0.0, v[f]) for f in range(4)])
        return 0

    def middle(i, _):
        materials(i + RIM, *[mid[f, i] for f in range(4)])
        return 0

    def high(i, _):
        v = [jnp.where(even, in_a[f, i], in_b[f, i]) for f in range(4)]
        materials(
            i + RIM + planes,
            *[jnp.where(x == nx - 1, -1.0 if f == 0 else 0.0, v[f]) for f in range(4)],
        )
        return 0

    lax.fori_loop(0, RIM, low, 0)
    lax.fori_loop(0, planes, middle, 0)
    lax.fori_loop(0, RIM, high, 0)

    shape = (rows, LANES)
    lane = iota(shape, 1)
    ends = (lane == 0) | (lane == LANES - 1)
    top = lane == LANES - 1

    def x_faces(i):
        eps, mob, pot = fld[EPS, i], fld[MOB, i], fld[POT, i]
        kept[GX, i] = 0.5 * (eps + fld[EPS, i + 1])
        k = 0.5 * (mob + fld[MOB, i + 1])
        delta = fld[POT, i + 1] - pot
        kb = k * bernoulli(delta)
        kept[XP, i] = kb
        kept[XM, i] = kb + k * delta

    x_faces(0)

    def operators(i, _):
        x_faces(i)
        eps, mob, pot = fld[EPS, i], fld[MOB, i], fld[POT, i]
        gy = 0.5 * (eps + up(eps, 1, 0))
        k = 0.5 * (mob + up(mob, 1, 0))
        delta = up(pot, 1, 0) - pot
        yp = k * bernoulli(delta)
        ym = yp + k * delta
        gz = jnp.where(top, 0.0, 0.5 * (eps + up(eps, 1, 1)))
        k = jnp.where(top, 0.0, 0.5 * (mob + up(mob, 1, 1)))
        delta = up(pot, 1, 1) - pot
        zp = k * bernoulli(delta)
        zm = zp + k * delta
        kept[GY, i], kept[YP, i], kept[YM, i] = gy, yp, ym
        kept[GZ, i], kept[ZP, i], kept[ZM, i] = gz, zp, zm
        d_p = (kept[GX, i] + kept[GX, i - 1]) + (gy + down(gy, 1, 0)) + (gz + down(gz, 1, 1))
        d_p = d_p + jnp.where(ends, 0.5 * eps, 0.0)
        d_n = (kept[XM, i] + kept[XP, i - 1]) + (ym + down(yp, 1, 0)) + (zm + down(zp, 1, 1))
        d_n = d_n + jnp.where(ends, 0.5 * mob * bernoulli(pot), 0.0) + fld[CAP, i]
        inside = eps > 0.0
        w_p = jnp.where(inside, OMEGA / jnp.where(inside, d_p, 1.0), 0.0)
        w_n = jnp.where(inside, OMEGA / jnp.where(inside, d_n, 1.0), 0.0)
        kept[W_P, i], kept[W_N, i] = w_p, w_n
        kept[WF_P, i], kept[WF_N, i] = w_p * fld[F_P, i], w_n * fld[F_N, i]
        fld[D_P, i], fld[D_N, i] = d_p, d_n
        return 0

    lax.fori_loop(1, total - 1, operators, 0)

    def sweep(i, _):
        for poisson, w, wf, u in ((True, W_P, WF_P, U_P), (False, W_N, WF_N, U_N)):
            s = coupled_fine(kept, lambda j: kept[wf, j], i, poisson)
            kept[u, i] = (2.0 - OMEGA) * kept[wf, i] + kept[w, i] * s
        return 0

    lax.fori_loop(2, total - 2, sweep, 0)

    def residual(i, poisson, f, d, u):
        s = coupled_fine(kept, lambda j: kept[u, j], i, poisson)
        return fld[f, i] - fld[d, i] * kept[u, i] + s

    def halved(v):
        tmp[...] = v
        return tmp[0 : own : 2, :] + tmp[1 : own : 2, :]

    def coarse(i, _):
        at = RIM + 2 * i
        r_p = residual(at, True, F_P, D_P, U_P) + residual(at + 1, True, F_P, D_P, U_P)
        r_n = residual(at, False, F_N, D_N, U_N) + residual(at + 1, False, F_N, D_N, U_N)
        values = [r_p, r_n] + [fld[f, at] + fld[f, at + 1] for f in (EPS, MOB, CAP, POT)]
        for k, v in enumerate(values):
            work[k] = v[0:own]
        even_odd = [
            work[k, pl.ds(0, own // 2, stride=2), :] + work[k, pl.ds(1, own // 2, stride=2), :]
            for k in range(6)
        ]
        for k in range(3):
            block[(2, 0, 1)[k], i] = 0.125 * halve_lanes(even_odd[2 * k], even_odd[2 * k + 1])
        return 0

    lax.fori_loop(0, planes // 2, coarse, 0)


def low_lane(shape, bit):
    return (iota(shape, 1) & bit) == 0


class Level:
    def __init__(self, level, refs):
        self.level, self.step, self.factor = level, 1 << (level - 1), 0.25**level
        (self.eps, self.pot, self.cap, self.f, self.xp, self.xm, self.yp, self.ym, self.zp, self.zm,
         self.w, self.d, self.wf, self.u, self.v) = refs
        self.nx, self.ny = self.eps.shape[0], self.eps.shape[1]

    @staticmethod
    def scratch(nx, ny):
        plain, face, padded = (pltpu.VMEM((n, ny, LANES), jnp.float32) for n in (nx, nx + 1, nx + 2))
        return [plain] * 4 + [face] * 2 + [plain] * 7 + [padded] * 2

    def assemble(self):
        nx, ny, step = self.nx, self.ny, self.step
        shape = (ny, LANES)
        row, spot = iota(shape, 0), iota(shape, 1) % (LANES // 2)
        last_row, top = row == ny - 1, spot >= LANES // 2 - step
        walls = (
            jnp.where(row == 0, 1.0, 0.0)
            + jnp.where(last_row, 1.0, 0.0)
            + jnp.where(spot < step, 1.0, 0.0)
            + jnp.where(top, 1.0, 0.0)
        )
        zero = jnp.zeros(shape, jnp.float32)
        half = 0.5 * self.factor
        for ref in (self.xp, self.xm):
            ref[0], ref[nx] = zero, zero
        for ref in (self.u, self.v):
            ref[0], ref[nx + 1] = zero, zero

        def x_face(i, _):
            k = half * (self.eps[i - 1] + self.eps[i])
            delta = self.pot[i] - self.pot[i - 1]
            kb = k * bernoulli(delta)
            self.xp[i], self.xm[i] = kb, kb + k * delta
            return 0

        lax.fori_loop(1, nx, x_face, 0)

        def plane(i, _):
            eps, pot = self.eps[i], self.pot[i]
            k = jnp.where(last_row, 0.0, half * (eps + up(eps, 1, 0)))
            delta = up(pot, 1, 0) - pot
            yp = k * bernoulli(delta)
            ym = yp + k * delta
            k = jnp.where(top, 0.0, half * (eps + up(eps, step, 1)))
            delta = up(pot, step, 1) - pot
            zp = k * bernoulli(delta)
            zm = zp + k * delta
            outer = walls + jnp.where(i == 0, 1.0, 0.0) + jnp.where(i == nx - 1, 1.0, 0.0)
            d = (self.xm[i + 1] + self.xp[i]) + (ym + down(yp, 1, 0)) + (zm + down(zp, step, 1))
            d = d + outer * (half * eps * bernoulli(pot)) + self.cap[i]
            w = OMEGA / d
            self.yp[i], self.ym[i], self.zp[i], self.zm[i] = yp, ym, zp, zm
            self.d[i], self.w[i] = d, w
            return 0

        lax.fori_loop(0, nx, plane, 0)

    def coupled(self, u, i):
        v = u[i + 1]
        s = self.xp[i + 1] * u[i + 2] + self.xm[i] * u[i]
        s = s + (self.yp[i] * up(v, 1, 0) + down(self.ym[i] * v, 1, 0))
        return s + (self.zp[i] * up(v, self.step, 1) + down(self.zm[i] * v, self.step, 1))

    def start(self):
        def body(i, _):
            wf = self.w[i] * self.f[i]
            self.wf[i] = wf
            self.u[i + 1] = wf
            return 0

        lax.fori_loop(0, self.nx, body, 0)

    def sweep(self, u, v):
        def body(i, _):
            v[i + 1] = (1.0 - OMEGA) * u[i + 1] + self.wf[i] + self.w[i] * self.coupled(u, i)
            return 0

        lax.fori_loop(0, self.nx, body, 0)

    def halve(self, tmp, v):
        step, ny = self.step, self.ny
        tmp[0:ny] = v
        v = tmp[pl.ds(0, ny // 2, stride=2), :] + tmp[pl.ds(1, ny // 2, stride=2), :]
        other = jnp.where(low_lane(v.shape, step), up(v, step, 1), down(v, step, 1))
        return 0.125 * (v + other)

    def descend_fields(self, coarser, tmp):
        def body(i, _):
            for here, there in ((self.eps, coarser.eps), (self.pot, coarser.pot), (self.cap, coarser.cap)):
                there[i] = self.halve(tmp, here[2 * i] + here[2 * i + 1])
            return 0

        lax.fori_loop(0, coarser.nx, body, 0)

    def descend_residual(self, u, coarser, tmp):
        def residual(i):
            return self.f[i] - self.d[i] * u[i + 1] + self.coupled(u, i)

        def body(i, _):
            coarser.f[i] = self.halve(tmp, residual(2 * i) + residual(2 * i + 1))
            return 0

        lax.fori_loop(0, coarser.nx, body, 0)

    def correct(self, u, coarser_u, tmp):
        half_ny = self.ny // 2

        def body(i, _):
            e = coarser_u(i)
            tmp[pl.ds(0, half_ny, stride=2), :] = e
            tmp[pl.ds(1, half_ny, stride=2), :] = e
            wide = tmp[0 : self.ny]
            u[2 * i + 1] = u[2 * i + 1] + wide
            u[2 * i + 2] = u[2 * i + 2] + wide
            return 0

        lax.fori_loop(0, self.nx // 2, body, 0)


def coarsest(lv):
    nx, step = lv.nx, lv.step
    cxp = [lv.w[i] * lv.xp[i + 1] for i in range(nx)]
    cxm = [lv.w[i] * lv.xm[i] for i in range(nx)]
    cyp = [lv.w[i] * lv.yp[i] for i in range(nx)]
    cym = [lv.w[i] * down(lv.ym[i], 1, 0) for i in range(nx)]
    czp = [lv.w[i] * lv.zp[i] for i in range(nx)]
    czm = [lv.w[i] * down(lv.zm[i], step, 1) for i in range(nx)]
    wf = [lv.w[i] * lv.f[i] for i in range(nx)]

    def body(_, u):
        new = []
        for i in range(nx):
            s = czp[i] * up(u[i], step, 1) + czm[i] * down(u[i], step, 1)
            t = cyp[i] * up(u[i], 1, 0) + cym[i] * down(u[i], 1, 0)
            r = (1.0 - OMEGA) * u[i] + wf[i]
            if i + 1 < nx:
                r = r + cxp[i] * u[i + 1]
            if i > 0:
                r = r + cxm[i] * u[i - 1]
            new.append(r + t + s)
        return tuple(new)

    u = lax.fori_loop(0, COARSE_ITERS - 1, body, tuple(wf))
    for i in range(nx):
        lv.u[i + 1] = u[i]


def second_kernel(bits, near, far, kept, out_p, out_n, *scratch):
    x, y = lax.axis_index("gx"), lax.axis_index("gy")
    ny = lax.axis_size("gy")
    l1, l2, l3 = (Level(k + 1, scratch[15 * k : 15 * k + 15]) for k in range(3))
    sol, tmp, fine_a, fine_b = scratch[45:]
    bx, by = near.shape[2], near.shape[3]
    half = near.shape[0]
    lane = iota((by, LANES), 1)
    right = lane >= LANES // 2

    def place(ref, flip):
        def body(m, _):
            b = m // ny
            to_x = x ^ flip
            for k, bit in enumerate(bits[:-1]):
                to_x = to_x ^ (((b >> k) & 1) * bit)
            to_y = y ^ (m % ny)
            row = pl.ds(pl.multiple_of(to_y * by, by), by)
            for i in range(bx):
                at = to_x * bx + i
                q = ref[m, 1, i]
                l1.eps[at, row, :] = ref[m, 0, i]
                l1.pot[at, row, :] = jnp.where(right, q, 0.0)
                l1.cap[at, row, :] = jnp.where(right, down(q, LANES // 2, 1), 0.0)
                l1.f[at, row, :] = ref[m, 2, i]
            return 0

        lax.fori_loop(0, half, body, 0)

    place(near, 0)
    place(far, bits[-1])
    l1.assemble()
    l1.descend_fields(l2, tmp)
    l2.assemble()
    l2.descend_fields(l3, tmp)
    l3.assemble()
    for here, there in ((l1, l2), (l2, l3)):
        here.start()
        here.sweep(here.u, here.v)
        here.descend_residual(here.v, there, tmp)
    coarsest(l3)
    l2.correct(l2.v, lambda i: l3.u[i + 1], tmp)
    l2.sweep(l2.v, l2.u)
    l2.sweep(l2.u, l2.v)
    l1.correct(l1.v, lambda i: l2.v[i + 1], tmp)
    l1.sweep(l1.v, l1.u)
    edge = jnp.zeros((by, LANES), jnp.float32)
    n1x, n1y = l1.nx, l1.ny
    blank = jnp.zeros((n1y + 2 * by, LANES), jnp.float32)
    sol[0], sol[n1x + 1] = blank, blank

    def last(i, _):
        sol[i + 1, 0:by] = edge
        sol[i + 1, by + n1y :] = edge
        sol[i + 1, by : by + n1y] = (
            (1.0 - OMEGA) * l1.u[i + 1] + l1.wf[i] + l1.w[i] * l1.coupled(l1.u, i)
        )
        return 0

    lax.fori_loop(0, n1x, last, 0)

    rows = kept.shape[2]
    own = rows - 2 * RIM
    tile_row = iota((by, LANES), 0)
    spread = iota((by, LANES), 1) // 2

    def widen(v, channel):
        return jnp.take_along_axis(v, spread + channel * (LANES // 2), axis=1)

    def correct(i, _):
        at = x * bx + i
        middle, above, below = (
            sol[at, pl.ds(pl.multiple_of((y + k) * by, by), by), :] for k in (1, 2, 0)
        )
        rim = jnp.where(
            tile_row < 2,
            jnp.broadcast_to(above[0:1], (by, LANES)),
            jnp.where(tile_row >= by - 2, jnp.broadcast_to(below[by - 1 : by], (by, LANES)), 0.0),
        )
        for channel, u in ((0, U_P), (1, U_N)):
            e = widen(middle, channel)
            tmp[pl.ds(0, by, stride=2), :] = e
            tmp[pl.ds(1, by, stride=2), :] = e
            tmp[own:rows] = widen(rim, channel)
            e = tmp[0:rows]
            for k in (0, 1):
                p = RIM - 2 + 2 * i + k
                fine_a[channel, p] = kept[u, p] + e
        return 0

    lax.fori_loop(0, bx + 2, correct, 0)

    def fine(u, channel, i):
        w, wf = ((W_P, WF_P), (W_N, WF_N))[channel]
        s = coupled_fine(kept, lambda j: u[channel, j], i, channel == 0)
        return (1.0 - OMEGA) * u[channel, i] + kept[wf, i] + kept[w, i] * s

    def post_one(i, _):
        for channel in (0, 1):
            fine_b[channel, i] = fine(fine_a, channel, i)
        return 0

    def post_two(i, _):
        out_p[i] = fine(fine_b, 0, i + RIM)[0:own]
        out_n[i] = fine(fine_b, 1, i + RIM)[0:own]
        return 0

    lax.fori_loop(RIM - 1, RIM + 2 * bx + 1, post_one, 0)
    lax.fori_loop(0, 2 * bx, post_two, 0)


def moves(nx, ny):
    def of(partner):
        return [(a * ny + b, (lambda t: t[0] * ny + t[1])(partner(a, b))) for a in range(nx) for b in range(ny)]

    def other(k, n):
        return k + 1 if k % 2 else k - 1

    return {
        "xa": of(lambda a, b: (a ^ 1, b)),
        "xb": of(lambda a, b: (other(a, nx), b) if 0 < a < nx - 1 else (a, b ^ 1)),
        "ya": of(lambda a, b: (a, b ^ 1)),
        "yb": of(lambda a, b: (a, other(b, ny)) if 0 < b < ny - 1 else (a ^ 1, b)),
        **{("x", k): of(lambda a, b, k=k: (a ^ k, b)) for k in range(1, nx)},
        **{("y", k): of(lambda a, b, k=k: (a, b ^ k)) for k in range(1, ny)},
    }


def per_device(nx, ny, layer_class, permittivity, mobility, capture, potential, rhs_psi, rhs_n):
    send = moves(nx, ny)
    f32 = jnp.float32

    def permute(v, name):
        return lax.ppermute(v, ("gx", "gy"), send[name])

    planes, own = layer_class.shape[0], layer_class.shape[1]
    rows, total = own + 2 * RIM, planes + 2 * RIM
    bx, by = planes // 2, own // 2
    raw = (layer_class, potential, rhs_psi, rhs_n)

    def shape(*dims):
        return jax.ShapeDtypeStruct(dims, f32)

    a, b = pl.pallas_call(
        rim_y_kernel,
        out_shape=[shape(2, planes, 2 * RIM, LANES)] * 2,
        in_specs=[VMEM] * 4,
        out_specs=[VMEM] * 2,
        compiler_params=params(16),
    )(*raw)
    b = permute(b, "yb")
    a = permute(a, "ya")
    mid, a, b = pl.pallas_call(
        rim_x_kernel,
        out_shape=[shape(4, planes, rows, LANES)] + [shape(4, RIM, rows, LANES)] * 2,
        in_specs=[VMEM] * 6,
        out_specs=[VMEM] * 3,
        compiler_params=params(16),
    )(*raw, a, b)
    b = permute(b, "xb")
    a = permute(a, "xa")
    kept, block = pl.pallas_call(
        first_kernel,
        out_shape=[shape(KEPT, total, rows, LANES), shape(3, bx, by, LANES)],
        in_specs=[SMEM] * 3 + [VMEM] * 3,
        out_specs=[VMEM] * 2,
        scratch_shapes=[
            pltpu.VMEM((8, total, rows, LANES), f32),
            pltpu.VMEM((6, own, LANES), f32),
            pltpu.VMEM((rows, LANES), f32),
        ],
        compiler_params=params(24),
    )(permittivity, mobility, capture, mid, a, b)

    near = jnp.stack([block] + [permute(block, ("y", k)) for k in range(1, ny)])
    bits = []
    bit = nx // 2
    while bit:
        bits.append(bit)
        far = permute(near, ("x", bit))
        if bit > 1:
            near = jnp.concatenate([near, far], axis=0)
        bit //= 2
    gx1, gy1 = bx * nx, by * ny
    scratch = []
    for level in range(3):
        scratch += Level.scratch(gx1 >> level, gy1 >> level)
    scratch += [
        pltpu.VMEM((gx1 + 2, gy1 + 2 * by, LANES), f32),
        pltpu.VMEM((max(gy1, rows), LANES), f32),
        pltpu.VMEM((2, total, rows, LANES), f32),
        pltpu.VMEM((2, total, rows, LANES), f32),
    ]
    return pl.pallas_call(
        functools.partial(second_kernel, tuple(bits)),
        out_shape=[shape(planes, own, LANES)] * 2,
        in_specs=[VMEM] * 3,
        out_specs=[VMEM] * 2,
        scratch_shapes=scratch,
        compiler_params=params(60 if gx1 * gy1 > 1024 else 32),
    )(near, far, kept)


def solution(mesh):
    grid = P(("groups", "gx"), "gy", None)
    fn = functools.partial(per_device, mesh.shape["gx"], mesh.shape["gy"])
    return jax.shard_map(
        fn,
        mesh=mesh,
        in_specs=(grid, P(), P(), P(), grid, grid, grid),
        out_specs=(grid, grid),
        check_vma=False,
    )
```

time: 328 us -> 60.9 us (0.19)
  starting transfers between devices: 190 us -> 15.5 us
  blocking collectives: 58.9 us -> 0 us
  local copies, waits for them, and re-layouts: 36.5 us -> 5.35 us
  Pallas kernels: 0 us -> 25.2 us
  other arithmetic: 18.2 us -> 0.01 us
  waiting for transfers between devices: 18 us -> 13.6 us
    ppermute x60 -> x9, starting transfers between devices: 190 us -> 15.5 us  [permute(): return lax.ppermute(v, ('gx', 'gy'), send[name])]
    all_gather x2 -> x0, blocking collectives: 58.9 us -> none  [the longest x1 30.1 us: coarse_solve(): lax.all_gather(source[None], ('gx', 'gy'), axis=0, tiled=True)]
    pallas_call x0 -> x4, Pallas kernels: none -> 25.2 us  [the longest x1 19.8 us: per_device(): pl.pallas_call(functools.partial(second_kernel, tuple(bits)), out_shape=[...]
    another operation x4 -> x0, local copies, waits for them, and re-layouts: 22.3 us -> none  [material_fields(): jnp.stack([select_table(permittivity), select_table(mobility), potential,...]
    reduce_sum x9 -> x0, other arithmetic: 12.8 us -> none  [the longest x8 11.8 us: restrict_mean(): return jnp.sum(blocks, axis=(-5, -3, -1)) * 0.125]
    reshape x6 -> x0, local copies, waits for them, and re-layouts: 11.6 us -> none  [the longest x2 10.9 us: restrict_mean(): array.reshape(leading + (rows // 2, 2, columns // 2, 2, layers // 2, 2))]
    unnamed x12 -> x18, local copies, waits for them, and re-layouts: 0.23 us -> 5.33 us
    ppermute x60 -> x9, waiting for transfers between devices: 18 us -> 13.6 us  [permute(): return lax.ppermute(v, ('gx', 'gy'), send[name])]
  transfers between devices with their start and end apart: 60 -> 9, of which waited for: 25 -> 7; matrix products, arithmetic and copies ran while one was open for 5% -> 0% of each run, Pallas kernels for 0% -> 0%
where the time goes in v1:
time: 60.9 us; the launch traced here: 60.3 us
  Pallas kernels  25.2 us (41%)
  starting transfers between devices  15.5 us (25%)
  waiting for transfers between devices  13.6 us (22%)
  local copies, waits for them, and re-layouts  5.35 us (9%)
  between operations  0.68 us (1%)
    pallas_call x1, Pallas kernels, per_device(): pl.pallas_call(functools.partial(second_kernel, tuple(bits)), out_shape=[...  19.8 us
    ppermute x9, starting transfers between devices, permute(): return lax.ppermute(v, ('gx', 'gy'), send[name])  15.5 us
    ppermute x9, waiting for transfers between devices, permute(): return lax.ppermute(v, ('gx', 'gy'), send[name])  13.6 us
    unnamed x18, local copies, waits for them, and re-layouts  5.33 us
    pallas_call x1, Pallas kernels, per_device(): pl.pallas_call(first_kernel, out_shape=[shape(KEPT, total, rows, LANES),...  5.31 us
  transfers between devices with their start and end apart: 9, of which 7 were waited for; matrix products, arithmetic and copies ran while one was open for 0% of the time, Pallas kernels for 0%

profile of v1, /device:TPU:1, one launch (start us, length us, event | category | flops | bytes accessed | tf_op | source)
XLA Modules:
  0.0 60.3 jit_solution(4552291670734681371)
XLA Ops:
  0.6 0.0 copy-start
  0.6 0.8 %copy-done = s32[8,16,128]{2,1,0:T(8,128)S(1)} copy-done((s32[8,16,128]{2,1,0:T(8,128)S(1)}, s32[8,16,128]{2,1,0:T(8,128)}, u32[]{:S(2)}) %copy-start) | copy-done | bytes 65560
  1.5 0.0 copy-start.1
  1.5 0.8 %copy-done.1 = f32[8,16,128]{2,1,0:T(8,128)S(1)} copy-done((f32[8,16,128]{2,1,0:T(8,128)S(1)}, f32[8,16,128]{2,1,0:T(8,128)}, u32[]{:S(2)}) %copy-start.1) | copy-done | bytes 65560
  2.3 0.0 copy-start.2
  2.3 0.8 %copy-done.2 = f32[8,16,128]{2,1,0:T(8,128)S(1)} copy-done((f32[8,16,128]{2,1,0:T(8,128)S(1)}, f32[8,16,128]{2,1,0:T(8,128)}, u32[]{:S(2)}) %copy-start.2) | copy-done | bytes 65560
  3.2 0.0 copy-start.3
  3.2 0.8 %copy-done.3 = f32[8,16,128]{2,1,0:T(8,128)S(1)} copy-done((f32[8,16,128]{2,1,0:T(8,128)S(1)}, f32[8,16,128]{2,1,0:T(8,128)}, u32[]{:S(2)}) %copy-start.3) | copy-done | bytes 65560
  4.0 2.2 %collective-permute-start = (f32[2,8,8,128]{3,2,1,0:T(8,128)S(1)}, f32[2,8,8,128]{3,2,1,0:T(8,128)S(1)}, u32[]{:S(2)}, u32[]{:S(2)}) collective-permute-start(f32[2,8,8,128]{3,2,1,0:T(8,128)S(1)} %get-tuple-element.9), channel_id=1, source_target_pairs={{0,1},{1,0},{2,3},{3,2},{4,5},{5,4},{6,7},{7,6},{8,9},{9,8},{10,11... | collective-permute-start | bytes 196616 | tf_op jit(solution)/shard_map/ppermute | solution.py:509
  6.2 1.0 %collective-permute-start.1 = (f32[2,8,8,128]{3,2,1,0:T(8,128)S(1)}, f32[2,8,8,128]{3,2,1,0:T(8,128)S(1)}, u32[]{:S(2)}, u32[]{:S(2)}) collective-permute-start(f32[2,8,8,128]{3,2,1,0:T(8,128)S(1)} %get-tuple-element.10), channel_id=1, source_target_pairs={{0,4},{1,2},{2,1},{3,7},{4,0},{5,6},{6,5},{7,3},{8,12},{9,10},{10,... | collective-permute-start | bytes 196616 | tf_op jit(solution)/shard_map/ppermute | solution.py:509
  7.2 0.7 %collective-permute-done.in_a = f32[2,8,8,128]{3,2,1,0:T(8,128)S(1)} collective-permute-done((f32[2,8,8,128]{3,2,1,0:T(8,128)S(1)}, f32[2,8,8,128]{3,2,1,0:T(8,128)S(1)}, u32[]{:S(2)}, u32[]{:S(2)}) %collective-permute-start) | collective-permute-done | bytes 65568 | tf_op jit(solution)/shard_map/ppermute | solution.py:509
  7.9 0.2 collective-permute-done.1.in_b
  8.1 0.1 shard_map.87
  8.1 1.4 %collective-permute-start.2 = (f32[4,4,24,128]{3,2,1,0:T(8,128)S(1)}, f32[4,4,24,128]{3,2,1,0:T(8,128)S(1)}, u32[]{:S(2)}, u32[]{:S(2)}) collective-permute-start(f32[4,4,24,128]{3,2,1,0:T(8,128)S(1)} %get-tuple-element.12), channel_id=1, source_target_pairs={{0,4},{1,5},{2,6},{3,7},{4,0},{5,1},{6,2},{7,3},{8,12},{9,13},{10,... | collective-permute-start | bytes 589832 | tf_op jit(solution)/shard_map/ppermute | solution.py:509
  9.6 1.6 %collective-permute-start.3 = (f32[4,4,24,128]{3,2,1,0:T(8,128)S(1)}, f32[4,4,24,128]{3,2,1,0:T(8,128)S(1)}, u32[]{:S(2)}, u32[]{:S(2)}) collective-permute-start(f32[4,4,24,128]{3,2,1,0:T(8,128)S(1)} %get-tuple-element.13), channel_id=1, source_target_pairs={{0,1},{1,0},{2,3},{3,2},{4,8},{5,9},{6,10},{7,11},{8,4},{9,5},{10,... | collective-permute-start | bytes 589832 | tf_op jit(solution)/shard_map/ppermute | solution.py:509
  11.2 0.0 collective-permute-done.2.in_a
  11.2 3.8 %collective-permute-done.3.in_b = f32[4,4,24,128]{3,2,1,0:T(8,128)S(1)} collective-permute-done((f32[4,4,24,128]{3,2,1,0:T(8,128)S(1)}, f32[4,4,24,128]{3,2,1,0:T(8,128)S(1)}, u32[]{:S(2)}, u32[]{:S(2)}) %collective-permute-start.3) | collective-permute-done | bytes 196640 | tf_op jit(solution)/shard_map/ppermute | solution.py:509
  14.9 0.7 %copy-done.4 = f32[6]{0:T(128)S(1)} copy-done((f32[6]{0:T(128)S(1)}, f32[6]{0:T(128)}, u32[]{:S(2)}) %copy-start.4) | copy-done | bytes 48
  15.6 0.7 %copy-done.5 = f32[6]{0:T(128)S(1)} copy-done((f32[6]{0:T(128)S(1)}, f32[6]{0:T(128)}, u32[]{:S(2)}) %copy-start.5) | copy-done | bytes 48
  16.3 0.7 %copy-done.6 = f32[6]{0:T(128)S(1)} copy-done((f32[6]{0:T(128)S(1)}, f32[6]{0:T(128)}, u32[]{:S(2)}) %copy-start.6) | copy-done | bytes 48
  16.9 5.3 %shard_map.88 = (f32[15,16,24,128]{3,2,1,0:T(8,128)S(1)}, f32[3,4,8,128]{3,2,1,0:T(8,128)S(1)}) custom-call(f32[6]{0:T(128)S(1)} %copy-done.4, f32[6]{0:T(128)S(1)} %copy-done.5, f32[6]{0:T(128)S(1)} %copy-done.6, f32[4,8,24,128]{3,2,1,0:T(8,128)S(1)} %get-tuple-element.11.mid, f32[4,4,24,128]{3,2,1,0:T(8,128)S(1)} %collective-permute-done.2.in_a, ...), custom_call_target="tpu_custom_call" | custom-call | tf_op jit(solution)/shard_map/pallas_call | solution.py:537
  22.2 2.9 %collective-permute-start.4 = (f32[3,4,8,128]{3,2,1,0:T(8,128)S(1)}, f32[3,4,8,128]{3,2,1,0:T(8,128)S(1)}, u32[]{:S(2)}, u32[]{:S(2)}) collective-permute-start(f32[3,4,8,128]{3,2,1,0:T(8,128)S(1)} %get-tuple-element.14), channel_id=1, source_target_pairs={{0,1},{1,0},{2,3},{3,2},{4,5},{5,4},{6,7},{7,6},{8,9},{9,8},{10,11... | collective-permute-start | bytes 147464 | tf_op jit(solution)/shard_map/ppermute | solution.py:509
  25.1 1.5 %collective-permute-start.5 = (f32[3,4,8,128]{3,2,1,0:T(8,128)S(1)}, f32[3,4,8,128]{3,2,1,0:T(8,128)S(1)}, u32[]{:S(2)}, u32[]{:S(2)}) collective-permute-start(f32[3,4,8,128]{3,2,1,0:T(8,128)S(1)} %get-tuple-element.14), channel_id=1, source_target_pairs={{0,2},{1,3},{2,0},{3,1},{4,6},{5,7},{6,4},{7,5},{8,10},{9,11},{10,... | collective-permute-start | bytes 147464 | tf_op jit(solution)/shard_map/ppermute | solution.py:509
  26.6 1.1 %collective-permute-start.6 = (f32[3,4,8,128]{3,2,1,0:T(8,128)S(1)}, f32[3,4,8,128]{3,2,1,0:T(8,128)S(1)}, u32[]{:S(2)}, u32[]{:S(2)}) collective-permute-start(f32[3,4,8,128]{3,2,1,0:T(8,128)S(1)} %get-tuple-element.14), channel_id=1, source_target_pairs={{0,3},{1,2},{2,1},{3,0},{4,7},{5,6},{6,5},{7,4},{8,11},{9,10},{10,... | collective-permute-start | bytes 147464 | tf_op jit(solution)/shard_map/ppermute | solution.py:509
  27.7 0.0 collective-permute-done.4
  27.7 1.2 %collective-permute-done.5 = f32[3,4,8,128]{3,2,1,0:T(8,128)S(1)} collective-permute-done((f32[3,4,8,128]{3,2,1,0:T(8,128)S(1)}, f32[3,4,8,128]{3,2,1,0:T(8,128)S(1)}, u32[]{:S(2)}, u32[]{:S(2)}) %collective-permute-start.5) | collective-permute-done | bytes 49184 | tf_op jit(solution)/shard_map/ppermute | solution.py:509
  28.9 2.5 %collective-permute-done.6 = f32[3,4,8,128]{3,2,1,0:T(8,128)S(1)} collective-permute-done((f32[3,4,8,128]{3,2,1,0:T(8,128)S(1)}, f32[3,4,8,128]{3,2,1,0:T(8,128)S(1)}, u32[]{:S(2)}, u32[]{:S(2)}) %collective-permute-start.6) | collective-permute-done | bytes 49184 | tf_op jit(solution)/shard_map/ppermute | solution.py:509
  31.4 0.7 %collective-permute-start.7 = (f32[4,3,4,8,128]{4,3,2,1,0:T(8,128)S(1)}, f32[4,3,4,8,128]{4,3,2,1,0:T(8,128)S(1)}, u32[]{:S(2)}, u32[]{:S(2)}) collective-permute-start(f32[4,3,4,8,128]{4,3,2,1,0:T(8,128)S(1)} %pad_maximum_fusion), channel_id=1, source_target_pairs={{0,8},{1,9},{2,10},{3,11},{4,12},{5,13},{6,14},{7,15},{8,0},{9,1},... | collective-permute-start | bytes 589832 | tf_op jit(solution)/shard_map/ppermute | solution.py:509
  32.1 3.9 %collective-permute-done.7 = f32[4,3,4,8,128]{4,3,2,1,0:T(8,128)S(1)} collective-permute-done((f32[4,3,4,8,128]{4,3,2,1,0:T(8,128)S(1)}, f32[4,3,4,8,128]{4,3,2,1,0:T(8,128)S(1)}, u32[]{:S(2)}, u32[]{:S(2)}) %collective-permute-start.7) | collective-permute-done | bytes 196640 | tf_op jit(solution)/shard_map/ppermute | solution.py:509
  36.0 3.1 %collective-permute-start.8 = (f32[8,3,4,8,128]{4,3,2,1,0:T(8,128)S(1)}, f32[8,3,4,8,128]{4,3,2,1,0:T(8,128)S(1)}, u32[]{:S(2)}, u32[]{:S(2)}) collective-permute-start(f32[8,3,4,8,128]{4,3,2,1,0:T(8,128)S(1)} %constant_dynamic-update-slice_fusion.near), channel_id=1, source_target_pairs={{0,4},{1,5},{2,6},{3,7},{4,0},{5,1},{6,2},{7,3},{8,12},{9,13},{10,... | collective-permute-start | bytes 1179656 | tf_op jit(solution)/shard_map/ppermute | solution.py:509
  39.1 1.3 %collective-permute-done.8.far = f32[8,3,4,8,128]{4,3,2,1,0:T(8,128)S(1)} collective-permute-done((f32[8,3,4,8,128]{4,3,2,1,0:T(8,128)S(1)}, f32[8,3,4,8,128]{4,3,2,1,0:T(8,128)S(1)}, u32[]{:S(2)}, u32[]{:S(2)}) %collective-permute-start.8) | collective-permute-done | bytes 393248 | tf_op jit(solution)/shard_map/ppermute | solution.py:509
  40.5 19.8 %shard_map.89 = (f32[8,16,128]{2,1,0:T(8,128)}, f32[8,16,128]{2,1,0:T(8,128)}) custom-call(f32[8,3,4,8,128]{4,3,2,1,0:T(8,128)S(1)} %constant_dynamic-update-slice_fusion.near, f32[8,3,4,8,128]{4,3,2,1,0:T(8,128)S(1)} %collective-permute-done.8.far, f32[15,16,24,128]{3,2,1,0:T(8,128)S(1)} %get-tuple-element.15.kept), custom_call_target="tpu_custom_call" | custom-call | tf_op jit(solution)/shard_map/pallas_call | solution.py:569
  (10 shorter events, 0.1 us)
Async XLA Ops:
  0.6 0.8 %copy-start = (s32[8,16,128]{2,1,0:T(8,128)S(1)}, s32[8,16,128]{2,1,0:T(8,128)}, u32[]{:S(2)}) copy-start(s32[8,16,128]{2,1,0:T(8,128)} %cls.3) | copy-start | bytes 196612
  1.5 0.8 %copy-start.1 = (f32[8,16,128]{2,1,0:T(8,128)S(1)}, f32[8,16,128]{2,1,0:T(8,128)}, u32[]{:S(2)}) copy-start(f32[8,16,128]{2,1,0:T(8,128)} %pot.3) | copy-start | bytes 196612
  2.3 0.8 %copy-start.2 = (f32[8,16,128]{2,1,0:T(8,128)S(1)}, f32[8,16,128]{2,1,0:T(8,128)}, u32[]{:S(2)}) copy-start(f32[8,16,128]{2,1,0:T(8,128)} %fp.3) | copy-start | bytes 196612
  3.2 0.8 %copy-start.3 = (f32[8,16,128]{2,1,0:T(8,128)S(1)}, f32[8,16,128]{2,1,0:T(8,128)}, u32[]{:S(2)}) copy-start(f32[8,16,128]{2,1,0:T(8,128)} %fn.3) | copy-start | bytes 196612
  4.0 3.8 %collective-permute-start = (f32[2,8,8,128]{3,2,1,0:T(8,128)S(1)}, f32[2,8,8,128]{3,2,1,0:T(8,128)S(1)}, u32[]{:S(2)}, u32[]{:S(2)}) collective-permute-start(f32[2,8,8,128]{3,2,1,0:T(8,128)S(1)} %get-tuple-element.9), channel_id=1, source_target_pairs={{0,1},{1,0},{2,3},{3,2},{4,5},{5,4},{6,7},{7,6},{8,9},{9,8},{10,11... | collective-permute-start | bytes 196616 | tf_op jit(solution)/shard_map/ppermute | solution.py:509
  6.2 1.9 %collective-permute-start.1 = (f32[2,8,8,128]{3,2,1,0:T(8,128)S(1)}, f32[2,8,8,128]{3,2,1,0:T(8,128)S(1)}, u32[]{:S(2)}, u32[]{:S(2)}) collective-permute-start(f32[2,8,8,128]{3,2,1,0:T(8,128)S(1)} %get-tuple-element.10), channel_id=1, source_target_pairs={{0,4},{1,2},{2,1},{3,7},{4,0},{5,6},{6,5},{7,3},{8,12},{9,10},{10,... | collective-permute-start | bytes 196616 | tf_op jit(solution)/shard_map/ppermute | solution.py:509
  8.1 3.0 %collective-permute-start.2 = (f32[4,4,24,128]{3,2,1,0:T(8,128)S(1)}, f32[4,4,24,128]{3,2,1,0:T(8,128)S(1)}, u32[]{:S(2)}, u32[]{:S(2)}) collective-permute-start(f32[4,4,24,128]{3,2,1,0:T(8,128)S(1)} %get-tuple-element.12), channel_id=1, source_target_pairs={{0,4},{1,5},{2,6},{3,7},{4,0},{5,1},{6,2},{7,3},{8,12},{9,13},{10,... | collective-permute-start | bytes 589832 | tf_op jit(solution)/shard_map/ppermute | solution.py:509
  9.6 5.4 %collective-permute-start.3 = (f32[4,4,24,128]{3,2,1,0:T(8,128)S(1)}, f32[4,4,24,128]{3,2,1,0:T(8,128)S(1)}, u32[]{:S(2)}, u32[]{:S(2)}) collective-permute-start(f32[4,4,24,128]{3,2,1,0:T(8,128)S(1)} %get-tuple-element.13), channel_id=1, source_target_pairs={{0,1},{1,0},{2,3},{3,2},{4,8},{5,9},{6,10},{7,11},{8,4},{9,5},{10,... | collective-permute-start | bytes 589832 | tf_op jit(solution)/shard_map/ppermute | solution.py:509
  14.9 0.7 %copy-start.4 = (f32[6]{0:T(128)S(1)}, f32[6]{0:T(128)}, u32[]{:S(2)}) copy-start(f32[6]{0:T(128)} %eps_t.1) | copy-start | bytes 76
  15.6 0.7 %copy-start.5 = (f32[6]{0:T(128)S(1)}, f32[6]{0:T(128)}, u32[]{:S(2)}) copy-start(f32[6]{0:T(128)} %mob_t.1) | copy-start | bytes 76
  16.3 0.7 %copy-start.6 = (f32[6]{0:T(128)S(1)}, f32[6]{0:T(128)}, u32[]{:S(2)}) copy-start(f32[6]{0:T(128)} %cap_t.1) | copy-start | bytes 76
  22.2 5.5 %collective-permute-start.4 = (f32[3,4,8,128]{3,2,1,0:T(8,128)S(1)}, f32[3,4,8,128]{3,2,1,0:T(8,128)S(1)}, u32[]{:S(2)}, u32[]{:S(2)}) collective-permute-start(f32[3,4,8,128]{3,2,1,0:T(8,128)S(1)} %get-tuple-element.14), channel_id=1, source_target_pairs={{0,1},{1,0},{2,3},{3,2},{4,5},{5,4},{6,7},{7,6},{8,9},{9,8},{10,11... | collective-permute-start | bytes 147464 | tf_op jit(solution)/shard_map/ppermute | solution.py:509
  25.1 3.8 %collective-permute-start.5 = (f32[3,4,8,128]{3,2,1,0:T(8,128)S(1)}, f32[3,4,8,128]{3,2,1,0:T(8,128)S(1)}, u32[]{:S(2)}, u32[]{:S(2)}) collective-permute-start(f32[3,4,8,128]{3,2,1,0:T(8,128)S(1)} %get-tuple-element.14), channel_id=1, source_target_pairs={{0,2},{1,3},{2,0},{3,1},{4,6},{5,7},{6,4},{7,5},{8,10},{9,11},{10,... | collective-permute-start | bytes 147464 | tf_op jit(solution)/shard_map/ppermute | solution.py:509
  26.6 4.8 %collective-permute-start.6 = (f32[3,4,8,128]{3,2,1,0:T(8,128)S(1)}, f32[3,4,8,128]{3,2,1,0:T(8,128)S(1)}, u32[]{:S(2)}, u32[]{:S(2)}) collective-permute-start(f32[3,4,8,128]{3,2,1,0:T(8,128)S(1)} %get-tuple-element.14), channel_id=1, source_target_pairs={{0,3},{1,2},{2,1},{3,0},{4,7},{5,6},{6,5},{7,4},{8,11},{9,10},{10,... | collective-permute-start | bytes 147464 | tf_op jit(solution)/shard_map/ppermute | solution.py:509
  31.4 4.6 %collective-permute-start.7 = (f32[4,3,4,8,128]{4,3,2,1,0:T(8,128)S(1)}, f32[4,3,4,8,128]{4,3,2,1,0:T(8,128)S(1)}, u32[]{:S(2)}, u32[]{:S(2)}) collective-permute-start(f32[4,3,4,8,128]{4,3,2,1,0:T(8,128)S(1)} %pad_maximum_fusion), channel_id=1, source_target_pairs={{0,8},{1,9},{2,10},{3,11},{4,12},{5,13},{6,14},{7,15},{8,0},{9,1},... | collective-permute-start | bytes 589832 | tf_op jit(solution)/shard_map/ppermute | solution.py:509
  36.0 4.5 %collective-permute-start.8 = (f32[8,3,4,8,128]{4,3,2,1,0:T(8,128)S(1)}, f32[8,3,4,8,128]{4,3,2,1,0:T(8,128)S(1)}, u32[]{:S(2)}, u32[]{:S(2)}) collective-permute-start(f32[8,3,4,8,128]{4,3,2,1,0:T(8,128)S(1)} %constant_dynamic-update-slice_fusion.near), channel_id=1, source_target_pairs={{0,4},{1,5},{2,6},{3,7},{4,0},{5,1},{6,2},{7,3},{8,12},{9,13},{10,... | collective-permute-start | bytes 1179656 | tf_op jit(solution)/shard_map/ppermute | solution.py:509

commit v2 on v1

--- a/solution.py
+++ b/solution.py
@@ -12,6 +12,17 @@
 LANES = 128
 VMEM = pl.BlockSpec(memory_space=pltpu.VMEM)
 SMEM = pl.BlockSpec(memory_space=pltpu.SMEM)
+
+
+UNROLL = 16
+
+
+def loop(first, end, body, init):
+    if end - first > UNROLL:
+        return lax.fori_loop(first, end, body, init)
+    for i in range(first, end):
+        body(i, 0)
+    return init
 
 
 def params(mib):
@@ -100,7 +111,7 @@
     return jnp.where(lane < LANES // 2, a, b)
 
 
-def first_kernel(eps_t, mob_t, cap_t, mid, in_a, in_b, kept, block, fld, work, tmp):
+def first_kernel(eps_t, mob_t, cap_t, mid, in_a, in_b, kept, block, fld, work):
     x, nx = lax.axis_index("gx"), lax.axis_size("gx")
     even = x % 2 == 0
     planes = mid.shape[1]
@@ -137,9 +148,9 @@
         )
         return 0
 
-    lax.fori_loop(0, RIM, low, 0)
-    lax.fori_loop(0, planes, middle, 0)
-    lax.fori_loop(0, RIM, high, 0)
+    loop(0, RIM, low, 0)
+    loop(0, planes, middle, 0)
+    loop(0, RIM, high, 0)
 
     shape = (rows, LANES)
     lane = iota(shape, 1)
@@ -184,7 +195,7 @@
         fld[D_P, i], fld[D_N, i] = d_p, d_n
         return 0
 
-    lax.fori_loop(1, total - 1, operators, 0)
+    loop(1, total - 1, operators, 0)
 
     def sweep(i, _):
         for poisson, w, wf, u in ((True, W_P, WF_P, U_P), (False, W_N, WF_N, U_N)):
@@ -192,15 +203,11 @@
             kept[u, i] = (2.0 - OMEGA) * kept[wf, i] + kept[w, i] * s
         return 0
 
-    lax.fori_loop(2, total - 2, sweep, 0)
+    loop(2, total - 2, sweep, 0)
 
     def residual(i, poisson, f, d, u):
         s = coupled_fine(kept, lambda j: kept[u, j], i, poisson)
         return fld[f, i] - fld[d, i] * kept[u, i] + s
-
-    def halved(v):
-        tmp[...] = v
-        return tmp[0 : own : 2, :] + tmp[1 : own : 2, :]
 
     def coarse(i, _):
         at = RIM + 2 * i
@@ -217,7 +224,7 @@
             block[(2, 0, 1)[k], i] = 0.125 * halve_lanes(even_odd[2 * k], even_odd[2 * k + 1])
         return 0
 
-    lax.fori_loop(0, planes // 2, coarse, 0)
+    loop(0, planes // 2, coarse, 0)
 
 
 def low_lane(shape, bit):
@@ -261,7 +268,7 @@
             self.xp[i], self.xm[i] = kb, kb + k * delta
             return 0
 
-        lax.fori_loop(1, nx, x_face, 0)
+        loop(1, nx, x_face, 0)
 
         def plane(i, _):
             eps, pot = self.eps[i], self.pot[i]
@@ -281,7 +288,7 @@
             self.d[i], self.w[i] = d, w
             return 0
 
-        lax.fori_loop(0, nx, plane, 0)
+        loop(0, nx, plane, 0)
 
     def coupled(self, u, i):
         v = u[i + 1]
@@ -296,14 +303,14 @@
             self.u[i + 1] = wf
             return 0
 
-        lax.fori_loop(0, self.nx, body, 0)
+        loop(0, self.nx, body, 0)
 
     def sweep(self, u, v):
         def body(i, _):
             v[i + 1] = (1.0 - OMEGA) * u[i + 1] + self.wf[i] + self.w[i] * self.coupled(u, i)
             return 0
 
-        lax.fori_loop(0, self.nx, body, 0)
+        loop(0, self.nx, body, 0)
 
     def halve(self, tmp, v):
         step, ny = self.step, self.ny
@@ -318,7 +325,7 @@
                 there[i] = self.halve(tmp, here[2 * i] + here[2 * i + 1])
             return 0
 
-        lax.fori_loop(0, coarser.nx, body, 0)
+        loop(0, coarser.nx, body, 0)
 
     def descend_residual(self, u, coarser, tmp):
         def residual(i):
@@ -328,7 +335,7 @@
             coarser.f[i] = self.halve(tmp, residual(2 * i) + residual(2 * i + 1))
             return 0
 
-        lax.fori_loop(0, coarser.nx, body, 0)
+        loop(0, coarser.nx, body, 0)
 
     def correct(self, u, coarser_u, tmp):
         half_ny = self.ny // 2
@@ -342,7 +349,7 @@
             u[2 * i + 2] = u[2 * i + 2] + wide
             return 0
 
-        lax.fori_loop(0, self.nx // 2, body, 0)
+        loop(0, self.nx // 2, body, 0)
 
 
 def coarsest(lv):
@@ -400,7 +407,7 @@
                 l1.f[at, row, :] = ref[m, 2, i]
             return 0
 
-        lax.fori_loop(0, half, body, 0)
+        loop(0, half, body, 0)
 
     place(near, 0)
     place(far, bits[-1])
@@ -432,7 +439,7 @@
         )
         return 0
 
-    lax.fori_loop(0, n1x, last, 0)
+    loop(0, n1x, last, 0)
 
     rows = kept.shape[2]
     own = rows - 2 * RIM
@@ -463,7 +470,7 @@
                 fine_a[channel, p] = kept[u, p] + e
         return 0
 
-    lax.fori_loop(0, bx + 2, correct, 0)
+    loop(0, bx + 2, correct, 0)
 
     def fine(u, channel, i):
         w, wf = ((W_P, WF_P), (W_N, WF_N))[channel]
@@ -480,8 +487,8 @@
         out_n[i] = fine(fine_b, 1, i + RIM)[0:own]
         return 0
 
-    lax.fori_loop(RIM - 1, RIM + 2 * bx + 1, post_one, 0)
-    lax.fori_loop(0, 2 * bx, post_two, 0)
+    loop(RIM - 1, RIM + 2 * bx + 1, post_one, 0)
+    loop(0, 2 * bx, post_two, 0)
 
 
 def moves(nx, ny):
@@ -542,7 +549,6 @@
         scratch_shapes=[
             pltpu.VMEM((8, total, rows, LANES), f32),
             pltpu.VMEM((6, own, LANES), f32),
-            pltpu.VMEM((rows, LANES), f32),
         ],
         compiler_params=params(24),
     )(permittivity, mobility, capture, mid, a, b)

time: 60.9 us -> 44.8 us (0.74)
  Pallas kernels: 25.2 us -> 9 us
    pallas_call x1, Pallas kernels: 19.8 us -> 6.61 us  [per_device(): pl.pallas_call(functools.partial(second_kernel, tuple(bits)), out_shape=[...]
    pallas_call x1, Pallas kernels: 5.31 us -> 2.29 us  [per_device(): pl.pallas_call(first_kernel, out_shape=[shape(KEPT, total, rows, LANES),...]
where the time goes in v2:
time: 44.8 us; the launch traced here: 44.1 us
  starting transfers between devices  15.5 us (35%)
  waiting for transfers between devices  13.6 us (30%)
  Pallas kernels  9 us (20%)
  local copies, waits for them, and re-layouts  5.35 us (12%)
  between operations  0.69 us (2%)
    ppermute x9, starting transfers between devices, permute(): return lax.ppermute(v, ('gx', 'gy'), send[name])  15.5 us
    ppermute x9, waiting for transfers between devices, permute(): return lax.ppermute(v, ('gx', 'gy'), send[name])  13.6 us
    pallas_call x1, Pallas kernels, per_device(): pl.pallas_call(functools.partial(second_kernel, tuple(bits)), out_shape=[...  6.61 us
    unnamed x18, local copies, waits for them, and re-layouts  5.33 us
    pallas_call x1, Pallas kernels, per_device(): pl.pallas_call(first_kernel, out_shape=[shape(KEPT, total, rows, LANES),...  2.29 us
  transfers between devices with their start and end apart: 9, of which 7 were waited for; matrix products, arithmetic and copies ran while one was open for 0% of the time, Pallas kernels for 0%

profile of v2, /device:TPU:1, one launch (start us, length us, event | category | flops | bytes accessed | tf_op | source)
XLA Modules:
  0.0 44.1 jit_solution(14655530125259664327)
XLA Ops:
  0.6 0.0 copy-start
  0.6 0.8 %copy-done = s32[8,16,128]{2,1,0:T(8,128)S(1)} copy-done((s32[8,16,128]{2,1,0:T(8,128)S(1)}, s32[8,16,128]{2,1,0:T(8,128)}, u32[]{:S(2)}) %copy-start) | copy-done | bytes 65560
  1.5 0.0 copy-start.1
  1.5 0.8 %copy-done.1 = f32[8,16,128]{2,1,0:T(8,128)S(1)} copy-done((f32[8,16,128]{2,1,0:T(8,128)S(1)}, f32[8,16,128]{2,1,0:T(8,128)}, u32[]{:S(2)}) %copy-start.1) | copy-done | bytes 65560
  2.3 0.0 copy-start.2
  2.3 0.8 %copy-done.2 = f32[8,16,128]{2,1,0:T(8,128)S(1)} copy-done((f32[8,16,128]{2,1,0:T(8,128)S(1)}, f32[8,16,128]{2,1,0:T(8,128)}, u32[]{:S(2)}) %copy-start.2) | copy-done | bytes 65560
  3.2 0.0 copy-start.3
  3.2 0.8 %copy-done.3 = f32[8,16,128]{2,1,0:T(8,128)S(1)} copy-done((f32[8,16,128]{2,1,0:T(8,128)S(1)}, f32[8,16,128]{2,1,0:T(8,128)}, u32[]{:S(2)}) %copy-start.3) | copy-done | bytes 65560
  4.0 2.2 %collective-permute-start = (f32[2,8,8,128]{3,2,1,0:T(8,128)S(1)}, f32[2,8,8,128]{3,2,1,0:T(8,128)S(1)}, u32[]{:S(2)}, u32[]{:S(2)}) collective-permute-start(f32[2,8,8,128]{3,2,1,0:T(8,128)S(1)} %get-tuple-element.9), channel_id=1, source_target_pairs={{0,1},{1,0},{2,3},{3,2},{4,5},{5,4},{6,7},{7,6},{8,9},{9,8},{10,11... | collective-permute-start | bytes 196616 | tf_op jit(solution)/shard_map/ppermute | solution.py:516
  6.2 1.0 %collective-permute-start.1 = (f32[2,8,8,128]{3,2,1,0:T(8,128)S(1)}, f32[2,8,8,128]{3,2,1,0:T(8,128)S(1)}, u32[]{:S(2)}, u32[]{:S(2)}) collective-permute-start(f32[2,8,8,128]{3,2,1,0:T(8,128)S(1)} %get-tuple-element.10), channel_id=1, source_target_pairs={{0,4},{1,2},{2,1},{3,7},{4,0},{5,6},{6,5},{7,3},{8,12},{9,10},{10,... | collective-permute-start | bytes 196616 | tf_op jit(solution)/shard_map/ppermute | solution.py:516
  7.2 0.7 %collective-permute-done.in_a = f32[2,8,8,128]{3,2,1,0:T(8,128)S(1)} collective-permute-done((f32[2,8,8,128]{3,2,1,0:T(8,128)S(1)}, f32[2,8,8,128]{3,2,1,0:T(8,128)S(1)}, u32[]{:S(2)}, u32[]{:S(2)}) %collective-permute-start) | collective-permute-done | bytes 65568 | tf_op jit(solution)/shard_map/ppermute | solution.py:516
  7.9 0.2 collective-permute-done.1.in_b
  8.1 0.1 shard_map.87
  8.1 1.4 %collective-permute-start.2 = (f32[4,4,24,128]{3,2,1,0:T(8,128)S(1)}, f32[4,4,24,128]{3,2,1,0:T(8,128)S(1)}, u32[]{:S(2)}, u32[]{:S(2)}) collective-permute-start(f32[4,4,24,128]{3,2,1,0:T(8,128)S(1)} %get-tuple-element.12), channel_id=1, source_target_pairs={{0,4},{1,5},{2,6},{3,7},{4,0},{5,1},{6,2},{7,3},{8,12},{9,13},{10,... | collective-permute-start | bytes 589832 | tf_op jit(solution)/shard_map/ppermute | solution.py:516
  9.6 1.6 %collective-permute-start.3 = (f32[4,4,24,128]{3,2,1,0:T(8,128)S(1)}, f32[4,4,24,128]{3,2,1,0:T(8,128)S(1)}, u32[]{:S(2)}, u32[]{:S(2)}) collective-permute-start(f32[4,4,24,128]{3,2,1,0:T(8,128)S(1)} %get-tuple-element.13), channel_id=1, source_target_pairs={{0,1},{1,0},{2,3},{3,2},{4,8},{5,9},{6,10},{7,11},{8,4},{9,5},{10,... | collective-permute-start | bytes 589832 | tf_op jit(solution)/shard_map/ppermute | solution.py:516
  11.2 0.0 collective-permute-done.2.in_a
  11.2 3.8 %collective-permute-done.3.in_b = f32[4,4,24,128]{3,2,1,0:T(8,128)S(1)} collective-permute-done((f32[4,4,24,128]{3,2,1,0:T(8,128)S(1)}, f32[4,4,24,128]{3,2,1,0:T(8,128)S(1)}, u32[]{:S(2)}, u32[]{:S(2)}) %collective-permute-start.3) | collective-permute-done | bytes 196640 | tf_op jit(solution)/shard_map/ppermute | solution.py:516
  14.9 0.7 %copy-done.4 = f32[6]{0:T(128)S(1)} copy-done((f32[6]{0:T(128)S(1)}, f32[6]{0:T(128)}, u32[]{:S(2)}) %copy-start.4) | copy-done | bytes 48
  15.6 0.7 %copy-done.5 = f32[6]{0:T(128)S(1)} copy-done((f32[6]{0:T(128)S(1)}, f32[6]{0:T(128)}, u32[]{:S(2)}) %copy-start.5) | copy-done | bytes 48
  16.3 0.7 %copy-done.6 = f32[6]{0:T(128)S(1)} copy-done((f32[6]{0:T(128)S(1)}, f32[6]{0:T(128)}, u32[]{:S(2)}) %copy-start.6) | copy-done | bytes 48
  16.9 2.3 %shard_map.88 = (f32[15,16,24,128]{3,2,1,0:T(8,128)S(1)}, f32[3,4,8,128]{3,2,1,0:T(8,128)S(1)}) custom-call(f32[6]{0:T(128)S(1)} %copy-done.4, f32[6]{0:T(128)S(1)} %copy-done.5, f32[6]{0:T(128)S(1)} %copy-done.6, f32[4,8,24,128]{3,2,1,0:T(8,128)S(1)} %get-tuple-element.11.mid, f32[4,4,24,128]{3,2,1,0:T(8,128)S(1)} %collective-permute-done.2.in_a, ...), custom_call_target="tpu_custom_call" | custom-call | tf_op jit(solution)/shard_map/pallas_call | solution.py:544
  19.2 2.9 %collective-permute-start.4 = (f32[3,4,8,128]{3,2,1,0:T(8,128)S(1)}, f32[3,4,8,128]{3,2,1,0:T(8,128)S(1)}, u32[]{:S(2)}, u32[]{:S(2)}) collective-permute-start(f32[3,4,8,128]{3,2,1,0:T(8,128)S(1)} %get-tuple-element.14), channel_id=1, source_target_pairs={{0,1},{1,0},{2,3},{3,2},{4,5},{5,4},{6,7},{7,6},{8,9},{9,8},{10,11... | collective-permute-start | bytes 147464 | tf_op jit(solution)/shard_map/ppermute | solution.py:516
  22.1 1.5 %collective-permute-start.5 = (f32[3,4,8,128]{3,2,1,0:T(8,128)S(1)}, f32[3,4,8,128]{3,2,1,0:T(8,128)S(1)}, u32[]{:S(2)}, u32[]{:S(2)}) collective-permute-start(f32[3,4,8,128]{3,2,1,0:T(8,128)S(1)} %get-tuple-element.14), channel_id=1, source_target_pairs={{0,2},{1,3},{2,0},{3,1},{4,6},{5,7},{6,4},{7,5},{8,10},{9,11},{10,... | collective-permute-start | bytes 147464 | tf_op jit(solution)/shard_map/ppermute | solution.py:516
  23.6 1.1 %collective-permute-start.6 = (f32[3,4,8,128]{3,2,1,0:T(8,128)S(1)}, f32[3,4,8,128]{3,2,1,0:T(8,128)S(1)}, u32[]{:S(2)}, u32[]{:S(2)}) collective-permute-start(f32[3,4,8,128]{3,2,1,0:T(8,128)S(1)} %get-tuple-element.14), channel_id=1, source_target_pairs={{0,3},{1,2},{2,1},{3,0},{4,7},{5,6},{6,5},{7,4},{8,11},{9,10},{10,... | collective-permute-start | bytes 147464 | tf_op jit(solution)/shard_map/ppermute | solution.py:516
  24.8 0.0 collective-permute-done.4
  24.8 1.2 %collective-permute-done.5 = f32[3,4,8,128]{3,2,1,0:T(8,128)S(1)} collective-permute-done((f32[3,4,8,128]{3,2,1,0:T(8,128)S(1)}, f32[3,4,8,128]{3,2,1,0:T(8,128)S(1)}, u32[]{:S(2)}, u32[]{:S(2)}) %collective-permute-start.5) | collective-permute-done | bytes 49184 | tf_op jit(solution)/shard_map/ppermute | solution.py:516
  26.0 2.5 %collective-permute-done.6 = f32[3,4,8,128]{3,2,1,0:T(8,128)S(1)} collective-permute-done((f32[3,4,8,128]{3,2,1,0:T(8,128)S(1)}, f32[3,4,8,128]{3,2,1,0:T(8,128)S(1)}, u32[]{:S(2)}, u32[]{:S(2)}) %collective-permute-start.6) | collective-permute-done | bytes 49184 | tf_op jit(solution)/shard_map/ppermute | solution.py:516
  28.5 0.7 %collective-permute-start.7 = (f32[4,3,4,8,128]{4,3,2,1,0:T(8,128)S(1)}, f32[4,3,4,8,128]{4,3,2,1,0:T(8,128)S(1)}, u32[]{:S(2)}, u32[]{:S(2)}) collective-permute-start(f32[4,3,4,8,128]{4,3,2,1,0:T(8,128)S(1)} %pad_maximum_fusion), channel_id=1, source_target_pairs={{0,8},{1,9},{2,10},{3,11},{4,12},{5,13},{6,14},{7,15},{8,0},{9,1},... | collective-permute-start | bytes 589832 | tf_op jit(solution)/shard_map/ppermute | solution.py:516
  29.2 3.9 %collective-permute-done.7 = f32[4,3,4,8,128]{4,3,2,1,0:T(8,128)S(1)} collective-permute-done((f32[4,3,4,8,128]{4,3,2,1,0:T(8,128)S(1)}, f32[4,3,4,8,128]{4,3,2,1,0:T(8,128)S(1)}, u32[]{:S(2)}, u32[]{:S(2)}) %collective-permute-start.7) | collective-permute-done | bytes 196640 | tf_op jit(solution)/shard_map/ppermute | solution.py:516
  33.1 3.1 %collective-permute-start.8 = (f32[8,3,4,8,128]{4,3,2,1,0:T(8,128)S(1)}, f32[8,3,4,8,128]{4,3,2,1,0:T(8,128)S(1)}, u32[]{:S(2)}, u32[]{:S(2)}) collective-permute-start(f32[8,3,4,8,128]{4,3,2,1,0:T(8,128)S(1)} %constant_dynamic-update-slice_fusion.near), channel_id=1, source_target_pairs={{0,4},{1,5},{2,6},{3,7},{4,0},{5,1},{6,2},{7,3},{8,12},{9,13},{10,... | collective-permute-start | bytes 1179656 | tf_op jit(solution)/shard_map/ppermute | solution.py:516
  36.2 1.3 %collective-permute-done.8.far = f32[8,3,4,8,128]{4,3,2,1,0:T(8,128)S(1)} collective-permute-done((f32[8,3,4,8,128]{4,3,2,1,0:T(8,128)S(1)}, f32[8,3,4,8,128]{4,3,2,1,0:T(8,128)S(1)}, u32[]{:S(2)}, u32[]{:S(2)}) %collective-permute-start.8) | collective-permute-done | bytes 393248 | tf_op jit(solution)/shard_map/ppermute | solution.py:516
  37.5 6.6 %shard_map.89 = (f32[8,16,128]{2,1,0:T(8,128)}, f32[8,16,128]{2,1,0:T(8,128)}) custom-call(f32[8,3,4,8,128]{4,3,2,1,0:T(8,128)S(1)} %constant_dynamic-update-slice_fusion.near, f32[8,3,4,8,128]{4,3,2,1,0:T(8,128)S(1)} %collective-permute-done.8.far, f32[15,16,24,128]{3,2,1,0:T(8,128)S(1)} %get-tuple-element.15.kept), custom_call_target="tpu_custom_call" | custom-call | tf_op jit(solution)/shard_map/pallas_call | solution.py:575
  (10 shorter events, 0.1 us)
Async XLA Ops:
  0.6 0.8 %copy-start = (s32[8,16,128]{2,1,0:T(8,128)S(1)}, s32[8,16,128]{2,1,0:T(8,128)}, u32[]{:S(2)}) copy-start(s32[8,16,128]{2,1,0:T(8,128)} %cls.3) | copy-start | bytes 196612
  1.5 0.8 %copy-start.1 = (f32[8,16,128]{2,1,0:T(8,128)S(1)}, f32[8,16,128]{2,1,0:T(8,128)}, u32[]{:S(2)}) copy-start(f32[8,16,128]{2,1,0:T(8,128)} %pot.3) | copy-start | bytes 196612
  2.3 0.8 %copy-start.2 = (f32[8,16,128]{2,1,0:T(8,128)S(1)}, f32[8,16,128]{2,1,0:T(8,128)}, u32[]{:S(2)}) copy-start(f32[8,16,128]{2,1,0:T(8,128)} %fp.3) | copy-start | bytes 196612
  3.2 0.8 %copy-start.3 = (f32[8,16,128]{2,1,0:T(8,128)S(1)}, f32[8,16,128]{2,1,0:T(8,128)}, u32[]{:S(2)}) copy-start(f32[8,16,128]{2,1,0:T(8,128)} %fn.3) | copy-start | bytes 196612
  4.0 3.8 %collective-permute-start = (f32[2,8,8,128]{3,2,1,0:T(8,128)S(1)}, f32[2,8,8,128]{3,2,1,0:T(8,128)S(1)}, u32[]{:S(2)}, u32[]{:S(2)}) collective-permute-start(f32[2,8,8,128]{3,2,1,0:T(8,128)S(1)} %get-tuple-element.9), channel_id=1, source_target_pairs={{0,1},{1,0},{2,3},{3,2},{4,5},{5,4},{6,7},{7,6},{8,9},{9,8},{10,11... | collective-permute-start | bytes 196616 | tf_op jit(solution)/shard_map/ppermute | solution.py:516
  6.2 1.9 %collective-permute-start.1 = (f32[2,8,8,128]{3,2,1,0:T(8,128)S(1)}, f32[2,8,8,128]{3,2,1,0:T(8,128)S(1)}, u32[]{:S(2)}, u32[]{:S(2)}) collective-permute-start(f32[2,8,8,128]{3,2,1,0:T(8,128)S(1)} %get-tuple-element.10), channel_id=1, source_target_pairs={{0,4},{1,2},{2,1},{3,7},{4,0},{5,6},{6,5},{7,3},{8,12},{9,10},{10,... | collective-permute-start | bytes 196616 | tf_op jit(solution)/shard_map/ppermute | solution.py:516
  8.1 3.0 %collective-permute-start.2 = (f32[4,4,24,128]{3,2,1,0:T(8,128)S(1)}, f32[4,4,24,128]{3,2,1,0:T(8,128)S(1)}, u32[]{:S(2)}, u32[]{:S(2)}) collective-permute-start(f32[4,4,24,128]{3,2,1,0:T(8,128)S(1)} %get-tuple-element.12), channel_id=1, source_target_pairs={{0,4},{1,5},{2,6},{3,7},{4,0},{5,1},{6,2},{7,3},{8,12},{9,13},{10,... | collective-permute-start | bytes 589832 | tf_op jit(solution)/shard_map/ppermute | solution.py:516
  9.6 5.4 %collective-permute-start.3 = (f32[4,4,24,128]{3,2,1,0:T(8,128)S(1)}, f32[4,4,24,128]{3,2,1,0:T(8,128)S(1)}, u32[]{:S(2)}, u32[]{:S(2)}) collective-permute-start(f32[4,4,24,128]{3,2,1,0:T(8,128)S(1)} %get-tuple-element.13), channel_id=1, source_target_pairs={{0,1},{1,0},{2,3},{3,2},{4,8},{5,9},{6,10},{7,11},{8,4},{9,5},{10,... | collective-permute-start | bytes 589832 | tf_op jit(solution)/shard_map/ppermute | solution.py:516
  14.9 0.7 %copy-start.4 = (f32[6]{0:T(128)S(1)}, f32[6]{0:T(128)}, u32[]{:S(2)}) copy-start(f32[6]{0:T(128)} %eps_t.1) | copy-start | bytes 76
  15.6 0.7 %copy-start.5 = (f32[6]{0:T(128)S(1)}, f32[6]{0:T(128)}, u32[]{:S(2)}) copy-start(f32[6]{0:T(128)} %mob_t.1) | copy-start | bytes 76
  16.3 0.7 %copy-start.6 = (f32[6]{0:T(128)S(1)}, f32[6]{0:T(128)}, u32[]{:S(2)}) copy-start(f32[6]{0:T(128)} %cap_t.1) | copy-start | bytes 76
  19.2 5.5 %collective-permute-start.4 = (f32[3,4,8,128]{3,2,1,0:T(8,128)S(1)}, f32[3,4,8,128]{3,2,1,0:T(8,128)S(1)}, u32[]{:S(2)}, u32[]{:S(2)}) collective-permute-start(f32[3,4,8,128]{3,2,1,0:T(8,128)S(1)} %get-tuple-element.14), channel_id=1, source_target_pairs={{0,1},{1,0},{2,3},{3,2},{4,5},{5,4},{6,7},{7,6},{8,9},{9,8},{10,11... | collective-permute-start | bytes 147464 | tf_op jit(solution)/shard_map/ppermute | solution.py:516
  22.1 3.8 %collective-permute-start.5 = (f32[3,4,8,128]{3,2,1,0:T(8,128)S(1)}, f32[3,4,8,128]{3,2,1,0:T(8,128)S(1)}, u32[]{:S(2)}, u32[]{:S(2)}) collective-permute-start(f32[3,4,8,128]{3,2,1,0:T(8,128)S(1)} %get-tuple-element.14), channel_id=1, source_target_pairs={{0,2},{1,3},{2,0},{3,1},{4,6},{5,7},{6,4},{7,5},{8,10},{9,11},{10,... | collective-permute-start | bytes 147464 | tf_op jit(solution)/shard_map/ppermute | solution.py:516
  23.6 4.8 %collective-permute-start.6 = (f32[3,4,8,128]{3,2,1,0:T(8,128)S(1)}, f32[3,4,8,128]{3,2,1,0:T(8,128)S(1)}, u32[]{:S(2)}, u32[]{:S(2)}) collective-permute-start(f32[3,4,8,128]{3,2,1,0:T(8,128)S(1)} %get-tuple-element.14), channel_id=1, source_target_pairs={{0,3},{1,2},{2,1},{3,0},{4,7},{5,6},{6,5},{7,4},{8,11},{9,10},{10,... | collective-permute-start | bytes 147464 | tf_op jit(solution)/shard_map/ppermute | solution.py:516
  28.5 4.6 %collective-permute-start.7 = (f32[4,3,4,8,128]{4,3,2,1,0:T(8,128)S(1)}, f32[4,3,4,8,128]{4,3,2,1,0:T(8,128)S(1)}, u32[]{:S(2)}, u32[]{:S(2)}) collective-permute-start(f32[4,3,4,8,128]{4,3,2,1,0:T(8,128)S(1)} %pad_maximum_fusion), channel_id=1, source_target_pairs={{0,8},{1,9},{2,10},{3,11},{4,12},{5,13},{6,14},{7,15},{8,0},{9,1},... | collective-permute-start | bytes 589832 | tf_op jit(solution)/shard_map/ppermute | solution.py:516
  33.1 4.5 %collective-permute-start.8 = (f32[8,3,4,8,128]{4,3,2,1,0:T(8,128)S(1)}, f32[8,3,4,8,128]{4,3,2,1,0:T(8,128)S(1)}, u32[]{:S(2)}, u32[]{:S(2)}) collective-permute-start(f32[8,3,4,8,128]{4,3,2,1,0:T(8,128)S(1)} %constant_dynamic-update-slice_fusion.near), channel_id=1, source_target_pairs={{0,4},{1,5},{2,6},{3,7},{4,0},{5,1},{6,2},{7,3},{8,12},{9,13},{10,... | collective-permute-start | bytes 1179656 | tf_op jit(solution)/shard_map/ppermute | solution.py:516

commit v3 on v2

--- a/solution.py
+++ b/solution.py
@@ -1,4 +1,5 @@
 import functools
+import itertools
 import jax
 import jax.numpy as jnp
 from jax import lax
@@ -11,7 +12,6 @@
 RIM = 4
 LANES = 128
 VMEM = pl.BlockSpec(memory_space=pltpu.VMEM)
-SMEM = pl.BlockSpec(memory_space=pltpu.SMEM)
 
 
 UNROLL = 16
@@ -49,29 +49,67 @@
     return pltpu.roll(v, step, dim)
 
 
-def rim_y_kernel(cls, pot, fp, fn, out_a, out_b):
+def halve_lanes(a, b):
+    lane = iota(a.shape, 1)
+    at = (2 * lane) % LANES
+    a = jnp.take_along_axis(a + up(a, 1, 1), at, axis=1)
+    b = jnp.take_along_axis(b + up(b, 1, 1), at, axis=1)
+    return jnp.where(lane < LANES // 2, a, b)
+
+
+def look_up(table, c, shape):
+    found = [jnp.zeros(shape, jnp.float32)] * 3
+    for k in range(table.shape[1]):
+        same = c == float(k)
+        found = [
+            jnp.where(same, jnp.broadcast_to(table[f, k : k + 1], shape), found[f]) for f in range(3)
+        ]
+    return found
+
+
+def rim_y_kernel(cls, raw, out_a, out_b):
     even = lax.axis_index("gy") % 2 == 0
-    length = cls.shape[1]
-    for pair, (first, second) in enumerate(((cls, pot), (fp, fn))):
+    planes, length = cls.shape[0], cls.shape[1]
+    for pair in range(2):
+        first = cls if pair == 0 else raw.at[1]
         lo, hi = (
             jnp.concatenate(
-                [r[:, at : at + RIM, :].astype(jnp.float32) for r in (first, second)], axis=1
+                [r[:, at : at + RIM, :].astype(jnp.float32) for r in (first, raw.at[2 * pair])], axis=1
             )
             for at in (0, length - RIM)
         )
-        out_a[pair] = jnp.where(even, hi, lo)
-        out_b[pair] = jnp.where(even, lo, hi)
-
-
-def rim_x_kernel(cls, pot, fp, fn, in_a, in_b, out, out_a, out_b):
+        out_a[pair * planes : (pair + 1) * planes] = jnp.where(even, hi, lo)
+        out_b[pair * planes : (pair + 1) * planes] = jnp.where(even, lo, hi)
+
+
+def fields_kernel(table, cls, raw, block, work):
+    planes, length = cls.shape[0], cls.shape[1]
+    bx = planes // 2
+    for i in range(bx):
+        one, two = (
+            look_up(table, cls[2 * i + k].astype(jnp.float32), (length, LANES)) for k in (0, 1)
+        )
+        values = [p + q for p, q in zip(one, two)] + [raw[0, 2 * i] + raw[0, 2 * i + 1]]
+        for k, v in enumerate(values):
+            work[k, i] = v
+    for i in range(bx):
+        eps, mob, cap, pot = (
+            work[k, i, pl.ds(0, length // 2, stride=2), :] + work[k, i, pl.ds(1, length // 2, stride=2), :]
+            for k in range(4)
+        )
+        for f, v in enumerate((halve_lanes(eps, mob), halve_lanes(cap, pot))):
+            block[0, f, i] = 0.125 * v
+
+
+def rim_x_kernel(cls, raw, in_a, in_b, out, out_a, out_b):
     y, ny = lax.axis_index("gy"), lax.axis_size("gy")
     even_x, even_y = lax.axis_index("gx") % 2 == 0, y % 2 == 0
     planes, length = cls.shape[0], cls.shape[1]
     row = iota((planes, 2 * RIM, LANES), 1)
-    for pair, refs in enumerate(((cls, pot), (fp, fn))):
-        a, b = in_a[pair], in_b[pair]
+    for pair in range(2):
+        a, b = (r[pair * planes : (pair + 1) * planes] for r in (in_a, in_b))
         hi, lo = jnp.where(even_y, a, b), jnp.where(even_y, b, a)
-        for slot, ref in enumerate(refs):
+        for slot in range(2):
             field = 2 * pair + slot
             outside = -1.0 if field == 0 else 0.0
             h, l = jnp.where(y == ny - 1, outside, hi), jnp.where(y == 0, outside, lo)
@@ -79,7 +117,8 @@
                 l = down(l, RIM, 1)
             else:
                 h = down(h, RIM, 1)
-            out[field, :, 0:length, :] = ref[...].astype(jnp.float32)
+            own = cls[...].astype(jnp.float32) if field == 0 else raw[field - 1]
+            out[field, :, 0:length, :] = own
             out[field, :, length : length + 2 * RIM, :] = jnp.where(row < RIM, h, l)
         for slot in range(2):
             field = 2 * pair + slot
@@ -103,15 +142,7 @@
     return s + (kept[zp, i] * up(v, 1, 1) + down(kept[zm, i] * v, 1, 1))
 
 
-def halve_lanes(a, b):
-    lane = iota(a.shape, 1)
-    at = (2 * lane) % LANES
-    a = jnp.take_along_axis(a + up(a, 1, 1), at, axis=1)
-    b = jnp.take_along_axis(b + up(b, 1, 1), at, axis=1)
-    return jnp.where(lane < LANES // 2, a, b)
-
-
-def first_kernel(eps_t, mob_t, cap_t, mid, in_a, in_b, kept, block, fld, work):
+def first_kernel(table, mid, in_a, in_b, kept, block, fld, work):
     x, nx = lax.axis_index("gx"), lax.axis_size("gx")
     even = x % 2 == 0
     planes = mid.shape[1]
@@ -119,15 +150,9 @@
     own = rows - 2 * RIM
     total = planes + 2 * RIM
     EPS, MOB, POT, CAP, F_P, F_N, D_P, D_N = range(8)
-    classes = eps_t.shape[0]
 
     def materials(i, c, pot, fp, fn):
-        eps, mob, cap = jnp.zeros_like(c), jnp.zeros_like(c), jnp.zeros_like(c)
-        for k in range(classes):
-            same = c == float(k)
-            eps = jnp.where(same, eps_t[k], eps)
-            mob = jnp.where(same, mob_t[k], mob)
-            cap = jnp.where(same, cap_t[k], cap)
+        eps, mob, cap = look_up(table, c, (rows, LANES))
         fld[EPS, i], fld[MOB, i], fld[POT, i], fld[CAP, i] = eps, mob, pot, cap
         fld[F_P, i], fld[F_N, i] = fp, fn
 
@@ -213,15 +238,12 @@
         at = RIM + 2 * i
         r_p = residual(at, True, F_P, D_P, U_P) + residual(at + 1, True, F_P, D_P, U_P)
         r_n = residual(at, False, F_N, D_N, U_N) + residual(at + 1, False, F_N, D_N, U_N)
-        values = [r_p, r_n] + [fld[f, at] + fld[f, at + 1] for f in (EPS, MOB, CAP, POT)]
-        for k, v in enumerate(values):
-            work[k] = v[0:own]
-        even_odd = [
-            work[k, pl.ds(0, own // 2, stride=2), :] + work[k, pl.ds(1, own // 2, stride=2), :]
-            for k in range(6)
-        ]
-        for k in range(3):
-            block[(2, 0, 1)[k], i] = 0.125 * halve_lanes(even_odd[2 * k], even_odd[2 * k + 1])
+        work[0, i], work[1, i] = r_p[0:own], r_n[0:own]
+        r_p, r_n = (
+            work[k, i, pl.ds(0, own // 2, stride=2), :] + work[k, i, pl.ds(1, own // 2, stride=2), :]
+            for k in range(2)
+        )
+        block[0, i] = 0.125 * halve_lanes(r_p, r_n)
         return 0
 
     loop(0, planes // 2, coarse, 0)
@@ -229,19 +251,32 @@
 
 def low_lane(shape, bit):
     return (iota(shape, 1) & bit) == 0
+
+
+OPERATOR = 8
 
 
 class Level:
     def __init__(self, level, refs):
         self.level, self.step, self.factor = level, 1 << (level - 1), 0.25**level
-        (self.eps, self.pot, self.cap, self.f, self.xp, self.xm, self.yp, self.ym, self.zp, self.zm,
-         self.w, self.d, self.wf, self.u, self.v) = refs
-        self.nx, self.ny = self.eps.shape[0], self.eps.shape[1]
+        (self.xp, self.xm, self.yp, self.ym, self.zp, self.zm, self.w, self.d) = refs[:OPERATOR]
+        if len(refs) == OPERATOR + 3:
+            self.eps, self.pot, self.cap = refs[OPERATOR:]
+        else:
+            self.f, self.wf, self.u, self.v = refs[OPERATOR:]
+        self.nx, self.ny = self.w.shape[0], self.w.shape[1]
 
     @staticmethod
-    def scratch(nx, ny):
-        plain, face, padded = (pltpu.VMEM((n, ny, LANES), jnp.float32) for n in (nx, nx + 1, nx + 2))
-        return [plain] * 4 + [face] * 2 + [plain] * 7 + [padded] * 2
+    def operator(nx, ny):
+        return [(nx + 1, ny, LANES)] * 2 + [(nx, ny, LANES)] * 6
+
+    @staticmethod
+    def fields(nx, ny):
+        return [(nx, ny, LANES)] * 3
+
+    @staticmethod
+    def iterates(nx, ny):
+        return [(nx, ny, LANES)] * 2 + [(nx + 2, ny, LANES)] * 2
 
     def assemble(self):
         nx, ny, step = self.nx, self.ny, self.step
@@ -258,8 +293,6 @@
         half = 0.5 * self.factor
         for ref in (self.xp, self.xm):
             ref[0], ref[nx] = zero, zero
-        for ref in (self.u, self.v):
-            ref[0], ref[nx + 1] = zero, zero
 
         def x_face(i, _):
             k = half * (self.eps[i - 1] + self.eps[i])
@@ -297,6 +330,10 @@
         return s + (self.zp[i] * up(v, self.step, 1) + down(self.zm[i] * v, self.step, 1))
 
     def start(self):
+        zero = jnp.zeros((self.ny, LANES), jnp.float32)
+        for ref in (self.u, self.v):
+            ref[0], ref[self.nx + 1] = zero, zero
+
         def body(i, _):
             wf = self.w[i] * self.f[i]
             self.wf[i] = wf
@@ -380,42 +417,60 @@
         lv.u[i + 1] = u[i]
 
 
-def second_kernel(bits, near, far, kept, out_p, out_n, *scratch):
-    x, y = lax.axis_index("gx"), lax.axis_index("gy")
-    ny = lax.axis_size("gy")
-    l1, l2, l3 = (Level(k + 1, scratch[15 * k : 15 * k + 15]) for k in range(3))
-    sol, tmp, fine_a, fine_b = scratch[45:]
-    bx, by = near.shape[2], near.shape[3]
-    half = near.shape[0]
-    lane = iota((by, LANES), 1)
-    right = lane >= LANES // 2
-
-    def place(ref, flip):
-        def body(m, _):
-            b = m // ny
-            to_x = x ^ flip
-            for k, bit in enumerate(bits[:-1]):
-                to_x = to_x ^ (((b >> k) & 1) * bit)
-            to_y = y ^ (m % ny)
-            row = pl.ds(pl.multiple_of(to_y * by, by), by)
-            for i in range(bx):
-                at = to_x * bx + i
-                q = ref[m, 1, i]
-                l1.eps[at, row, :] = ref[m, 0, i]
-                l1.pot[at, row, :] = jnp.where(right, q, 0.0)
-                l1.cap[at, row, :] = jnp.where(right, down(q, LANES // 2, 1), 0.0)
-                l1.f[at, row, :] = ref[m, 2, i]
-            return 0
-
-        loop(0, half, body, 0)
-
-    place(near, 0)
-    place(far, bits[-1])
+def place(bits, ref, flip, x, y, ny, put):
+    bx, by = ref.shape[-3], ref.shape[-2]
+
+    def body(m, _):
+        b = m // ny
+        to_x = x ^ flip
+        for k, bit in enumerate(bits[:-1]):
+            to_x = to_x ^ (((b >> k) & 1) * bit)
+        row = pl.ds(pl.multiple_of((y ^ (m % ny)) * by, by), by)
+        for i in range(bx):
+            put(m, i, to_x * bx + i, row)
+        return 0
+
+    loop(0, ref.shape[0], body, 0)
+
+
+def operators_kernel(bits, near, far, *refs):
+    x, y, ny = lax.axis_index("gx"), lax.axis_index("gy"), lax.axis_size("gy")
+    outs, scratch = refs[: 3 * OPERATOR], refs[3 * OPERATOR :]
+    l1, l2, l3 = (
+        Level(k + 1, outs[OPERATOR * k : OPERATOR * (k + 1)] + scratch[3 * k : 3 * k + 3]) for k in range(3)
+    )
+    tmp = scratch[9]
+    right = iota((near.shape[-2], LANES), 1) >= LANES // 2
+    for ref, flip in ((near, 0), (far, bits[-1])):
+
+        def put(m, i, at, row, ref=ref):
+            q = ref[m, 1, i]
+            l1.eps[at, row, :] = ref[m, 0, i]
+            l1.pot[at, row, :] = jnp.where(right, q, 0.0)
+            l1.cap[at, row, :] = jnp.where(right, down(q, LANES // 2, 1), 0.0)
+
+        place(bits, ref, flip, x, y, ny, put)
     l1.assemble()
     l1.descend_fields(l2, tmp)
     l2.assemble()
     l2.descend_fields(l3, tmp)
     l3.assemble()
+
+
+def second_kernel(bits, near, far, kept, *refs):
+    x, y, ny = lax.axis_index("gx"), lax.axis_index("gy"), lax.axis_size("gy")
+    given, (out_p, out_n), scratch = refs[: 3 * OPERATOR], refs[3 * OPERATOR : 3 * OPERATOR + 2], refs[3 * OPERATOR + 2 :]
+    l1, l2, l3 = (
+        Level(k + 1, given[OPERATOR * k : OPERATOR * (k + 1)] + scratch[4 * k : 4 * k + 4]) for k in range(3)
+    )
+    sol, tmp, fine_a, fine_b = scratch[12:]
+    bx, by = near.shape[-3], near.shape[-2]
+    for ref, flip in ((near, 0), (far, bits[-1])):
+
+        def put(m, i, at, row, ref=ref):
+            l1.f[at, row, :] = ref[m, i]
+
+        place(bits, ref, flip, x, y, ny, put)
     for here, there in ((l1, l2), (l2, l3)):
         here.start()
         here.sweep(here.u, here.v)
@@ -491,100 +546,130 @@
     loop(0, 2 * bx, post_two, 0)
 
 
-def moves(nx, ny):
+def moves(ng, nx, ny):
     def of(partner):
-        return [(a * ny + b, (lambda t: t[0] * ny + t[1])(partner(a, b))) for a in range(nx) for b in range(ny)]
-
-    def other(k, n):
+        place = {p: k for k, p in enumerate(itertools.product(range(ng), range(nx), range(ny)))}
+        return [(k, place[partner(*p)]) for p, k in place.items()]
+
+    def other(k):
         return k + 1 if k % 2 else k - 1
 
     return {
-        "xa": of(lambda a, b: (a ^ 1, b)),
-        "xb": of(lambda a, b: (other(a, nx), b) if 0 < a < nx - 1 else (a, b ^ 1)),
-        "ya": of(lambda a, b: (a, b ^ 1)),
-        "yb": of(lambda a, b: (a, other(b, ny)) if 0 < b < ny - 1 else (a ^ 1, b)),
-        **{("x", k): of(lambda a, b, k=k: (a ^ k, b)) for k in range(1, nx)},
-        **{("y", k): of(lambda a, b, k=k: (a, b ^ k)) for k in range(1, ny)},
+        "xa": of(lambda g, a, b: (g, a ^ 1, b)),
+        "xb": of(lambda g, a, b: (g, other(a), b) if 0 < a < nx - 1 else (g ^ 1, a, b)),
+        "ya": of(lambda g, a, b: (g, a, b ^ 1)),
+        "yb": of(lambda g, a, b: (g, a, other(b)) if 0 < b < ny - 1 else (g, a ^ 1, b)),
+        **{("x", 1 << k): of(lambda g, a, b, k=k: (g, a ^ (1 << k), b)) for k in range((nx - 1).bit_length())},
+        **{("y", 1 << k): of(lambda g, a, b, k=k: (g, a, b ^ (1 << k))) for k in range((ny - 1).bit_length())},
     }
 
 
-def per_device(nx, ny, layer_class, permittivity, mobility, capture, potential, rhs_psi, rhs_n):
-    send = moves(nx, ny)
+def per_device(ng, nx, ny, layer_class, permittivity, mobility, capture, potential, rhs_psi, rhs_n):
+    send = moves(ng, nx, ny)
     f32 = jnp.float32
 
     def permute(v, name):
-        return lax.ppermute(v, ("gx", "gy"), send[name])
+        return lax.ppermute(v, ("groups", "gx", "gy"), send[name])
 
     planes, own = layer_class.shape[0], layer_class.shape[1]
     rows, total = own + 2 * RIM, planes + 2 * RIM
     bx, by = planes // 2, own // 2
-    raw = (layer_class, potential, rhs_psi, rhs_n)
-
     def shape(*dims):
         return jax.ShapeDtypeStruct(dims, f32)
 
+    raw = jnp.stack([potential, rhs_psi, rhs_n])
     a, b = pl.pallas_call(
         rim_y_kernel,
-        out_shape=[shape(2, planes, 2 * RIM, LANES)] * 2,
-        in_specs=[VMEM] * 4,
+        out_shape=[shape(2 * planes, by, LANES)] * 2,
+        in_specs=[VMEM] * 2,
         out_specs=[VMEM] * 2,
         compiler_params=params(16),
-    )(*raw)
+    )(layer_class, raw)
+    cut = a
     b = permute(b, "yb")
     a = permute(a, "ya")
+    later, _ = lax.optimization_barrier(((raw, permittivity, mobility, capture), cut))
+    table = jnp.stack(later[1:])
+    table = jnp.broadcast_to(table[:, :, None], (*table.shape, LANES))
+    fields = pl.pallas_call(
+        fields_kernel,
+        out_shape=shape(1, 2, bx, by, LANES),
+        in_specs=[VMEM] * 3,
+        out_specs=VMEM,
+        scratch_shapes=[pltpu.VMEM((4, bx, own, LANES), f32)],
+        compiler_params=params(16),
+    )(table, layer_class, later[0])
+    fields_y = [fields, permute(fields, ("y", 1))]
     mid, a, b = pl.pallas_call(
         rim_x_kernel,
         out_shape=[shape(4, planes, rows, LANES)] + [shape(4, RIM, rows, LANES)] * 2,
-        in_specs=[VMEM] * 6,
+        in_specs=[VMEM] * 4,
         out_specs=[VMEM] * 3,
         compiler_params=params(16),
-    )(*raw, a, b)
+    )(layer_class, raw, a, b)
+    fields_y, _ = lax.optimization_barrier((jnp.concatenate(fields_y), mid))
     b = permute(b, "xb")
     a = permute(a, "xa")
     kept, block = pl.pallas_call(
         first_kernel,
-        out_shape=[shape(KEPT, total, rows, LANES), shape(3, bx, by, LANES)],
-        in_specs=[SMEM] * 3 + [VMEM] * 3,
+        out_shape=[shape(KEPT, total, rows, LANES), shape(1, bx, by, LANES)],
+        in_specs=[VMEM] * 4,
         out_specs=[VMEM] * 2,
         scratch_shapes=[
             pltpu.VMEM((8, total, rows, LANES), f32),
-            pltpu.VMEM((6, own, LANES), f32),
+            pltpu.VMEM((2, bx, own, LANES), f32),
         ],
         compiler_params=params(24),
-    )(permittivity, mobility, capture, mid, a, b)
-
-    near = jnp.stack([block] + [permute(block, ("y", k)) for k in range(1, ny)])
-    bits = []
-    bit = nx // 2
-    while bit:
-        bits.append(bit)
-        far = permute(near, ("x", bit))
-        if bit > 1:
-            near = jnp.concatenate([near, far], axis=0)
-        bit //= 2
-    gx1, gy1 = bx * nx, by * ny
-    scratch = []
-    for level in range(3):
-        scratch += Level.scratch(gx1 >> level, gy1 >> level)
-    scratch += [
-        pltpu.VMEM((gx1 + 2, gy1 + 2 * by, LANES), f32),
-        pltpu.VMEM((max(gy1, rows), LANES), f32),
-        pltpu.VMEM((2, total, rows, LANES), f32),
-        pltpu.VMEM((2, total, rows, LANES), f32),
-    ]
+    )(table, mid, a, b)
+
+    bits = [1 << k for k in reversed(range((nx - 1).bit_length()))]
+
+    def over_y(near, first):
+        bit = first
+        while bit < ny:
+            near = jnp.concatenate([near, permute(near, ("y", bit))])
+            bit *= 2
+        return near
+
+    def over_x(near):
+        for bit in bits[:-1]:
+            near = jnp.concatenate([near, permute(near, ("x", bit))], axis=0)
+        return near, permute(near, ("x", bits[-1]))
+
+    fields_y = over_y(fields_y, 2)
+    pair = jnp.concatenate([block, permute(block, ("y", 1))])
+    fields_y, _ = lax.optimization_barrier((fields_y, pair))
+    grids = [(bx * nx >> level, by * ny >> level) for level in range(3)]
+    large = grids[0][0] * grids[0][1] > 1024
+    operators = pl.pallas_call(
+        functools.partial(operators_kernel, tuple(bits)),
+        out_shape=[shape(*s) for g in grids for s in Level.operator(*g)],
+        in_specs=[VMEM] * 2,
+        out_specs=[VMEM] * (3 * OPERATOR),
+        scratch_shapes=[pltpu.VMEM(s, f32) for g in grids for s in Level.fields(*g)]
+        + [pltpu.VMEM((grids[0][1], LANES), f32)],
+        compiler_params=params(60 if large else 16),
+    )(*over_x(fields_y))
+    near, far = over_x(over_y(pair, 2))
     return pl.pallas_call(
         functools.partial(second_kernel, tuple(bits)),
         out_shape=[shape(planes, own, LANES)] * 2,
-        in_specs=[VMEM] * 3,
+        in_specs=[VMEM] * (3 + 3 * OPERATOR),
         out_specs=[VMEM] * 2,
-        scratch_shapes=scratch,
-        compiler_params=params(60 if gx1 * gy1 > 1024 else 32),
-    )(near, far, kept)
+        scratch_shapes=[pltpu.VMEM(s, f32) for g in grids for s in Level.iterates(*g)]
+        + [
+            pltpu.VMEM((grids[0][0] + 2, grids[0][1] + 2 * by, LANES), f32),
+            pltpu.VMEM((max(grids[0][1], rows), LANES), f32),
+            pltpu.VMEM((2, total, rows, LANES), f32),
+            pltpu.VMEM((2, total, rows, LANES), f32),
+        ],
+        compiler_params=params(60 if large else 16),
+    )(near, far, kept, *operators)
 
 
 def solution(mesh):
     grid = P(("groups", "gx"), "gy", None)
-    fn = functools.partial(per_device, mesh.shape["gx"], mesh.shape["gy"])
+    fn = functools.partial(per_device, *(mesh.shape[a] for a in ("groups", "gx", "gy")))
     return jax.shard_map(
         fn,
         mesh=mesh,

time: 44.8 us -> 38.2 us (0.85); the launches traced: 44.1 us -> 38 us
  waiting for transfers between devices: 13.6 us -> 4.12 us
  starting transfers between devices: 15.5 us -> 22.5 us
  local copies, waits for them, and re-layouts: 5.35 us -> 0.94 us
  other arithmetic: 0.01 us -> 1.64 us
  Pallas kernels: 9 us -> 8.08 us
    ppermute x9 -> x12, waiting for transfers between devices: 13.6 us -> 4.12 us  [permute(): return lax.ppermute(v, ('groups', 'gx', 'gy'), send[name])]
    ppermute x9 -> x12, starting transfers between devices: 15.5 us -> 22.5 us  [permute(): return lax.ppermute(v, ('groups', 'gx', 'gy'), send[name])]
    unnamed x18 -> x5, local copies, waits for them, and re-layouts: 5.33 us -> 0.85 us
    pallas_call x1, Pallas kernels: 6.61 us -> 4.19 us  [per_device(): pl.pallas_call(functools.partial(second_kernel, tuple(bits)), out_shape=[...]
    pallas_call x1 -> x3, Pallas kernels: 0.02 us -> 2.17 us  [the longest x1 1.92 us: per_device(): pl.pallas_call(functools.partial(operators_kernel, tuple(bits)), out_shap...]
    another operation x1 -> x2, other arithmetic: 0.01 us -> 1.61 us  [the longest x1 0.92 us: per_device(): raw = jnp.stack([potential, rhs_psi, rhs_n])]
    pallas_call x1, Pallas kernels: 2.29 us -> 1.65 us  [per_device(): pl.pallas_call(first_kernel, out_shape=[shape(KEPT, total, rows, LANES),...]
  transfers between devices with their start and end apart: 9 -> 12, of which waited for: 7 -> 4; matrix products, arithmetic and copies ran while one was open for 0% -> 2% of each run, Pallas kernels for 0% -> 6%
where the time goes in v3:
time: 38.2 us; the launch traced here: 38 us
  starting transfers between devices  22.5 us (59%)
  Pallas kernels  8.08 us (21%)
  waiting for transfers between devices  4.12 us (11%)
  other arithmetic  1.64 us (4%)
  local copies, waits for them, and re-layouts  0.94 us (2%)
  between operations  0.73 us (2%)
    ppermute x12, starting transfers between devices, permute(): return lax.ppermute(v, ('groups', 'gx', 'gy'), send[name])  22.5 us
    pallas_call x1, Pallas kernels, per_device(): pl.pallas_call(functools.partial(second_kernel, tuple(bits)), out_shape=[...  4.19 us
    ppermute x12, waiting for transfers between devices, permute(): return lax.ppermute(v, ('groups', 'gx', 'gy'), send[name])  4.12 us
    pallas_call x1, Pallas kernels, per_device(): pl.pallas_call(functools.partial(operators_kernel, tuple(bits)), out_shap...  1.92 us
    pallas_call x1, Pallas kernels, per_device(): pl.pallas_call(first_kernel, out_shape=[shape(KEPT, total, rows, LANES),...  1.65 us
    another operation x1, other arithmetic, per_device(): raw = jnp.stack([potential, rhs_psi, rhs_n])  0.92 us
    unnamed x5, local copies, waits for them, and re-layouts  0.85 us
  transfers between devices with their start and end apart: 12, of which 4 were waited for; matrix products, arithmetic and copies ran while one was open for 2% of the time, Pallas kernels for 6%

profile of v3, /device:TPU:1, one launch (start us, length us, event | category | flops | bytes accessed | tf_op | source)
XLA Modules:
  0.0 38.0 jit_solution(6851593355535899659)
XLA Ops:
  0.6 0.9 %pad_maximum_fusion.raw = f32[3,8,16,128]{3,2,1,0:T(8,128)S(1)} fusion(f32[1,8,16,128]{3,2,1,0:T(8,128)} %bitcast.6, f32[1,8,16,128]{3,2,1,0:T(8,128)} %bitcast.7, f32[1,8,16,128]{3,2,1,0:T(8,128)} %bitcast.8), kind=kLoop, calls=%fused_computation | loop fusion | flops 98304 | bytes 393216 | tf_op jit(solution)/shard_map/stack | solution.py:580
  1.6 0.0 copy-start
  1.6 0.8 %copy-done = s32[8,16,128]{2,1,0:T(8,128)S(1)} copy-done((s32[8,16,128]{2,1,0:T(8,128)S(1)}, s32[8,16,128]{2,1,0:T(8,128)}, u32[]{:S(2)}) %copy-start) | copy-done | bytes 65560
  2.4 2.2 %collective-permute-start = (f32[16,8,128]{2,1,0:T(8,128)S(1)}, f32[16,8,128]{2,1,0:T(8,128)S(1)}, u32[]{:S(2)}, u32[]{:S(2)}) collective-permute-start(f32[16,8,128]{2,1,0:T(8,128)S(1)} %get-tuple-element.39), channel_id=1, source_target_pairs={{0,1},{1,0},{2,3},{3,2},{4,5},{5,4},{6,7},{7,6},{8,9},{9,8},{10,11... | collective-permute-start | bytes 196616 | tf_op jit(solution)/shard_map/ppermute | solution.py:572
  4.6 1.0 %collective-permute-start.1 = (f32[16,8,128]{2,1,0:T(8,128)S(1)}, f32[16,8,128]{2,1,0:T(8,128)S(1)}, u32[]{:S(2)}, u32[]{:S(2)}) collective-permute-start(f32[16,8,128]{2,1,0:T(8,128)S(1)} %get-tuple-element.43), channel_id=1, source_target_pairs={{0,4},{1,2},{2,1},{3,7},{4,0},{5,6},{6,5},{7,3},{8,12},{9,10},{10,... | collective-permute-start | bytes 196616 | tf_op jit(solution)/shard_map/ppermute | solution.py:572
  5.6 0.7 %pad_maximum_fusion.4 = f32[3,6]{1,0:T(4,128)S(1)} fusion(f32[1,6]{1,0:T(1,128)} %bitcast.9, f32[1,6]{1,0:T(1,128)} %bitcast.10, f32[1,6]{1,0:T(1,128)} %bitcast.11), kind=kLoop, calls=%fused_computation.12 | loop fusion | flops 36 | bytes 144 | tf_op jit(solution)/shard_map/stack | solution.py:592
  6.3 0.1 broadcast_in_dim.2.table
  6.3 0.2 shard_map.89
  6.6 1.7 %collective-permute-start.8 = (f32[1,2,4,8,128]{4,3,2,1,0:T(8,128)S(1)}, f32[1,2,4,8,128]{4,3,2,1,0:T(8,128)S(1)}, u32[]{:S(2)}, u32[]{:S(2)}) collective-permute-start(f32[1,2,4,8,128]{4,3,2,1,0:T(8,128)S(1)} %shard_map.89), channel_id=1, source_target_pairs={{0,1},{1,0},{2,3},{3,2},{4,5},{5,4},{6,7},{7,6},{8,9},{9,8},{10,11... | collective-permute-start | bytes 98312 | tf_op jit(solution)/shard_map/ppermute | solution.py:572
  8.3 0.0 collective-permute-done.in_a
  8.3 0.0 collective-permute-done.1.in_b
  8.3 0.1 shard_map.87
  8.4 1.6 %collective-permute-start.2 = (f32[4,4,24,128]{3,2,1,0:T(8,128)S(1)}, f32[4,4,24,128]{3,2,1,0:T(8,128)S(1)}, u32[]{:S(2)}, u32[]{:S(2)}) collective-permute-start(f32[4,4,24,128]{3,2,1,0:T(8,128)S(1)} %get-tuple-element.45), channel_id=1, source_target_pairs={{0,4},{1,5},{2,6},{3,7},{4,0},{5,1},{6,2},{7,3},{8,12},{9,13},{10,... | collective-permute-start | bytes 589832 | tf_op jit(solution)/shard_map/ppermute | solution.py:572
  9.9 1.2 %collective-permute-start.3 = (f32[4,4,24,128]{3,2,1,0:T(8,128)S(1)}, f32[4,4,24,128]{3,2,1,0:T(8,128)S(1)}, u32[]{:S(2)}, u32[]{:S(2)}) collective-permute-start(f32[4,4,24,128]{3,2,1,0:T(8,128)S(1)} %get-tuple-element.46), channel_id=1, source_target_pairs={{0,16},{1,17},{2,18},{3,19},{4,8},{5,9},{6,10},{7,11},{8,4},{9,5},... | collective-permute-start | bytes 589832 | tf_op jit(solution)/shard_map/ppermute | solution.py:572
  11.1 0.0 collective-permute-done.8
  11.1 2.4 %collective-permute-start.9 = (f32[2,2,4,8,128]{4,3,2,1,0:T(8,128)S(1)}, f32[2,2,4,8,128]{4,3,2,1,0:T(8,128)S(1)}, u32[]{:S(2)}, u32[]{:S(2)}) collective-permute-start(f32[2,2,4,8,128]{4,3,2,1,0:T(8,128)S(1)} %pad_maximum_fusion.3), channel_id=1, source_target_pairs={{0,2},{1,3},{2,0},{3,1},{4,6},{5,7},{6,4},{7,5},{8,10},{9,11},{10,... | collective-permute-start | bytes 196616 | tf_op jit(solution)/shard_map/ppermute | solution.py:572
  13.5 1.7 %collective-permute-done.9 = f32[2,2,4,8,128]{4,3,2,1,0:T(8,128)S(1)} collective-permute-done((f32[2,2,4,8,128]{4,3,2,1,0:T(8,128)S(1)}, f32[2,2,4,8,128]{4,3,2,1,0:T(8,128)S(1)}, u32[]{:S(2)}, u32[]{:S(2)}) %collective-permute-start.9) | collective-permute-done | bytes 65568 | tf_op jit(solution)/shard_map/ppermute | solution.py:572
  15.2 0.0 collective-permute-done.2.in_a
  15.2 0.1 collective-permute-done.3.in_b
  15.3 1.6 %shard_map.88 = (f32[15,16,24,128]{3,2,1,0:T(8,128)S(1)}, f32[1,4,8,128]{3,2,1,0:T(8,128)S(1)}) custom-call(f32[3,6,128]{2,1,0:T(8,128)S(1)} %broadcast_in_dim.2.table, f32[4,8,24,128]{3,2,1,0:T(8,128)S(1)} %get-tuple-element.44.mid, f32[4,4,24,128]{3,2,1,0:T(8,128)S(1)} %collective-permute-done.2.in_a, f32[4,4,24,128]{3,2,1,0:T(8,128)S(1)} %collective-permute-done.3.in_b), custom_call_target="tpu_custom_call" | custom-call | tf_op jit(solution)/shard_map/pallas_call | solution.py:613
  16.9 1.0 %collective-permute-start.4 = (f32[1,4,8,128]{3,2,1,0:T(8,128)S(1)}, f32[1,4,8,128]{3,2,1,0:T(8,128)S(1)}, u32[]{:S(2)}, u32[]{:S(2)}) collective-permute-start(f32[1,4,8,128]{3,2,1,0:T(8,128)S(1)} %get-tuple-element.47), channel_id=1, source_target_pairs={{0,1},{1,0},{2,3},{3,2},{4,5},{5,4},{6,7},{7,6},{8,9},{9,8},{10,11... | collective-permute-start | bytes 49160 | tf_op jit(solution)/shard_map/ppermute | solution.py:572
  17.9 1.6 %collective-permute-done.4 = f32[1,4,8,128]{3,2,1,0:T(8,128)S(1)} collective-permute-done((f32[1,4,8,128]{3,2,1,0:T(8,128)S(1)}, f32[1,4,8,128]{3,2,1,0:T(8,128)S(1)}, u32[]{:S(2)}, u32[]{:S(2)}) %collective-permute-start.4) | collective-permute-done | bytes 16416 | tf_op jit(solution)/shard_map/ppermute | solution.py:572
  19.6 2.4 %collective-permute-start.5 = (f32[2,4,8,128]{3,2,1,0:T(8,128)S(1)}, f32[2,4,8,128]{3,2,1,0:T(8,128)S(1)}, u32[]{:S(2)}, u32[]{:S(2)}) collective-permute-start(f32[2,4,8,128]{3,2,1,0:T(8,128)S(1)} %get-tuple-element.76), channel_id=1, source_target_pairs={{0,2},{1,3},{2,0},{3,1},{4,6},{5,7},{6,4},{7,5},{8,10},{9,11},{10,... | collective-permute-start | bytes 98312 | tf_op jit(solution)/shard_map/ppermute | solution.py:572
  22.0 1.9 %collective-permute-start.10 = (f32[4,2,4,8,128]{4,3,2,1,0:T(8,128)S(1)}, f32[4,2,4,8,128]{4,3,2,1,0:T(8,128)S(1)}, u32[]{:S(2)}, u32[]{:S(2)}) collective-permute-start(f32[4,2,4,8,128]{4,3,2,1,0:T(8,128)S(1)} %pad_maximum_fusion.1), channel_id=1, source_target_pairs={{0,8},{1,9},{2,10},{3,11},{4,12},{5,13},{6,14},{7,15},{8,0},{9,1},... | collective-permute-start | bytes 393224 | tf_op jit(solution)/shard_map/ppermute | solution.py:572
  24.0 1.6 %collective-permute-start.6 = (f32[4,4,8,128]{3,2,1,0:T(8,128)S(1)}, f32[4,4,8,128]{3,2,1,0:T(8,128)S(1)}, u32[]{:S(2)}, u32[]{:S(2)}) collective-permute-start(f32[4,4,8,128]{3,2,1,0:T(8,128)S(1)} %pad_maximum_fusion.2), channel_id=1, source_target_pairs={{0,8},{1,9},{2,10},{3,11},{4,12},{5,13},{6,14},{7,15},{8,0},{9,1},... | collective-permute-start | bytes 196616 | tf_op jit(solution)/shard_map/ppermute | solution.py:572
  25.5 0.7 %collective-permute-done.10 = f32[4,2,4,8,128]{4,3,2,1,0:T(8,128)S(1)} collective-permute-done((f32[4,2,4,8,128]{4,3,2,1,0:T(8,128)S(1)}, f32[4,2,4,8,128]{4,3,2,1,0:T(8,128)S(1)}, u32[]{:S(2)}, u32[]{:S(2)}) %collective-permute-start.10) | collective-permute-done | bytes 131104 | tf_op jit(solution)/shard_map/ppermute | solution.py:572
  26.3 3.7 %collective-permute-start.11 = (f32[8,2,4,8,128]{4,3,2,1,0:T(8,128)S(1)}, f32[8,2,4,8,128]{4,3,2,1,0:T(8,128)S(1)}, u32[]{:S(2)}, u32[]{:S(2)}) collective-permute-start(f32[8,2,4,8,128]{4,3,2,1,0:T(8,128)S(1)} %constant_dynamic-update-slice_fusion.6.near), channel_id=1, source_target_pairs={{0,4},{1,5},{2,6},{3,7},{4,0},{5,1},{6,2},{7,3},{8,12},{9,13},{10,... | collective-permute-start | bytes 786440 | tf_op jit(solution)/shard_map/ppermute | solution.py:572
  30.0 1.8 %collective-permute-start.7 = (f32[8,4,8,128]{3,2,1,0:T(8,128)S(1)}, f32[8,4,8,128]{3,2,1,0:T(8,128)S(1)}, u32[]{:S(2)}, u32[]{:S(2)}) collective-permute-start(f32[8,4,8,128]{3,2,1,0:T(8,128)S(1)} %constant_dynamic-update-slice_fusion.2.near), channel_id=1, source_target_pairs={{0,4},{1,5},{2,6},{3,7},{4,0},{5,1},{6,2},{7,3},{8,12},{9,13},{10,... | collective-permute-start | bytes 393224 | tf_op jit(solution)/shard_map/ppermute | solution.py:572
  31.9 0.0 collective-permute-done.11.far
  31.9 1.9 %shard_map.90 = (f32[17,32,128]{2,1,0:T(8,128)S(1)}, f32[17,32,128]{2,1,0:T(8,128)S(1)}, f32[16,32,128]{2,1,0:T(8,128)S(1)}, f32[16,32,128]{2,1,0:T(8,128)S(1)},...) custom-call(f32[8,2,4,8,128]{4,3,2,1,0:T(8,128)S(1)} %constant_dynam, ...), custom_call_target="tpu_custom_call" | custom-call | tf_op jit(solution)/shard_map/pallas_call | solution.py:644
  33.8 0.0 collective-permute-done.7.far
  33.8 4.2 %shard_map.91 = (f32[8,16,128]{2,1,0:T(8,128)}, f32[8,16,128]{2,1,0:T(8,128)}) custom-call(f32[8,4,8,128]{3,2,1,0:T(8,128)S(1)} %constant_dynamic-update-slice_fusion.2.near, f32[8,4,8,128]{3,2,1,0:T(8,128)S(1)} %collective-permute-done.7.far, f32[15,16,24,128]{3,2,1,0:T(8,128)S(1)} %get-tuple-element.48.kept, f32[17,32,128]{2,1,0:T(8,128)S(1)} %get-tuple-element.52.refs_0_, ...), custom_call_target="tpu_custom_call" | custom-call | tf_op jit(solution)/shard_map/pallas_call | solution.py:654
  (12 shorter events, 0.1 us)
Async XLA Ops:
  1.6 0.8 %copy-start = (s32[8,16,128]{2,1,0:T(8,128)S(1)}, s32[8,16,128]{2,1,0:T(8,128)}, u32[]{:S(2)}) copy-start(s32[8,16,128]{2,1,0:T(8,128)} %cls.5) | copy-start | bytes 196612
  2.4 5.9 %collective-permute-start = (f32[16,8,128]{2,1,0:T(8,128)S(1)}, f32[16,8,128]{2,1,0:T(8,128)S(1)}, u32[]{:S(2)}, u32[]{:S(2)}) collective-permute-start(f32[16,8,128]{2,1,0:T(8,128)S(1)} %get-tuple-element.39), channel_id=1, source_target_pairs={{0,1},{1,0},{2,3},{3,2},{4,5},{5,4},{6,7},{7,6},{8,9},{9,8},{10,11... | collective-permute-start | bytes 196616 | tf_op jit(solution)/shard_map/ppermute | solution.py:572
  4.6 3.7 %collective-permute-start.1 = (f32[16,8,128]{2,1,0:T(8,128)S(1)}, f32[16,8,128]{2,1,0:T(8,128)S(1)}, u32[]{:S(2)}, u32[]{:S(2)}) collective-permute-start(f32[16,8,128]{2,1,0:T(8,128)S(1)} %get-tuple-element.43), channel_id=1, source_target_pairs={{0,4},{1,2},{2,1},{3,7},{4,0},{5,6},{6,5},{7,3},{8,12},{9,10},{10,... | collective-permute-start | bytes 196616 | tf_op jit(solution)/shard_map/ppermute | solution.py:572
  6.6 4.5 %collective-permute-start.8 = (f32[1,2,4,8,128]{4,3,2,1,0:T(8,128)S(1)}, f32[1,2,4,8,128]{4,3,2,1,0:T(8,128)S(1)}, u32[]{:S(2)}, u32[]{:S(2)}) collective-permute-start(f32[1,2,4,8,128]{4,3,2,1,0:T(8,128)S(1)} %shard_map.89), channel_id=1, source_target_pairs={{0,1},{1,0},{2,3},{3,2},{4,5},{5,4},{6,7},{7,6},{8,9},{9,8},{10,11... | collective-permute-start | bytes 98312 | tf_op jit(solution)/shard_map/ppermute | solution.py:572
  8.4 6.9 %collective-permute-start.2 = (f32[4,4,24,128]{3,2,1,0:T(8,128)S(1)}, f32[4,4,24,128]{3,2,1,0:T(8,128)S(1)}, u32[]{:S(2)}, u32[]{:S(2)}) collective-permute-start(f32[4,4,24,128]{3,2,1,0:T(8,128)S(1)} %get-tuple-element.45), channel_id=1, source_target_pairs={{0,4},{1,5},{2,6},{3,7},{4,0},{5,1},{6,2},{7,3},{8,12},{9,13},{10,... | collective-permute-start | bytes 589832 | tf_op jit(solution)/shard_map/ppermute | solution.py:572
  9.9 5.4 %collective-permute-start.3 = (f32[4,4,24,128]{3,2,1,0:T(8,128)S(1)}, f32[4,4,24,128]{3,2,1,0:T(8,128)S(1)}, u32[]{:S(2)}, u32[]{:S(2)}) collective-permute-start(f32[4,4,24,128]{3,2,1,0:T(8,128)S(1)} %get-tuple-element.46), channel_id=1, source_target_pairs={{0,16},{1,17},{2,18},{3,19},{4,8},{5,9},{6,10},{7,11},{8,4},{9,5},... | collective-permute-start | bytes 589832 | tf_op jit(solution)/shard_map/ppermute | solution.py:572
  11.1 4.1 %collective-permute-start.9 = (f32[2,2,4,8,128]{4,3,2,1,0:T(8,128)S(1)}, f32[2,2,4,8,128]{4,3,2,1,0:T(8,128)S(1)}, u32[]{:S(2)}, u32[]{:S(2)}) collective-permute-start(f32[2,2,4,8,128]{4,3,2,1,0:T(8,128)S(1)} %pad_maximum_fusion.3), channel_id=1, source_target_pairs={{0,2},{1,3},{2,0},{3,1},{4,6},{5,7},{6,4},{7,5},{8,10},{9,11},{10,... | collective-permute-start | bytes 196616 | tf_op jit(solution)/shard_map/ppermute | solution.py:572
  16.9 2.6 %collective-permute-start.4 = (f32[1,4,8,128]{3,2,1,0:T(8,128)S(1)}, f32[1,4,8,128]{3,2,1,0:T(8,128)S(1)}, u32[]{:S(2)}, u32[]{:S(2)}) collective-permute-start(f32[1,4,8,128]{3,2,1,0:T(8,128)S(1)} %get-tuple-element.47), channel_id=1, source_target_pairs={{0,1},{1,0},{2,3},{3,2},{4,5},{5,4},{6,7},{7,6},{8,9},{9,8},{10,11... | collective-permute-start | bytes 49160 | tf_op jit(solution)/shard_map/ppermute | solution.py:572
  19.6 4.3 %collective-permute-start.5 = (f32[2,4,8,128]{3,2,1,0:T(8,128)S(1)}, f32[2,4,8,128]{3,2,1,0:T(8,128)S(1)}, u32[]{:S(2)}, u32[]{:S(2)}) collective-permute-start(f32[2,4,8,128]{3,2,1,0:T(8,128)S(1)} %get-tuple-element.76), channel_id=1, source_target_pairs={{0,2},{1,3},{2,0},{3,1},{4,6},{5,7},{6,4},{7,5},{8,10},{9,11},{10,... | collective-permute-start | bytes 98312 | tf_op jit(solution)/shard_map/ppermute | solution.py:572
  22.0 4.3 %collective-permute-start.10 = (f32[4,2,4,8,128]{4,3,2,1,0:T(8,128)S(1)}, f32[4,2,4,8,128]{4,3,2,1,0:T(8,128)S(1)}, u32[]{:S(2)}, u32[]{:S(2)}) collective-permute-start(f32[4,2,4,8,128]{4,3,2,1,0:T(8,128)S(1)} %pad_maximum_fusion.1), channel_id=1, source_target_pairs={{0,8},{1,9},{2,10},{3,11},{4,12},{5,13},{6,14},{7,15},{8,0},{9,1},... | collective-permute-start | bytes 393224 | tf_op jit(solution)/shard_map/ppermute | solution.py:572
  24.0 6.1 %collective-permute-start.6 = (f32[4,4,8,128]{3,2,1,0:T(8,128)S(1)}, f32[4,4,8,128]{3,2,1,0:T(8,128)S(1)}, u32[]{:S(2)}, u32[]{:S(2)}) collective-permute-start(f32[4,4,8,128]{3,2,1,0:T(8,128)S(1)} %pad_maximum_fusion.2), channel_id=1, source_target_pairs={{0,8},{1,9},{2,10},{3,11},{4,12},{5,13},{6,14},{7,15},{8,0},{9,1},... | collective-permute-start | bytes 196616 | tf_op jit(solution)/shard_map/ppermute | solution.py:572
  26.3 5.6 %collective-permute-start.11 = (f32[8,2,4,8,128]{4,3,2,1,0:T(8,128)S(1)}, f32[8,2,4,8,128]{4,3,2,1,0:T(8,128)S(1)}, u32[]{:S(2)}, u32[]{:S(2)}) collective-permute-start(f32[8,2,4,8,128]{4,3,2,1,0:T(8,128)S(1)} %constant_dynamic-update-slice_fusion.6.near), channel_id=1, source_target_pairs={{0,4},{1,5},{2,6},{3,7},{4,0},{5,1},{6,2},{7,3},{8,12},{9,13},{10,... | collective-permute-start | bytes 786440 | tf_op jit(solution)/shard_map/ppermute | solution.py:572
  30.0 3.8 %collective-permute-start.7 = (f32[8,4,8,128]{3,2,1,0:T(8,128)S(1)}, f32[8,4,8,128]{3,2,1,0:T(8,128)S(1)}, u32[]{:S(2)}, u32[]{:S(2)}) collective-permute-start(f32[8,4,8,128]{3,2,1,0:T(8,128)S(1)} %constant_dynamic-update-slice_fusion.2.near), channel_id=1, source_target_pairs={{0,4},{1,5},{2,6},{3,7},{4,0},{5,1},{6,2},{7,3},{8,12},{9,13},{10,... | collective-permute-start | bytes 393224 | tf_op jit(solution)/shard_map/ppermute | solution.py:572

commit v4 on v3

--- a/solution.py
+++ b/solution.py
@@ -12,6 +12,7 @@
 RIM = 4
 LANES = 128
 VMEM = pl.BlockSpec(memory_space=pltpu.VMEM)
+HBM = pl.BlockSpec(memory_space=pltpu.HBM)
 
 
 UNROLL = 16
@@ -26,7 +27,7 @@
 
 
 def params(mib):
-    return pltpu.CompilerParams(vmem_limit_bytes=mib * 1024 * 1024)
+    return pltpu.CompilerParams(vmem_limit_bytes=int(mib * 1024 * 1024))
 
 
 def bernoulli(x):
@@ -67,29 +68,36 @@
     return found
 
 
-def rim_y_kernel(cls, raw, out_a, out_b):
+def rim_y_kernel(c_in, p_in, fp_in, fn_in, out_a, out_b, c_out, p_out, fp_out, fn_out, cls, sems):
+    outs = (c_out, p_out, fp_out, fn_out)
+    copies = [
+        pltpu.make_async_copy(s, d, sems.at[k])
+        for k, (s, d) in enumerate(zip((c_in, p_in, fp_in, fn_in), (cls, *outs[1:])))
+    ]
+    for c in copies:
+        c.start()
+    for c in copies:
+        c.wait()
+    c_out[...] = cls[...].astype(jnp.float32)
     even = lax.axis_index("gy") % 2 == 0
     planes, length = cls.shape[0], cls.shape[1]
     for pair in range(2):
-        first = cls if pair == 0 else raw.at[1]
         lo, hi = (
-            jnp.concatenate(
-                [r[:, at : at + RIM, :].astype(jnp.float32) for r in (first, raw.at[2 * pair])], axis=1
-            )
+            jnp.concatenate([r[:, at : at + RIM, :] for r in outs[2 * pair : 2 * pair + 2]], axis=1)
             for at in (0, length - RIM)
         )
         out_a[pair * planes : (pair + 1) * planes] = jnp.where(even, hi, lo)
         out_b[pair * planes : (pair + 1) * planes] = jnp.where(even, lo, hi)
 
 
-def fields_kernel(table, cls, raw, block, work):
+def fields_kernel(table, cls, pot, block, work):
     planes, length = cls.shape[0], cls.shape[1]
     bx = planes // 2
     for i in range(bx):
         one, two = (
-            look_up(table, cls[2 * i + k].astype(jnp.float32), (length, LANES)) for k in (0, 1)
-        )
-        values = [p + q for p, q in zip(one, two)] + [raw[0, 2 * i] + raw[0, 2 * i + 1]]
+            look_up(table, cls[2 * i + k], (length, LANES)) for k in (0, 1)
+        )
+        values = [p + q for p, q in zip(one, two)] + [pot[2 * i] + pot[2 * i + 1]]
         for k, v in enumerate(values):
             work[k, i] = v
     for i in range(bx):
@@ -101,7 +109,7 @@
             block[0, f, i] = 0.125 * v
 
 
-def rim_x_kernel(cls, raw, in_a, in_b, out, out_a, out_b):
+def rim_x_kernel(cls, pot, fp, fn, in_a, in_b, out, out_a, out_b):
     y, ny = lax.axis_index("gy"), lax.axis_size("gy")
     even_x, even_y = lax.axis_index("gx") % 2 == 0, y % 2 == 0
     planes, length = cls.shape[0], cls.shape[1]
@@ -117,8 +125,7 @@
                 l = down(l, RIM, 1)
             else:
                 h = down(h, RIM, 1)
-            own = cls[...].astype(jnp.float32) if field == 0 else raw[field - 1]
-            out[field, :, 0:length, :] = own
+            out[field, :, 0:length, :] = (cls, pot, fp, fn)[field][...]
             out[field, :, length : length + 2 * RIM, :] = jnp.where(row < RIM, h, l)
         for slot in range(2):
             field = 2 * pair + slot
@@ -577,19 +584,20 @@
     def shape(*dims):
         return jax.ShapeDtypeStruct(dims, f32)
 
-    raw = jnp.stack([potential, rhs_psi, rhs_n])
-    a, b = pl.pallas_call(
+    cell = (planes, own, LANES)
+    a, b, *raw = pl.pallas_call(
         rim_y_kernel,
-        out_shape=[shape(2 * planes, by, LANES)] * 2,
-        in_specs=[VMEM] * 2,
-        out_specs=[VMEM] * 2,
-        compiler_params=params(16),
-    )(layer_class, raw)
+        out_shape=[shape(2 * planes, by, LANES)] * 2 + [shape(*cell)] * 4,
+        in_specs=[HBM] * 4,
+        out_specs=[VMEM] * 6,
+        scratch_shapes=[pltpu.VMEM(cell, jnp.int32), pltpu.SemaphoreType.DMA((4,))],
+        compiler_params=params(53.55),
+    )(layer_class, potential, rhs_psi, rhs_n)
     cut = a
     b = permute(b, "yb")
     a = permute(a, "ya")
-    later, _ = lax.optimization_barrier(((raw, permittivity, mobility, capture), cut))
-    table = jnp.stack(later[1:])
+    later, _ = lax.optimization_barrier(((permittivity, mobility, capture, raw[1]), cut))
+    table = jnp.stack(later[:3])
     table = jnp.broadcast_to(table[:, :, None], (*table.shape, LANES))
     fields = pl.pallas_call(
         fields_kernel,
@@ -598,15 +606,15 @@
         out_specs=VMEM,
         scratch_shapes=[pltpu.VMEM((4, bx, own, LANES), f32)],
         compiler_params=params(16),
-    )(table, layer_class, later[0])
+    )(table, raw[0], later[3])
     fields_y = [fields, permute(fields, ("y", 1))]
     mid, a, b = pl.pallas_call(
         rim_x_kernel,
         out_shape=[shape(4, planes, rows, LANES)] + [shape(4, RIM, rows, LANES)] * 2,
-        in_specs=[VMEM] * 4,
+        in_specs=[VMEM] * 6,
         out_specs=[VMEM] * 3,
         compiler_params=params(16),
-    )(layer_class, raw, a, b)
+    )(*raw, a, b)
     fields_y, _ = lax.optimization_barrier((jnp.concatenate(fields_y), mid))
     b = permute(b, "xb")
     a = permute(a, "xa")

time: 38.2 us -> 37.4 us (0.979)
  Pallas kernels: 8.08 us -> 9.05 us
  other arithmetic: 1.64 us -> 0.72 us
  local copies, waits for them, and re-layouts: 0.94 us -> 0.11 us
    pallas_call x1, Pallas kernels: 0.02 us -> 1 us  [per_device(): pl.pallas_call(rim_y_kernel, out_shape=[shape(2 * planes, by, LANES)] * 2...]
    another operation x2 -> x1, other arithmetic: 1.61 us -> 0.7 us  [per_device(): table = jnp.stack(later[:3])]
    unnamed x5 -> x3, local copies, waits for them, and re-layouts: 0.85 us -> 0.02 us
where the time goes in v4:
time: 37.4 us; the launch traced here: 37.2 us
  starting transfers between devices  22.5 us (60%)
  Pallas kernels  9.05 us (24%)
  waiting for transfers between devices  4.12 us (11%)
  other arithmetic  0.72 us (2%)
  between operations  0.72 us (2%)
    ppermute x12, starting transfers between devices, permute(): return lax.ppermute(v, ('groups', 'gx', 'gy'), send[name])  22.5 us
    pallas_call x1, Pallas kernels, per_device(): pl.pallas_call(functools.partial(second_kernel, tuple(bits)), out_shape=[...  4.19 us
    ppermute x12, waiting for transfers between devices, permute(): return lax.ppermute(v, ('groups', 'gx', 'gy'), send[name])  4.12 us
    pallas_call x1, Pallas kernels, per_device(): pl.pallas_call(functools.partial(operators_kernel, tuple(bits)), out_shap...  1.92 us
    pallas_call x1, Pallas kernels, per_device(): pl.pallas_call(first_kernel, out_shape=[shape(KEPT, total, rows, LANES),...  1.65 us
    pallas_call x1, Pallas kernels, per_device(): pl.pallas_call(rim_y_kernel, out_shape=[shape(2 * planes, by, LANES)] * 2...  1 us
  transfers between devices with their start and end apart: 12, of which 4 were waited for; matrix products, arithmetic and copies ran while one was open for 2% of the time, Pallas kernels for 6%

profile of v4, /device:TPU:1, one launch (start us, length us, event | category | flops | bytes accessed | tf_op | source)
XLA Modules:
  0.0 37.2 jit_solution(13154577813904925675)
XLA Ops:
  0.6 1.0 %shard_map.86 = (f32[16,8,128]{2,1,0:T(8,128)S(1)}, f32[16,8,128]{2,1,0:T(8,128)S(1)}, f32[8,16,128]{2,1,0:T(8,128)S(1)}, f32[8,16,128]{2,1,0:T(8,128)S(1)}, f32...) custom-call(s32[8,16,128]{2,1,0:T(8,128)} %c_in.1, f32[8,16,128]{2,1,0:T(8,128)} %p_in.1, f32[8,16,128]{2,1,0:T(8,128)} %fp_in.1, ...), custom_call_target="tpu_custom_call" | custom-call | tf_op jit(solution)/shard_map/pallas_call | solution.py:588
  1.6 2.2 %collective-permute-start = (f32[16,8,128]{2,1,0:T(8,128)S(1)}, f32[16,8,128]{2,1,0:T(8,128)S(1)}, u32[]{:S(2)}, u32[]{:S(2)}) collective-permute-start(f32[16,8,128]{2,1,0:T(8,128)S(1)} %get-tuple-element.44), channel_id=1, source_target_pairs={{0,1},{1,0},{2,3},{3,2},{4,5},{5,4},{6,7},{7,6},{8,9},{9,8},{10,11... | collective-permute-start | bytes 196616 | tf_op jit(solution)/shard_map/ppermute | solution.py:579
  3.8 1.0 %collective-permute-start.1 = (f32[16,8,128]{2,1,0:T(8,128)S(1)}, f32[16,8,128]{2,1,0:T(8,128)S(1)}, u32[]{:S(2)}, u32[]{:S(2)}) collective-permute-start(f32[16,8,128]{2,1,0:T(8,128)S(1)} %get-tuple-element.51), channel_id=1, source_target_pairs={{0,4},{1,2},{2,1},{3,7},{4,0},{5,6},{6,5},{7,3},{8,12},{9,10},{10,... | collective-permute-start | bytes 196616 | tf_op jit(solution)/shard_map/ppermute | solution.py:579
  4.8 0.7 %pad_maximum_fusion.3 = f32[3,6]{1,0:T(4,128)S(1)} fusion(f32[1,6]{1,0:T(1,128)} %bitcast.3, f32[1,6]{1,0:T(1,128)} %bitcast.4, f32[1,6]{1,0:T(1,128)} %bitcast.5), kind=kLoop, calls=%fused_computation.11 | loop fusion | flops 36 | bytes 144 | tf_op jit(solution)/shard_map/stack | solution.py:600
  5.5 0.1 broadcast_in_dim.2.table
  5.6 0.2 shard_map.89
  5.8 1.7 %collective-permute-start.8 = (f32[1,2,4,8,128]{4,3,2,1,0:T(8,128)S(1)}, f32[1,2,4,8,128]{4,3,2,1,0:T(8,128)S(1)}, u32[]{:S(2)}, u32[]{:S(2)}) collective-permute-start(f32[1,2,4,8,128]{4,3,2,1,0:T(8,128)S(1)} %shard_map.89), channel_id=1, source_target_pairs={{0,1},{1,0},{2,3},{3,2},{4,5},{5,4},{6,7},{7,6},{8,9},{9,8},{10,11... | collective-permute-start | bytes 98312 | tf_op jit(solution)/shard_map/ppermute | solution.py:579
  7.5 0.0 collective-permute-done.in_a
  7.5 0.0 collective-permute-done.1.in_b
  7.5 0.1 shard_map.87
  7.6 1.6 %collective-permute-start.2 = (f32[4,4,24,128]{3,2,1,0:T(8,128)S(1)}, f32[4,4,24,128]{3,2,1,0:T(8,128)S(1)}, u32[]{:S(2)}, u32[]{:S(2)}) collective-permute-start(f32[4,4,24,128]{3,2,1,0:T(8,128)S(1)} %get-tuple-element.53), channel_id=1, source_target_pairs={{0,4},{1,5},{2,6},{3,7},{4,0},{5,1},{6,2},{7,3},{8,12},{9,13},{10,... | collective-permute-start | bytes 589832 | tf_op jit(solution)/shard_map/ppermute | solution.py:579
  9.1 1.2 %collective-permute-start.3 = (f32[4,4,24,128]{3,2,1,0:T(8,128)S(1)}, f32[4,4,24,128]{3,2,1,0:T(8,128)S(1)}, u32[]{:S(2)}, u32[]{:S(2)}) collective-permute-start(f32[4,4,24,128]{3,2,1,0:T(8,128)S(1)} %get-tuple-element.54), channel_id=1, source_target_pairs={{0,16},{1,17},{2,18},{3,19},{4,8},{5,9},{6,10},{7,11},{8,4},{9,5},... | collective-permute-start | bytes 589832 | tf_op jit(solution)/shard_map/ppermute | solution.py:579
  10.3 0.0 collective-permute-done.8
  10.3 2.4 %collective-permute-start.9 = (f32[2,2,4,8,128]{4,3,2,1,0:T(8,128)S(1)}, f32[2,2,4,8,128]{4,3,2,1,0:T(8,128)S(1)}, u32[]{:S(2)}, u32[]{:S(2)}) collective-permute-start(f32[2,2,4,8,128]{4,3,2,1,0:T(8,128)S(1)} %pad_maximum_fusion.2), channel_id=1, source_target_pairs={{0,2},{1,3},{2,0},{3,1},{4,6},{5,7},{6,4},{7,5},{8,10},{9,11},{10,... | collective-permute-start | bytes 196616 | tf_op jit(solution)/shard_map/ppermute | solution.py:579
  12.8 1.7 %collective-permute-done.9 = f32[2,2,4,8,128]{4,3,2,1,0:T(8,128)S(1)} collective-permute-done((f32[2,2,4,8,128]{4,3,2,1,0:T(8,128)S(1)}, f32[2,2,4,8,128]{4,3,2,1,0:T(8,128)S(1)}, u32[]{:S(2)}, u32[]{:S(2)}) %collective-permute-start.9) | collective-permute-done | bytes 65568 | tf_op jit(solution)/shard_map/ppermute | solution.py:579
  14.4 0.0 collective-permute-done.2.in_a
  14.5 0.1 collective-permute-done.3.in_b
  14.5 1.6 %shard_map.88 = (f32[15,16,24,128]{3,2,1,0:T(8,128)S(1)}, f32[1,4,8,128]{3,2,1,0:T(8,128)S(1)}) custom-call(f32[3,6,128]{2,1,0:T(8,128)S(1)} %broadcast_in_dim.2.table, f32[4,8,24,128]{3,2,1,0:T(8,128)S(1)} %get-tuple-element.52.mid, f32[4,4,24,128]{3,2,1,0:T(8,128)S(1)} %collective-permute-done.2.in_a, f32[4,4,24,128]{3,2,1,0:T(8,128)S(1)} %collective-permute-done.3.in_b), custom_call_target="tpu_custom_call" | custom-call | tf_op jit(solution)/shard_map/pallas_call | solution.py:621
  16.2 1.0 %collective-permute-start.4 = (f32[1,4,8,128]{3,2,1,0:T(8,128)S(1)}, f32[1,4,8,128]{3,2,1,0:T(8,128)S(1)}, u32[]{:S(2)}, u32[]{:S(2)}) collective-permute-start(f32[1,4,8,128]{3,2,1,0:T(8,128)S(1)} %get-tuple-element.55), channel_id=1, source_target_pairs={{0,1},{1,0},{2,3},{3,2},{4,5},{5,4},{6,7},{7,6},{8,9},{9,8},{10,11... | collective-permute-start | bytes 49160 | tf_op jit(solution)/shard_map/ppermute | solution.py:579
  17.2 1.6 %collective-permute-done.4 = f32[1,4,8,128]{3,2,1,0:T(8,128)S(1)} collective-permute-done((f32[1,4,8,128]{3,2,1,0:T(8,128)S(1)}, f32[1,4,8,128]{3,2,1,0:T(8,128)S(1)}, u32[]{:S(2)}, u32[]{:S(2)}) %collective-permute-start.4) | collective-permute-done | bytes 16416 | tf_op jit(solution)/shard_map/ppermute | solution.py:579
  18.8 2.4 %collective-permute-start.5 = (f32[2,4,8,128]{3,2,1,0:T(8,128)S(1)}, f32[2,4,8,128]{3,2,1,0:T(8,128)S(1)}, u32[]{:S(2)}, u32[]{:S(2)}) collective-permute-start(f32[2,4,8,128]{3,2,1,0:T(8,128)S(1)} %get-tuple-element.84), channel_id=1, source_target_pairs={{0,2},{1,3},{2,0},{3,1},{4,6},{5,7},{6,4},{7,5},{8,10},{9,11},{10,... | collective-permute-start | bytes 98312 | tf_op jit(solution)/shard_map/ppermute | solution.py:579
  21.2 1.9 %collective-permute-start.10 = (f32[4,2,4,8,128]{4,3,2,1,0:T(8,128)S(1)}, f32[4,2,4,8,128]{4,3,2,1,0:T(8,128)S(1)}, u32[]{:S(2)}, u32[]{:S(2)}) collective-permute-start(f32[4,2,4,8,128]{4,3,2,1,0:T(8,128)S(1)} %pad_maximum_fusion), channel_id=1, source_target_pairs={{0,8},{1,9},{2,10},{3,11},{4,12},{5,13},{6,14},{7,15},{8,0},{9,1},... | collective-permute-start | bytes 393224 | tf_op jit(solution)/shard_map/ppermute | solution.py:579
  23.1 0.0 collective-permute-done.5
  23.2 1.6 %collective-permute-start.6 = (f32[4,4,8,128]{3,2,1,0:T(8,128)S(1)}, f32[4,4,8,128]{3,2,1,0:T(8,128)S(1)}, u32[]{:S(2)}, u32[]{:S(2)}) collective-permute-start(f32[4,4,8,128]{3,2,1,0:T(8,128)S(1)} %pad_maximum_fusion.1), channel_id=1, source_target_pairs={{0,8},{1,9},{2,10},{3,11},{4,12},{5,13},{6,14},{7,15},{8,0},{9,1},... | collective-permute-start | bytes 196616 | tf_op jit(solution)/shard_map/ppermute | solution.py:579
  24.8 0.7 %collective-permute-done.10 = f32[4,2,4,8,128]{4,3,2,1,0:T(8,128)S(1)} collective-permute-done((f32[4,2,4,8,128]{4,3,2,1,0:T(8,128)S(1)}, f32[4,2,4,8,128]{4,3,2,1,0:T(8,128)S(1)}, u32[]{:S(2)}, u32[]{:S(2)}) %collective-permute-start.10) | collective-permute-done | bytes 131104 | tf_op jit(solution)/shard_map/ppermute | solution.py:579
  25.5 3.7 %collective-permute-start.11 = (f32[8,2,4,8,128]{4,3,2,1,0:T(8,128)S(1)}, f32[8,2,4,8,128]{4,3,2,1,0:T(8,128)S(1)}, u32[]{:S(2)}, u32[]{:S(2)}) collective-permute-start(f32[8,2,4,8,128]{4,3,2,1,0:T(8,128)S(1)} %constant_dynamic-update-slice_fusion.6.near), channel_id=1, source_target_pairs={{0,4},{1,5},{2,6},{3,7},{4,0},{5,1},{6,2},{7,3},{8,12},{9,13},{10,... | collective-permute-start | bytes 786440 | tf_op jit(solution)/shard_map/ppermute | solution.py:579
  29.2 0.0 collective-permute-done.6
  29.2 1.8 %collective-permute-start.7 = (f32[8,4,8,128]{3,2,1,0:T(8,128)S(1)}, f32[8,4,8,128]{3,2,1,0:T(8,128)S(1)}, u32[]{:S(2)}, u32[]{:S(2)}) collective-permute-start(f32[8,4,8,128]{3,2,1,0:T(8,128)S(1)} %constant_dynamic-update-slice_fusion.2.near), channel_id=1, source_target_pairs={{0,4},{1,5},{2,6},{3,7},{4,0},{5,1},{6,2},{7,3},{8,12},{9,13},{10,... | collective-permute-start | bytes 393224 | tf_op jit(solution)/shard_map/ppermute | solution.py:579
  31.1 0.0 collective-permute-done.11.far
  31.1 1.9 %shard_map.90 = (f32[17,32,128]{2,1,0:T(8,128)S(1)}, f32[17,32,128]{2,1,0:T(8,128)S(1)}, f32[16,32,128]{2,1,0:T(8,128)S(1)}, f32[16,32,128]{2,1,0:T(8,128)S(1)},...) custom-call(f32[8,2,4,8,128]{4,3,2,1,0:T(8,128)S(1)} %constant_dynam, ...), custom_call_target="tpu_custom_call" | custom-call | tf_op jit(solution)/shard_map/pallas_call | solution.py:652
  33.0 0.0 collective-permute-done.7.far
  33.0 4.2 %shard_map.91 = (f32[8,16,128]{2,1,0:T(8,128)}, f32[8,16,128]{2,1,0:T(8,128)}) custom-call(f32[8,4,8,128]{3,2,1,0:T(8,128)S(1)} %constant_dynamic-update-slice_fusion.2.near, f32[8,4,8,128]{3,2,1,0:T(8,128)S(1)} %collective-permute-done.7.far, f32[15,16,24,128]{3,2,1,0:T(8,128)S(1)} %get-tuple-element.56.kept, f32[17,32,128]{2,1,0:T(8,128)S(1)} %get-tuple-element.60.refs_0_, ...), custom_call_target="tpu_custom_call" | custom-call | tf_op jit(solution)/shard_map/pallas_call | solution.py:662
  (9 shorter events, 0.1 us)
Async XLA Ops:
  1.6 5.9 %collective-permute-start = (f32[16,8,128]{2,1,0:T(8,128)S(1)}, f32[16,8,128]{2,1,0:T(8,128)S(1)}, u32[]{:S(2)}, u32[]{:S(2)}) collective-permute-start(f32[16,8,128]{2,1,0:T(8,128)S(1)} %get-tuple-element.44), channel_id=1, source_target_pairs={{0,1},{1,0},{2,3},{3,2},{4,5},{5,4},{6,7},{7,6},{8,9},{9,8},{10,11... | collective-permute-start | bytes 196616 | tf_op jit(solution)/shard_map/ppermute | solution.py:579
  3.8 3.7 %collective-permute-start.1 = (f32[16,8,128]{2,1,0:T(8,128)S(1)}, f32[16,8,128]{2,1,0:T(8,128)S(1)}, u32[]{:S(2)}, u32[]{:S(2)}) collective-permute-start(f32[16,8,128]{2,1,0:T(8,128)S(1)} %get-tuple-element.51), channel_id=1, source_target_pairs={{0,4},{1,2},{2,1},{3,7},{4,0},{5,6},{6,5},{7,3},{8,12},{9,10},{10,... | collective-permute-start | bytes 196616 | tf_op jit(solution)/shard_map/ppermute | solution.py:579
  5.8 4.5 %collective-permute-start.8 = (f32[1,2,4,8,128]{4,3,2,1,0:T(8,128)S(1)}, f32[1,2,4,8,128]{4,3,2,1,0:T(8,128)S(1)}, u32[]{:S(2)}, u32[]{:S(2)}) collective-permute-start(f32[1,2,4,8,128]{4,3,2,1,0:T(8,128)S(1)} %shard_map.89), channel_id=1, source_target_pairs={{0,1},{1,0},{2,3},{3,2},{4,5},{5,4},{6,7},{7,6},{8,9},{9,8},{10,11... | collective-permute-start | bytes 98312 | tf_op jit(solution)/shard_map/ppermute | solution.py:579
  7.6 6.9 %collective-permute-start.2 = (f32[4,4,24,128]{3,2,1,0:T(8,128)S(1)}, f32[4,4,24,128]{3,2,1,0:T(8,128)S(1)}, u32[]{:S(2)}, u32[]{:S(2)}) collective-permute-start(f32[4,4,24,128]{3,2,1,0:T(8,128)S(1)} %get-tuple-element.53), channel_id=1, source_target_pairs={{0,4},{1,5},{2,6},{3,7},{4,0},{5,1},{6,2},{7,3},{8,12},{9,13},{10,... | collective-permute-start | bytes 589832 | tf_op jit(solution)/shard_map/ppermute | solution.py:579
  9.1 5.4 %collective-permute-start.3 = (f32[4,4,24,128]{3,2,1,0:T(8,128)S(1)}, f32[4,4,24,128]{3,2,1,0:T(8,128)S(1)}, u32[]{:S(2)}, u32[]{:S(2)}) collective-permute-start(f32[4,4,24,128]{3,2,1,0:T(8,128)S(1)} %get-tuple-element.54), channel_id=1, source_target_pairs={{0,16},{1,17},{2,18},{3,19},{4,8},{5,9},{6,10},{7,11},{8,4},{9,5},... | collective-permute-start | bytes 589832 | tf_op jit(solution)/shard_map/ppermute | solution.py:579
  10.3 4.1 %collective-permute-start.9 = (f32[2,2,4,8,128]{4,3,2,1,0:T(8,128)S(1)}, f32[2,2,4,8,128]{4,3,2,1,0:T(8,128)S(1)}, u32[]{:S(2)}, u32[]{:S(2)}) collective-permute-start(f32[2,2,4,8,128]{4,3,2,1,0:T(8,128)S(1)} %pad_maximum_fusion.2), channel_id=1, source_target_pairs={{0,2},{1,3},{2,0},{3,1},{4,6},{5,7},{6,4},{7,5},{8,10},{9,11},{10,... | collective-permute-start | bytes 196616 | tf_op jit(solution)/shard_map/ppermute | solution.py:579
  16.2 2.6 %collective-permute-start.4 = (f32[1,4,8,128]{3,2,1,0:T(8,128)S(1)}, f32[1,4,8,128]{3,2,1,0:T(8,128)S(1)}, u32[]{:S(2)}, u32[]{:S(2)}) collective-permute-start(f32[1,4,8,128]{3,2,1,0:T(8,128)S(1)} %get-tuple-element.55), channel_id=1, source_target_pairs={{0,1},{1,0},{2,3},{3,2},{4,5},{5,4},{6,7},{7,6},{8,9},{9,8},{10,11... | collective-permute-start | bytes 49160 | tf_op jit(solution)/shard_map/ppermute | solution.py:579
  18.8 4.4 %collective-permute-start.5 = (f32[2,4,8,128]{3,2,1,0:T(8,128)S(1)}, f32[2,4,8,128]{3,2,1,0:T(8,128)S(1)}, u32[]{:S(2)}, u32[]{:S(2)}) collective-permute-start(f32[2,4,8,128]{3,2,1,0:T(8,128)S(1)} %get-tuple-element.84), channel_id=1, source_target_pairs={{0,2},{1,3},{2,0},{3,1},{4,6},{5,7},{6,4},{7,5},{8,10},{9,11},{10,... | collective-permute-start | bytes 98312 | tf_op jit(solution)/shard_map/ppermute | solution.py:579
  21.2 4.3 %collective-permute-start.10 = (f32[4,2,4,8,128]{4,3,2,1,0:T(8,128)S(1)}, f32[4,2,4,8,128]{4,3,2,1,0:T(8,128)S(1)}, u32[]{:S(2)}, u32[]{:S(2)}) collective-permute-start(f32[4,2,4,8,128]{4,3,2,1,0:T(8,128)S(1)} %pad_maximum_fusion), channel_id=1, source_target_pairs={{0,8},{1,9},{2,10},{3,11},{4,12},{5,13},{6,14},{7,15},{8,0},{9,1},... | collective-permute-start | bytes 393224 | tf_op jit(solution)/shard_map/ppermute | solution.py:579
  23.2 6.1 %collective-permute-start.6 = (f32[4,4,8,128]{3,2,1,0:T(8,128)S(1)}, f32[4,4,8,128]{3,2,1,0:T(8,128)S(1)}, u32[]{:S(2)}, u32[]{:S(2)}) collective-permute-start(f32[4,4,8,128]{3,2,1,0:T(8,128)S(1)} %pad_maximum_fusion.1), channel_id=1, source_target_pairs={{0,8},{1,9},{2,10},{3,11},{4,12},{5,13},{6,14},{7,15},{8,0},{9,1},... | collective-permute-start | bytes 196616 | tf_op jit(solution)/shard_map/ppermute | solution.py:579
  25.5 5.6 %collective-permute-start.11 = (f32[8,2,4,8,128]{4,3,2,1,0:T(8,128)S(1)}, f32[8,2,4,8,128]{4,3,2,1,0:T(8,128)S(1)}, u32[]{:S(2)}, u32[]{:S(2)}) collective-permute-start(f32[8,2,4,8,128]{4,3,2,1,0:T(8,128)S(1)} %constant_dynamic-update-slice_fusion.6.near), channel_id=1, source_target_pairs={{0,4},{1,5},{2,6},{3,7},{4,0},{5,1},{6,2},{7,3},{8,12},{9,13},{10,... | collective-permute-start | bytes 786440 | tf_op jit(solution)/shard_map/ppermute | solution.py:579
  29.2 3.8 %collective-permute-start.7 = (f32[8,4,8,128]{3,2,1,0:T(8,128)S(1)}, f32[8,4,8,128]{3,2,1,0:T(8,128)S(1)}, u32[]{:S(2)}, u32[]{:S(2)}) collective-permute-start(f32[8,4,8,128]{3,2,1,0:T(8,128)S(1)} %constant_dynamic-update-slice_fusion.2.near), channel_id=1, source_target_pairs={{0,4},{1,5},{2,6},{3,7},{4,0},{5,1},{6,2},{7,3},{8,12},{9,13},{10,... | collective-permute-start | bytes 393224 | tf_op jit(solution)/shard_map/ppermute | solution.py:579

commit v5 on v4

--- a/solution.py
+++ b/solution.py
@@ -32,8 +32,8 @@
 
 def bernoulli(x):
     t = x * x
-    series = 1.0 - 0.5 * x + t * (1 / 12 + t * (-1 / 720 + t * (1 / 30240)))
-    near = t < 0.25
+    series = (1.0 - 0.5 * x) + t * (1 / 12 - t * (1 / 720))
+    near = t < 0.0625
     guarded = jnp.where(near, 1.0, x)
     return jnp.where(near, series, guarded / (jnp.exp(guarded) - 1.0))
 
@@ -68,7 +68,7 @@
     return found
 
 
-def rim_y_kernel(c_in, p_in, fp_in, fn_in, out_a, out_b, c_out, p_out, fp_out, fn_out, cls, sems):
+def rim_y_kernel(table, c_in, p_in, fp_in, fn_in, out_a, out_b, block, c_out, p_out, fp_out, fn_out, cls, work, sems):
     outs = (c_out, p_out, fp_out, fn_out)
     copies = [
         pltpu.make_async_copy(s, d, sems.at[k])
@@ -88,16 +88,10 @@
         )
         out_a[pair * planes : (pair + 1) * planes] = jnp.where(even, hi, lo)
         out_b[pair * planes : (pair + 1) * planes] = jnp.where(even, lo, hi)
-
-
-def fields_kernel(table, cls, pot, block, work):
-    planes, length = cls.shape[0], cls.shape[1]
     bx = planes // 2
     for i in range(bx):
-        one, two = (
-            look_up(table, cls[2 * i + k], (length, LANES)) for k in (0, 1)
-        )
-        values = [p + q for p, q in zip(one, two)] + [pot[2 * i] + pot[2 * i + 1]]
+        one, two = (look_up(table, c_out[2 * i + k], (length, LANES)) for k in (0, 1))
+        values = [p + q for p, q in zip(one, two)] + [p_out[2 * i] + p_out[2 * i + 1]]
         for k, v in enumerate(values):
             work[k, i] = v
     for i in range(bx):
@@ -419,7 +413,9 @@
             new.append(r + t + s)
         return tuple(new)
 
-    u = lax.fori_loop(0, COARSE_ITERS - 1, body, tuple(wf))
+    u = tuple(wf)
+    for _ in range(COARSE_ITERS - 1):
+        u = body(0, u)
     for i in range(nx):
         lv.u[i + 1] = u[i]
 
@@ -584,30 +580,29 @@
     def shape(*dims):
         return jax.ShapeDtypeStruct(dims, f32)
 
+    table = jnp.stack([permittivity, mobility, capture])
+    table = jnp.broadcast_to(table[:, :, None], (*table.shape, LANES))
     cell = (planes, own, LANES)
-    a, b, *raw = pl.pallas_call(
+    a, b, fields, *raw = pl.pallas_call(
         rim_y_kernel,
-        out_shape=[shape(2 * planes, by, LANES)] * 2 + [shape(*cell)] * 4,
-        in_specs=[HBM] * 4,
-        out_specs=[VMEM] * 6,
-        scratch_shapes=[pltpu.VMEM(cell, jnp.int32), pltpu.SemaphoreType.DMA((4,))],
-        compiler_params=params(53.55),
-    )(layer_class, potential, rhs_psi, rhs_n)
-    cut = a
+        out_shape=[
+            shape(2 * planes, by, LANES),
+            shape(2 * planes, by, LANES),
+            shape(1, 2, bx, by, LANES),
+        ]
+        + [shape(*cell)] * 4,
+        in_specs=[VMEM] + [HBM] * 4,
+        out_specs=[VMEM] * 7,
+        scratch_shapes=[
+            pltpu.VMEM(cell, jnp.int32),
+            pltpu.VMEM((4, bx, own, LANES), f32),
+            pltpu.SemaphoreType.DMA((4,)),
+        ],
+        compiler_params=params(53.5),
+    )(table, layer_class, potential, rhs_psi, rhs_n)
     b = permute(b, "yb")
-    a = permute(a, "ya")
-    later, _ = lax.optimization_barrier(((permittivity, mobility, capture, raw[1]), cut))
-    table = jnp.stack(later[:3])
-    table = jnp.broadcast_to(table[:, :, None], (*table.shape, LANES))
-    fields = pl.pallas_call(
-        fields_kernel,
-        out_shape=shape(1, 2, bx, by, LANES),
-        in_specs=[VMEM] * 3,
-        out_specs=VMEM,
-        scratch_shapes=[pltpu.VMEM((4, bx, own, LANES), f32)],
-        compiler_params=params(16),
-    )(table, raw[0], later[3])
-    fields_y = [fields, permute(fields, ("y", 1))]
+    a = permute(jnp.concatenate([a, fields.reshape(-1, by, LANES)]), "ya")
+    fields_y = [fields, a[2 * planes :].reshape(fields.shape)]
     mid, a, b = pl.pallas_call(
         rim_x_kernel,
         out_shape=[shape(4, planes, rows, LANES)] + [shape(4, RIM, rows, LANES)] * 2,
@@ -644,9 +639,10 @@
             near = jnp.concatenate([near, permute(near, ("x", bit))], axis=0)
         return near, permute(near, ("x", bits[-1]))
 
-    fields_y = over_y(fields_y, 2)
+    halves = [fields_y, permute(fields_y, ("y", 2))]
     pair = jnp.concatenate([block, permute(block, ("y", 1))])
-    fields_y, _ = lax.optimization_barrier((fields_y, pair))
+    halves, _ = lax.optimization_barrier((halves, pair))
+    fields_y = over_y(jnp.concatenate(halves), 4)
     grids = [(bx * nx >> level, by * ny >> level) for level in range(3)]
     large = grids[0][0] * grids[0][1] > 1024
     operators = pl.pallas_call(

time: 37.4 us -> 36.5 us (0.976)
  starting transfers between devices: 22.5 us -> 20.2 us
  waiting for transfers between devices: 4.12 us -> 5.61 us
  Pallas kernels: 9.05 us -> 8.59 us
    ppermute x12 -> x11, starting transfers between devices: 22.5 us -> 20.2 us  [permute(): return lax.ppermute(v, ('groups', 'gx', 'gy'), send[name])]
    ppermute x12 -> x11, waiting for transfers between devices: 4.12 us -> 5.61 us  [permute(): return lax.ppermute(v, ('groups', 'gx', 'gy'), send[name])]
    pallas_call x1, Pallas kernels: 4.19 us -> 3.8 us  [per_device(): pl.pallas_call(functools.partial(second_kernel, tuple(bits)), out_shape=[...]
    pallas_call x2 -> x1, Pallas kernels: 1.22 us -> 1.24 us  [per_device(): pl.pallas_call(rim_y_kernel, out_shape=[shape(2 * planes, by, LANES), sha...]
  transfers between devices with their start and end apart: 12 -> 11, of which waited for: 4 -> 7; matrix products, arithmetic and copies ran while one was open for 2% -> 0% of each run, Pallas kernels for 6% -> 10%
where the time goes in v5:
time: 36.5 us; the launch traced here: 36 us
  starting transfers between devices  20.2 us (55%)
  Pallas kernels  8.59 us (24%)
  waiting for transfers between devices  5.61 us (15%)
  other arithmetic  0.73 us (2%)
  between operations  0.7 us (2%)
    ppermute x11, starting transfers between devices, permute(): return lax.ppermute(v, ('groups', 'gx', 'gy'), send[name])  20.2 us
    ppermute x11, waiting for transfers between devices, permute(): return lax.ppermute(v, ('groups', 'gx', 'gy'), send[name])  5.61 us
    pallas_call x1, Pallas kernels, per_device(): pl.pallas_call(functools.partial(second_kernel, tuple(bits)), out_shape=[...  3.8 us
    pallas_call x1, Pallas kernels, per_device(): pl.pallas_call(functools.partial(operators_kernel, tuple(bits)), out_shap...  1.87 us
    pallas_call x1, Pallas kernels, per_device(): pl.pallas_call(first_kernel, out_shape=[shape(KEPT, total, rows, LANES),...  1.61 us
    pallas_call x1, Pallas kernels, per_device(): pl.pallas_call(rim_y_kernel, out_shape=[shape(2 * planes, by, LANES), sha...  1.24 us
  transfers between devices with their start and end apart: 11, of which 7 were waited for; matrix products, arithmetic and copies ran while one was open for 0% of the time, Pallas kernels for 10%

profile of v5, /device:TPU:1, one launch (start us, length us, event | category | flops | bytes accessed | tf_op | source)
XLA Modules:
  0.0 36.0 jit_solution(745190006380900234)
XLA Ops:
  0.6 0.7 %pad_maximum_fusion.4 = f32[3,6]{1,0:T(4,128)S(1)} fusion(f32[1,6]{1,0:T(1,128)} %bitcast.7, f32[1,6]{1,0:T(1,128)} %bitcast.8, f32[1,6]{1,0:T(1,128)} %bitcast.9), kind=kLoop, calls=%fused_computation.13 | loop fusion | flops 36 | bytes 144 | tf_op jit(solution)/shard_map/stack | solution.py:583
  1.3 0.1 broadcast_in_dim.2.table
  1.4 1.2 %shard_map.86 = (f32[16,8,128]{2,1,0:T(8,128)S(1)}, f32[16,8,128]{2,1,0:T(8,128)S(1)}, f32[1,2,4,8,128]{4,3,2,1,0:T(8,128)S(1)}, f32[8,16,128]{2,1,0:T(8,128)S(1...) custom-call(f32[3,6,128]{2,1,0:T(8,128)S(1)} %broadcast_in_dim.2.table, ...), custom_call_target="tpu_custom_call" | custom-call | tf_op jit(solution)/shard_map/pallas_call | solution.py:586
  2.7 2.2 %collective-permute-start = (f32[24,8,128]{2,1,0:T(8,128)S(1)}, f32[24,8,128]{2,1,0:T(8,128)S(1)}, u32[]{:S(2)}, u32[]{:S(2)}) collective-permute-start(f32[24,8,128]{2,1,0:T(8,128)S(1)} %pad_maximum_fusion.1), channel_id=1, source_target_pairs={{0,1},{1,0},{2,3},{3,2},{4,5},{5,4},{6,7},{7,6},{8,9},{9,8},{10,11... | collective-permute-start | bytes 294920 | tf_op jit(solution)/shard_map/ppermute | solution.py:575
  4.9 1.0 %collective-permute-start.1 = (f32[16,8,128]{2,1,0:T(8,128)S(1)}, f32[16,8,128]{2,1,0:T(8,128)S(1)}, u32[]{:S(2)}, u32[]{:S(2)}) collective-permute-start(f32[16,8,128]{2,1,0:T(8,128)S(1)} %get-tuple-element.47), channel_id=1, source_target_pairs={{0,4},{1,2},{2,1},{3,7},{4,0},{5,6},{6,5},{7,3},{8,12},{9,10},{10,... | collective-permute-start | bytes 196616 | tf_op jit(solution)/shard_map/ppermute | solution.py:575
  5.8 0.9 %collective-permute-done.1.in_b = f32[16,8,128]{2,1,0:T(8,128)S(1)} collective-permute-done((f32[16,8,128]{2,1,0:T(8,128)S(1)}, f32[16,8,128]{2,1,0:T(8,128)S(1)}, u32[]{:S(2)}, u32[]{:S(2)}) %collective-permute-start.1) | collective-permute-done | bytes 65568 | tf_op jit(solution)/shard_map/ppermute | solution.py:575
  6.7 0.7 %collective-permute-done.in_a = f32[24,8,128]{2,1,0:T(8,128)S(1)} collective-permute-done((f32[24,8,128]{2,1,0:T(8,128)S(1)}, f32[24,8,128]{2,1,0:T(8,128)S(1)}, u32[]{:S(2)}, u32[]{:S(2)}) %collective-permute-start) | collective-permute-done | bytes 98336 | tf_op jit(solution)/shard_map/ppermute | solution.py:575
  7.4 0.1 shard_map.87
  7.5 1.3 %collective-permute-start.2 = (f32[4,4,24,128]{3,2,1,0:T(8,128)S(1)}, f32[4,4,24,128]{3,2,1,0:T(8,128)S(1)}, u32[]{:S(2)}, u32[]{:S(2)}) collective-permute-start(f32[4,4,24,128]{3,2,1,0:T(8,128)S(1)} %get-tuple-element.49), channel_id=1, source_target_pairs={{0,4},{1,5},{2,6},{3,7},{4,0},{5,1},{6,2},{7,3},{8,12},{9,13},{10,... | collective-permute-start | bytes 589832 | tf_op jit(solution)/shard_map/ppermute | solution.py:575
  8.7 1.4 %collective-permute-start.3 = (f32[4,4,24,128]{3,2,1,0:T(8,128)S(1)}, f32[4,4,24,128]{3,2,1,0:T(8,128)S(1)}, u32[]{:S(2)}, u32[]{:S(2)}) collective-permute-start(f32[4,4,24,128]{3,2,1,0:T(8,128)S(1)} %get-tuple-element.50), channel_id=1, source_target_pairs={{0,16},{1,17},{2,18},{3,19},{4,8},{5,9},{6,10},{7,11},{8,4},{9,5},... | collective-permute-start | bytes 589832 | tf_op jit(solution)/shard_map/ppermute | solution.py:575
  10.2 3.6 %collective-permute-start.8 = (f32[2,2,4,8,128]{4,3,2,1,0:T(8,128)S(1)}, f32[2,2,4,8,128]{4,3,2,1,0:T(8,128)S(1)}, u32[]{:S(2)}, u32[]{:S(2)}) collective-permute-start(f32[2,2,4,8,128]{4,3,2,1,0:T(8,128)S(1)} %pad_maximum_fusion.3), channel_id=1, source_target_pairs={{0,2},{1,3},{2,0},{3,1},{4,6},{5,7},{6,4},{7,5},{8,10},{9,11},{10,... | collective-permute-start | bytes 196616 | tf_op jit(solution)/shard_map/ppermute | solution.py:575
  13.8 0.0 collective-permute-done.2.in_a
  13.8 0.3 collective-permute-done.3.in_b
  14.1 1.6 %shard_map.88 = (f32[15,16,24,128]{3,2,1,0:T(8,128)S(1)}, f32[1,4,8,128]{3,2,1,0:T(8,128)S(1)}) custom-call(f32[3,6,128]{2,1,0:T(8,128)S(1)} %broadcast_in_dim.2.table, f32[4,8,24,128]{3,2,1,0:T(8,128)S(1)} %get-tuple-element.48.mid, f32[4,4,24,128]{3,2,1,0:T(8,128)S(1)} %collective-permute-done.2.in_a, f32[4,4,24,128]{3,2,1,0:T(8,128)S(1)} %collective-permute-done.3.in_b), custom_call_target="tpu_custom_call" | custom-call | tf_op jit(solution)/shard_map/pallas_call | solution.py:616
  15.7 2.4 %collective-permute-start.4 = (f32[1,4,8,128]{3,2,1,0:T(8,128)S(1)}, f32[1,4,8,128]{3,2,1,0:T(8,128)S(1)}, u32[]{:S(2)}, u32[]{:S(2)}) collective-permute-start(f32[1,4,8,128]{3,2,1,0:T(8,128)S(1)} %get-tuple-element.51), channel_id=1, source_target_pairs={{0,1},{1,0},{2,3},{3,2},{4,5},{5,4},{6,7},{7,6},{8,9},{9,8},{10,11... | collective-permute-start | bytes 49160 | tf_op jit(solution)/shard_map/ppermute | solution.py:575
  18.1 1.1 %collective-permute-done.4 = f32[1,4,8,128]{3,2,1,0:T(8,128)S(1)} collective-permute-done((f32[1,4,8,128]{3,2,1,0:T(8,128)S(1)}, f32[1,4,8,128]{3,2,1,0:T(8,128)S(1)}, u32[]{:S(2)}, u32[]{:S(2)}) %collective-permute-start.4) | collective-permute-done | bytes 16416 | tf_op jit(solution)/shard_map/ppermute | solution.py:575
  19.2 2.9 %collective-permute-start.5 = (f32[2,4,8,128]{3,2,1,0:T(8,128)S(1)}, f32[2,4,8,128]{3,2,1,0:T(8,128)S(1)}, u32[]{:S(2)}, u32[]{:S(2)}) collective-permute-start(f32[2,4,8,128]{3,2,1,0:T(8,128)S(1)} %get-tuple-element.80), channel_id=1, source_target_pairs={{0,2},{1,3},{2,0},{3,1},{4,6},{5,7},{6,4},{7,5},{8,10},{9,11},{10,... | collective-permute-start | bytes 98312 | tf_op jit(solution)/shard_map/ppermute | solution.py:575
  22.1 0.0 collective-permute-done.8
  22.2 0.7 %collective-permute-start.9 = (f32[4,2,4,8,128]{4,3,2,1,0:T(8,128)S(1)}, f32[4,2,4,8,128]{4,3,2,1,0:T(8,128)S(1)}, u32[]{:S(2)}, u32[]{:S(2)}) collective-permute-start(f32[4,2,4,8,128]{4,3,2,1,0:T(8,128)S(1)} %pad_maximum_fusion), channel_id=1, source_target_pairs={{0,8},{1,9},{2,10},{3,11},{4,12},{5,13},{6,14},{7,15},{8,0},{9,1},... | collective-permute-start | bytes 393224 | tf_op jit(solution)/shard_map/ppermute | solution.py:575
  22.9 0.5 %collective-permute-done.5 = f32[2,4,8,128]{3,2,1,0:T(8,128)S(1)} collective-permute-done((f32[2,4,8,128]{3,2,1,0:T(8,128)S(1)}, f32[2,4,8,128]{3,2,1,0:T(8,128)S(1)}, u32[]{:S(2)}, u32[]{:S(2)}) %collective-permute-start.5) | collective-permute-done | bytes 32800 | tf_op jit(solution)/shard_map/ppermute | solution.py:575
  23.4 0.7 %collective-permute-start.6 = (f32[4,4,8,128]{3,2,1,0:T(8,128)S(1)}, f32[4,4,8,128]{3,2,1,0:T(8,128)S(1)}, u32[]{:S(2)}, u32[]{:S(2)}) collective-permute-start(f32[4,4,8,128]{3,2,1,0:T(8,128)S(1)} %pad_maximum_fusion.2), channel_id=1, source_target_pairs={{0,8},{1,9},{2,10},{3,11},{4,12},{5,13},{6,14},{7,15},{8,0},{9,1},... | collective-permute-start | bytes 196616 | tf_op jit(solution)/shard_map/ppermute | solution.py:575
  24.1 1.9 %collective-permute-done.9 = f32[4,2,4,8,128]{4,3,2,1,0:T(8,128)S(1)} collective-permute-done((f32[4,2,4,8,128]{4,3,2,1,0:T(8,128)S(1)}, f32[4,2,4,8,128]{4,3,2,1,0:T(8,128)S(1)}, u32[]{:S(2)}, u32[]{:S(2)}) %collective-permute-start.9) | collective-permute-done | bytes 131104 | tf_op jit(solution)/shard_map/ppermute | solution.py:575
  26.1 3.0 %collective-permute-start.10 = (f32[8,2,4,8,128]{4,3,2,1,0:T(8,128)S(1)}, f32[8,2,4,8,128]{4,3,2,1,0:T(8,128)S(1)}, u32[]{:S(2)}, u32[]{:S(2)}) collective-permute-start(f32[8,2,4,8,128]{4,3,2,1,0:T(8,128)S(1)} %constant_dynamic-update-slice_fusion.6.near), channel_id=1, source_target_pairs={{0,4},{1,5},{2,6},{3,7},{4,0},{5,1},{6,2},{7,3},{8,12},{9,13},{10,... | collective-permute-start | bytes 786440 | tf_op jit(solution)/shard_map/ppermute | solution.py:575
  29.1 0.0 collective-permute-done.6
  29.1 1.0 %collective-permute-start.7 = (f32[8,4,8,128]{3,2,1,0:T(8,128)S(1)}, f32[8,4,8,128]{3,2,1,0:T(8,128)S(1)}, u32[]{:S(2)}, u32[]{:S(2)}) collective-permute-start(f32[8,4,8,128]{3,2,1,0:T(8,128)S(1)} %constant_dynamic-update-slice_fusion.2.near), channel_id=1, source_target_pairs={{0,4},{1,5},{2,6},{3,7},{4,0},{5,1},{6,2},{7,3},{8,12},{9,13},{10,... | collective-permute-start | bytes 393224 | tf_op jit(solution)/shard_map/ppermute | solution.py:575
  30.1 0.1 collective-permute-done.10.far
  30.3 1.9 %shard_map.89 = (f32[17,32,128]{2,1,0:T(8,128)S(1)}, f32[17,32,128]{2,1,0:T(8,128)S(1)}, f32[16,32,128]{2,1,0:T(8,128)S(1)}, f32[16,32,128]{2,1,0:T(8,128)S(1)},...) custom-call(f32[8,2,4,8,128]{4,3,2,1,0:T(8,128)S(1)} %constant_dynam, ...), custom_call_target="tpu_custom_call" | custom-call | tf_op jit(solution)/shard_map/pallas_call | solution.py:648
  32.1 0.0 collective-permute-done.7.far
  32.2 3.8 %shard_map.90 = (f32[8,16,128]{2,1,0:T(8,128)}, f32[8,16,128]{2,1,0:T(8,128)}) custom-call(f32[8,4,8,128]{3,2,1,0:T(8,128)S(1)} %constant_dynamic-update-slice_fusion.2.near, f32[8,4,8,128]{3,2,1,0:T(8,128)S(1)} %collective-permute-done.7.far, f32[15,16,24,128]{3,2,1,0:T(8,128)S(1)} %get-tuple-element.52.kept, f32[17,32,128]{2,1,0:T(8,128)S(1)} %get-tuple-element.56.refs_0_, ...), custom_call_target="tpu_custom_call" | custom-call | tf_op jit(solution)/shard_map/pallas_call | solution.py:658
  (12 shorter events, 0.1 us)
Async XLA Ops:
  2.7 4.7 %collective-permute-start = (f32[24,8,128]{2,1,0:T(8,128)S(1)}, f32[24,8,128]{2,1,0:T(8,128)S(1)}, u32[]{:S(2)}, u32[]{:S(2)}) collective-permute-start(f32[24,8,128]{2,1,0:T(8,128)S(1)} %pad_maximum_fusion.1), channel_id=1, source_target_pairs={{0,1},{1,0},{2,3},{3,2},{4,5},{5,4},{6,7},{7,6},{8,9},{9,8},{10,11... | collective-permute-start | bytes 294920 | tf_op jit(solution)/shard_map/ppermute | solution.py:575
  4.9 1.9 %collective-permute-start.1 = (f32[16,8,128]{2,1,0:T(8,128)S(1)}, f32[16,8,128]{2,1,0:T(8,128)S(1)}, u32[]{:S(2)}, u32[]{:S(2)}) collective-permute-start(f32[16,8,128]{2,1,0:T(8,128)S(1)} %get-tuple-element.47), channel_id=1, source_target_pairs={{0,4},{1,2},{2,1},{3,7},{4,0},{5,6},{6,5},{7,3},{8,12},{9,10},{10,... | collective-permute-start | bytes 196616 | tf_op jit(solution)/shard_map/ppermute | solution.py:575
  7.5 6.3 %collective-permute-start.2 = (f32[4,4,24,128]{3,2,1,0:T(8,128)S(1)}, f32[4,4,24,128]{3,2,1,0:T(8,128)S(1)}, u32[]{:S(2)}, u32[]{:S(2)}) collective-permute-start(f32[4,4,24,128]{3,2,1,0:T(8,128)S(1)} %get-tuple-element.49), channel_id=1, source_target_pairs={{0,4},{1,5},{2,6},{3,7},{4,0},{5,1},{6,2},{7,3},{8,12},{9,13},{10,... | collective-permute-start | bytes 589832 | tf_op jit(solution)/shard_map/ppermute | solution.py:575
  8.7 5.4 %collective-permute-start.3 = (f32[4,4,24,128]{3,2,1,0:T(8,128)S(1)}, f32[4,4,24,128]{3,2,1,0:T(8,128)S(1)}, u32[]{:S(2)}, u32[]{:S(2)}) collective-permute-start(f32[4,4,24,128]{3,2,1,0:T(8,128)S(1)} %get-tuple-element.50), channel_id=1, source_target_pairs={{0,16},{1,17},{2,18},{3,19},{4,8},{5,9},{6,10},{7,11},{8,4},{9,5},... | collective-permute-start | bytes 589832 | tf_op jit(solution)/shard_map/ppermute | solution.py:575
  10.2 12.0 %collective-permute-start.8 = (f32[2,2,4,8,128]{4,3,2,1,0:T(8,128)S(1)}, f32[2,2,4,8,128]{4,3,2,1,0:T(8,128)S(1)}, u32[]{:S(2)}, u32[]{:S(2)}) collective-permute-start(f32[2,2,4,8,128]{4,3,2,1,0:T(8,128)S(1)} %pad_maximum_fusion.3), channel_id=1, source_target_pairs={{0,2},{1,3},{2,0},{3,1},{4,6},{5,7},{6,4},{7,5},{8,10},{9,11},{10,... | collective-permute-start | bytes 196616 | tf_op jit(solution)/shard_map/ppermute | solution.py:575
  15.7 3.5 %collective-permute-start.4 = (f32[1,4,8,128]{3,2,1,0:T(8,128)S(1)}, f32[1,4,8,128]{3,2,1,0:T(8,128)S(1)}, u32[]{:S(2)}, u32[]{:S(2)}) collective-permute-start(f32[1,4,8,128]{3,2,1,0:T(8,128)S(1)} %get-tuple-element.51), channel_id=1, source_target_pairs={{0,1},{1,0},{2,3},{3,2},{4,5},{5,4},{6,7},{7,6},{8,9},{9,8},{10,11... | collective-permute-start | bytes 49160 | tf_op jit(solution)/shard_map/ppermute | solution.py:575
  19.2 4.2 %collective-permute-start.5 = (f32[2,4,8,128]{3,2,1,0:T(8,128)S(1)}, f32[2,4,8,128]{3,2,1,0:T(8,128)S(1)}, u32[]{:S(2)}, u32[]{:S(2)}) collective-permute-start(f32[2,4,8,128]{3,2,1,0:T(8,128)S(1)} %get-tuple-element.80), channel_id=1, source_target_pairs={{0,2},{1,3},{2,0},{3,1},{4,6},{5,7},{6,4},{7,5},{8,10},{9,11},{10,... | collective-permute-start | bytes 98312 | tf_op jit(solution)/shard_map/ppermute | solution.py:575
  22.2 3.9 %collective-permute-start.9 = (f32[4,2,4,8,128]{4,3,2,1,0:T(8,128)S(1)}, f32[4,2,4,8,128]{4,3,2,1,0:T(8,128)S(1)}, u32[]{:S(2)}, u32[]{:S(2)}) collective-permute-start(f32[4,2,4,8,128]{4,3,2,1,0:T(8,128)S(1)} %pad_maximum_fusion), channel_id=1, source_target_pairs={{0,8},{1,9},{2,10},{3,11},{4,12},{5,13},{6,14},{7,15},{8,0},{9,1},... | collective-permute-start | bytes 393224 | tf_op jit(solution)/shard_map/ppermute | solution.py:575
  23.4 5.7 %collective-permute-start.6 = (f32[4,4,8,128]{3,2,1,0:T(8,128)S(1)}, f32[4,4,8,128]{3,2,1,0:T(8,128)S(1)}, u32[]{:S(2)}, u32[]{:S(2)}) collective-permute-start(f32[4,4,8,128]{3,2,1,0:T(8,128)S(1)} %pad_maximum_fusion.2), channel_id=1, source_target_pairs={{0,8},{1,9},{2,10},{3,11},{4,12},{5,13},{6,14},{7,15},{8,0},{9,1},... | collective-permute-start | bytes 196616 | tf_op jit(solution)/shard_map/ppermute | solution.py:575
  26.1 4.2 %collective-permute-start.10 = (f32[8,2,4,8,128]{4,3,2,1,0:T(8,128)S(1)}, f32[8,2,4,8,128]{4,3,2,1,0:T(8,128)S(1)}, u32[]{:S(2)}, u32[]{:S(2)}) collective-permute-start(f32[8,2,4,8,128]{4,3,2,1,0:T(8,128)S(1)} %constant_dynamic-update-slice_fusion.6.near), channel_id=1, source_target_pairs={{0,4},{1,5},{2,6},{3,7},{4,0},{5,1},{6,2},{7,3},{8,12},{9,13},{10,... | collective-permute-start | bytes 786440 | tf_op jit(solution)/shard_map/ppermute | solution.py:575
  29.1 3.0 %collective-permute-start.7 = (f32[8,4,8,128]{3,2,1,0:T(8,128)S(1)}, f32[8,4,8,128]{3,2,1,0:T(8,128)S(1)}, u32[]{:S(2)}, u32[]{:S(2)}) collective-permute-start(f32[8,4,8,128]{3,2,1,0:T(8,128)S(1)} %constant_dynamic-update-slice_fusion.2.near), channel_id=1, source_target_pairs={{0,4},{1,5},{2,6},{3,7},{4,0},{5,1},{6,2},{7,3},{8,12},{9,13},{10,... | collective-permute-start | bytes 393224 | tf_op jit(solution)/shard_map/ppermute | solution.py:575

commit v6 on v5

--- a/solution.py
+++ b/solution.py
@@ -11,6 +11,7 @@
 COARSE_ITERS = 20
 RIM = 4
 LANES = 128
+RIM_PLANES = ((0, RIM), (RIM, RIM), (2 * RIM, RIM - 1), (3 * RIM - 1, RIM - 1))
 VMEM = pl.BlockSpec(memory_space=pltpu.VMEM)
 HBM = pl.BlockSpec(memory_space=pltpu.HBM)
 
@@ -123,9 +124,10 @@
             out[field, :, length : length + 2 * RIM, :] = jnp.where(row < RIM, h, l)
         for slot in range(2):
             field = 2 * pair + slot
-            lo_x, hi_x = out[field, 0:RIM], out[field, planes - RIM : planes]
-            out_a[field] = jnp.where(even_x, hi_x, lo_x)
-            out_b[field] = jnp.where(even_x, lo_x, hi_x)
+            at, n = RIM_PLANES[field]
+            lo_x, hi_x = out[field, 0:n], out[field, planes - n : planes]
+            out_a[at : at + n] = jnp.where(even_x, hi_x, lo_x)
+            out_b[at : at + n] = jnp.where(even_x, lo_x, hi_x)
 
 
 W_P, GX, GY, GZ, W_N, XP, XM, YP, YM, ZP, ZM, WF_P, WF_N, U_P, U_N = range(15)
@@ -157,9 +159,19 @@
         fld[EPS, i], fld[MOB, i], fld[POT, i], fld[CAP, i] = eps, mob, pot, cap
         fld[F_P, i], fld[F_N, i] = fp, fn
 
+    def rim(i, ref_even, ref_odd, skip, outside):
+        values = []
+        for f, (at, n) in enumerate(RIM_PLANES):
+            if n < RIM and i == skip:
+                values.append(jnp.zeros((rows, LANES), jnp.float32))
+                continue
+            k = at + i - (1 if n < RIM and skip == 0 else 0)
+            v = jnp.where(even, ref_even[k], ref_odd[k])
+            values.append(jnp.where(outside, -1.0 if f == 0 else 0.0, v))
+        return values
+
     def low(i, _):
-        v = [jnp.where(even, in_b[f, i], in_a[f, i]) for f in range(4)]
-        materials(i, *[jnp.where(x == 0, -1.0 if f == 0 else 0.0, v[f]) for f in range(4)])
+        materials(i, *rim(i, in_b, in_a, 0, x == 0))
         return 0
 
     def middle(i, _):
@@ -167,11 +179,7 @@
         return 0
 
     def high(i, _):
-        v = [jnp.where(even, in_a[f, i], in_b[f, i]) for f in range(4)]
-        materials(
-            i + RIM + planes,
-            *[jnp.where(x == nx - 1, -1.0 if f == 0 else 0.0, v[f]) for f in range(4)],
-        )
+        materials(i + RIM + planes, *rim(i, in_a, in_b, RIM - 1, x == nx - 1))
         return 0
 
     loop(0, RIM, low, 0)
@@ -605,7 +613,7 @@
     fields_y = [fields, a[2 * planes :].reshape(fields.shape)]
     mid, a, b = pl.pallas_call(
         rim_x_kernel,
-        out_shape=[shape(4, planes, rows, LANES)] + [shape(4, RIM, rows, LANES)] * 2,
+        out_shape=[shape(4, planes, rows, LANES)] + [shape(4 * RIM - 2, rows, LANES)] * 2,
         in_specs=[VMEM] * 6,
         out_specs=[VMEM] * 3,
         compiler_params=params(16),

time: 36.5 us -> 36.2 us (level)
  transfers between devices with their start and end apart: 11 -> 11, of which waited for: 7 -> 6; matrix products, arithmetic and copies ran while one was open for 0% -> 0% of each run, Pallas kernels for 10% -> 10%
where the time goes in v6:
time: 36.2 us; the launch traced here: 35.7 us
  starting transfers between devices  20.2 us (56%)
  Pallas kernels  8.59 us (24%)
  waiting for transfers between devices  5.42 us (15%)
  other arithmetic  0.73 us (2%)
  between operations  0.7 us (2%)
    ppermute x11, starting transfers between devices, permute(): return lax.ppermute(v, ('groups', 'gx', 'gy'), send[name])  20.2 us
    ppermute x11, waiting for transfers between devices, permute(): return lax.ppermute(v, ('groups', 'gx', 'gy'), send[name])  5.42 us
    pallas_call x1, Pallas kernels, per_device(): pl.pallas_call(functools.partial(second_kernel, tuple(bits)), out_shape=[...  3.8 us
    pallas_call x1, Pallas kernels, per_device(): pl.pallas_call(functools.partial(operators_kernel, tuple(bits)), out_shap...  1.87 us
    pallas_call x1, Pallas kernels, per_device(): pl.pallas_call(first_kernel, out_shape=[shape(KEPT, total, rows, LANES),...  1.61 us
    pallas_call x1, Pallas kernels, per_device(): pl.pallas_call(rim_y_kernel, out_shape=[shape(2 * planes, by, LANES), sha...  1.24 us
  transfers between devices with their start and end apart: 11, of which 6 were waited for; matrix products, arithmetic and copies ran while one was open for 0% of the time, Pallas kernels for 10%

profile of v6, /device:TPU:1, one launch (start us, length us, event | category | flops | bytes accessed | tf_op | source)
XLA Modules:
  0.0 35.7 jit_solution(17162905146959024962)
XLA Ops:
  0.6 0.7 %pad_maximum_fusion.4 = f32[3,6]{1,0:T(4,128)S(1)} fusion(f32[1,6]{1,0:T(1,128)} %bitcast.7, f32[1,6]{1,0:T(1,128)} %bitcast.8, f32[1,6]{1,0:T(1,128)} %bitcast.9), kind=kLoop, calls=%fused_computation.13 | loop fusion | flops 36 | bytes 144 | tf_op jit(solution)/shard_map/stack | solution.py:591
  1.3 0.1 broadcast_in_dim.2.table
  1.4 1.2 %shard_map.86 = (f32[16,8,128]{2,1,0:T(8,128)S(1)}, f32[16,8,128]{2,1,0:T(8,128)S(1)}, f32[1,2,4,8,128]{4,3,2,1,0:T(8,128)S(1)}, f32[8,16,128]{2,1,0:T(8,128)S(1...) custom-call(f32[3,6,128]{2,1,0:T(8,128)S(1)} %broadcast_in_dim.2.table, ...), custom_call_target="tpu_custom_call" | custom-call | tf_op jit(solution)/shard_map/pallas_call | solution.py:594
  2.7 2.2 %collective-permute-start = (f32[24,8,128]{2,1,0:T(8,128)S(1)}, f32[24,8,128]{2,1,0:T(8,128)S(1)}, u32[]{:S(2)}, u32[]{:S(2)}) collective-permute-start(f32[24,8,128]{2,1,0:T(8,128)S(1)} %pad_maximum_fusion.1), channel_id=1, source_target_pairs={{0,1},{1,0},{2,3},{3,2},{4,5},{5,4},{6,7},{7,6},{8,9},{9,8},{10,11... | collective-permute-start | bytes 294920 | tf_op jit(solution)/shard_map/ppermute | solution.py:583
  4.9 1.0 %collective-permute-start.1 = (f32[16,8,128]{2,1,0:T(8,128)S(1)}, f32[16,8,128]{2,1,0:T(8,128)S(1)}, u32[]{:S(2)}, u32[]{:S(2)}) collective-permute-start(f32[16,8,128]{2,1,0:T(8,128)S(1)} %get-tuple-element.47), channel_id=1, source_target_pairs={{0,4},{1,2},{2,1},{3,7},{4,0},{5,6},{6,5},{7,3},{8,12},{9,10},{10,... | collective-permute-start | bytes 196616 | tf_op jit(solution)/shard_map/ppermute | solution.py:583
  5.8 0.9 %collective-permute-done.1.in_b = f32[16,8,128]{2,1,0:T(8,128)S(1)} collective-permute-done((f32[16,8,128]{2,1,0:T(8,128)S(1)}, f32[16,8,128]{2,1,0:T(8,128)S(1)}, u32[]{:S(2)}, u32[]{:S(2)}) %collective-permute-start.1) | collective-permute-done | bytes 65568 | tf_op jit(solution)/shard_map/ppermute | solution.py:583
  6.7 0.7 %collective-permute-done.in_a = f32[24,8,128]{2,1,0:T(8,128)S(1)} collective-permute-done((f32[24,8,128]{2,1,0:T(8,128)S(1)}, f32[24,8,128]{2,1,0:T(8,128)S(1)}, u32[]{:S(2)}, u32[]{:S(2)}) %collective-permute-start) | collective-permute-done | bytes 98336 | tf_op jit(solution)/shard_map/ppermute | solution.py:583
  7.4 0.1 shard_map.87
  7.4 1.3 %collective-permute-start.2 = (f32[14,24,128]{2,1,0:T(8,128)S(1)}, f32[14,24,128]{2,1,0:T(8,128)S(1)}, u32[]{:S(2)}, u32[]{:S(2)}) collective-permute-start(f32[14,24,128]{2,1,0:T(8,128)S(1)} %get-tuple-element.49), channel_id=1, source_target_pairs={{0,4},{1,5},{2,6},{3,7},{4,0},{5,1},{6,2},{7,3},{8,12},{9,13},{10,... | collective-permute-start | bytes 516104 | tf_op jit(solution)/shard_map/ppermute | solution.py:583
  8.7 1.4 %collective-permute-start.3 = (f32[14,24,128]{2,1,0:T(8,128)S(1)}, f32[14,24,128]{2,1,0:T(8,128)S(1)}, u32[]{:S(2)}, u32[]{:S(2)}) collective-permute-start(f32[14,24,128]{2,1,0:T(8,128)S(1)} %get-tuple-element.50), channel_id=1, source_target_pairs={{0,16},{1,17},{2,18},{3,19},{4,8},{5,9},{6,10},{7,11},{8,4},{9,5},... | collective-permute-start | bytes 516104 | tf_op jit(solution)/shard_map/ppermute | solution.py:583
  10.2 3.6 %collective-permute-start.8 = (f32[2,2,4,8,128]{4,3,2,1,0:T(8,128)S(1)}, f32[2,2,4,8,128]{4,3,2,1,0:T(8,128)S(1)}, u32[]{:S(2)}, u32[]{:S(2)}) collective-permute-start(f32[2,2,4,8,128]{4,3,2,1,0:T(8,128)S(1)} %pad_maximum_fusion.3), channel_id=1, source_target_pairs={{0,2},{1,3},{2,0},{3,1},{4,6},{5,7},{6,4},{7,5},{8,10},{9,11},{10,... | collective-permute-start | bytes 196616 | tf_op jit(solution)/shard_map/ppermute | solution.py:583
  13.8 0.0 collective-permute-done.2.in_a
  13.8 0.0 collective-permute-done.3.in_b
  13.8 1.6 %shard_map.88 = (f32[15,16,24,128]{3,2,1,0:T(8,128)S(1)}, f32[1,4,8,128]{3,2,1,0:T(8,128)S(1)}) custom-call(f32[3,6,128]{2,1,0:T(8,128)S(1)} %broadcast_in_dim.2.table, f32[4,8,24,128]{3,2,1,0:T(8,128)S(1)} %get-tuple-element.48.mid, f32[14,24,128]{2,1,0:T(8,128)S(1)} %collective-permute-done.2.in_a, f32[14,24,128]{2,1,0:T(8,128)S(1)} %collective-permute-done.3.in_b), custom_call_target="tpu_custom_call" | custom-call | tf_op jit(solution)/shard_map/pallas_call | solution.py:624
  15.4 2.4 %collective-permute-start.4 = (f32[1,4,8,128]{3,2,1,0:T(8,128)S(1)}, f32[1,4,8,128]{3,2,1,0:T(8,128)S(1)}, u32[]{:S(2)}, u32[]{:S(2)}) collective-permute-start(f32[1,4,8,128]{3,2,1,0:T(8,128)S(1)} %get-tuple-element.51), channel_id=1, source_target_pairs={{0,1},{1,0},{2,3},{3,2},{4,5},{5,4},{6,7},{7,6},{8,9},{9,8},{10,11... | collective-permute-start | bytes 49160 | tf_op jit(solution)/shard_map/ppermute | solution.py:583
  17.8 1.1 %collective-permute-done.4 = f32[1,4,8,128]{3,2,1,0:T(8,128)S(1)} collective-permute-done((f32[1,4,8,128]{3,2,1,0:T(8,128)S(1)}, f32[1,4,8,128]{3,2,1,0:T(8,128)S(1)}, u32[]{:S(2)}, u32[]{:S(2)}) %collective-permute-start.4) | collective-permute-done | bytes 16416 | tf_op jit(solution)/shard_map/ppermute | solution.py:583
  19.0 2.9 %collective-permute-start.5 = (f32[2,4,8,128]{3,2,1,0:T(8,128)S(1)}, f32[2,4,8,128]{3,2,1,0:T(8,128)S(1)}, u32[]{:S(2)}, u32[]{:S(2)}) collective-permute-start(f32[2,4,8,128]{3,2,1,0:T(8,128)S(1)} %get-tuple-element.80), channel_id=1, source_target_pairs={{0,2},{1,3},{2,0},{3,1},{4,6},{5,7},{6,4},{7,5},{8,10},{9,11},{10,... | collective-permute-start | bytes 98312 | tf_op jit(solution)/shard_map/ppermute | solution.py:583
  21.9 0.0 collective-permute-done.8
  21.9 0.7 %collective-permute-start.9 = (f32[4,2,4,8,128]{4,3,2,1,0:T(8,128)S(1)}, f32[4,2,4,8,128]{4,3,2,1,0:T(8,128)S(1)}, u32[]{:S(2)}, u32[]{:S(2)}) collective-permute-start(f32[4,2,4,8,128]{4,3,2,1,0:T(8,128)S(1)} %pad_maximum_fusion), channel_id=1, source_target_pairs={{0,8},{1,9},{2,10},{3,11},{4,12},{5,13},{6,14},{7,15},{8,0},{9,1},... | collective-permute-start | bytes 393224 | tf_op jit(solution)/shard_map/ppermute | solution.py:583
  22.6 0.6 %collective-permute-done.5 = f32[2,4,8,128]{3,2,1,0:T(8,128)S(1)} collective-permute-done((f32[2,4,8,128]{3,2,1,0:T(8,128)S(1)}, f32[2,4,8,128]{3,2,1,0:T(8,128)S(1)}, u32[]{:S(2)}, u32[]{:S(2)}) %collective-permute-start.5) | collective-permute-done | bytes 32800 | tf_op jit(solution)/shard_map/ppermute | solution.py:583
  23.2 0.6 %collective-permute-start.6 = (f32[4,4,8,128]{3,2,1,0:T(8,128)S(1)}, f32[4,4,8,128]{3,2,1,0:T(8,128)S(1)}, u32[]{:S(2)}, u32[]{:S(2)}) collective-permute-start(f32[4,4,8,128]{3,2,1,0:T(8,128)S(1)} %pad_maximum_fusion.2), channel_id=1, source_target_pairs={{0,8},{1,9},{2,10},{3,11},{4,12},{5,13},{6,14},{7,15},{8,0},{9,1},... | collective-permute-start | bytes 196616 | tf_op jit(solution)/shard_map/ppermute | solution.py:583
  23.8 2.0 %collective-permute-done.9 = f32[4,2,4,8,128]{4,3,2,1,0:T(8,128)S(1)} collective-permute-done((f32[4,2,4,8,128]{4,3,2,1,0:T(8,128)S(1)}, f32[4,2,4,8,128]{4,3,2,1,0:T(8,128)S(1)}, u32[]{:S(2)}, u32[]{:S(2)}) %collective-permute-start.9) | collective-permute-done | bytes 131104 | tf_op jit(solution)/shard_map/ppermute | solution.py:583
  25.8 3.0 %collective-permute-start.10 = (f32[8,2,4,8,128]{4,3,2,1,0:T(8,128)S(1)}, f32[8,2,4,8,128]{4,3,2,1,0:T(8,128)S(1)}, u32[]{:S(2)}, u32[]{:S(2)}) collective-permute-start(f32[8,2,4,8,128]{4,3,2,1,0:T(8,128)S(1)} %constant_dynamic-update-slice_fusion.6.near), channel_id=1, source_target_pairs={{0,4},{1,5},{2,6},{3,7},{4,0},{5,1},{6,2},{7,3},{8,12},{9,13},{10,... | collective-permute-start | bytes 786440 | tf_op jit(solution)/shard_map/ppermute | solution.py:583
  28.8 0.0 collective-permute-done.6
  28.9 1.0 %collective-permute-start.7 = (f32[8,4,8,128]{3,2,1,0:T(8,128)S(1)}, f32[8,4,8,128]{3,2,1,0:T(8,128)S(1)}, u32[]{:S(2)}, u32[]{:S(2)}) collective-permute-start(f32[8,4,8,128]{3,2,1,0:T(8,128)S(1)} %constant_dynamic-update-slice_fusion.2.near), channel_id=1, source_target_pairs={{0,4},{1,5},{2,6},{3,7},{4,0},{5,1},{6,2},{7,3},{8,12},{9,13},{10,... | collective-permute-start | bytes 393224 | tf_op jit(solution)/shard_map/ppermute | solution.py:583
  29.9 0.1 collective-permute-done.10.far
  30.0 1.9 %shard_map.89 = (f32[17,32,128]{2,1,0:T(8,128)S(1)}, f32[17,32,128]{2,1,0:T(8,128)S(1)}, f32[16,32,128]{2,1,0:T(8,128)S(1)}, f32[16,32,128]{2,1,0:T(8,128)S(1)},...) custom-call(f32[8,2,4,8,128]{4,3,2,1,0:T(8,128)S(1)} %constant_dynam, ...), custom_call_target="tpu_custom_call" | custom-call | tf_op jit(solution)/shard_map/pallas_call | solution.py:656
  31.9 0.0 collective-permute-done.7.far
  31.9 3.8 %shard_map.90 = (f32[8,16,128]{2,1,0:T(8,128)}, f32[8,16,128]{2,1,0:T(8,128)}) custom-call(f32[8,4,8,128]{3,2,1,0:T(8,128)S(1)} %constant_dynamic-update-slice_fusion.2.near, f32[8,4,8,128]{3,2,1,0:T(8,128)S(1)} %collective-permute-done.7.far, f32[15,16,24,128]{3,2,1,0:T(8,128)S(1)} %get-tuple-element.52.kept, f32[17,32,128]{2,1,0:T(8,128)S(1)} %get-tuple-element.56.refs_0_, ...), custom_call_target="tpu_custom_call" | custom-call | tf_op jit(solution)/shard_map/pallas_call | solution.py:666
  (12 shorter events, 0.1 us)
Async XLA Ops:
  2.7 4.7 %collective-permute-start = (f32[24,8,128]{2,1,0:T(8,128)S(1)}, f32[24,8,128]{2,1,0:T(8,128)S(1)}, u32[]{:S(2)}, u32[]{:S(2)}) collective-permute-start(f32[24,8,128]{2,1,0:T(8,128)S(1)} %pad_maximum_fusion.1), channel_id=1, source_target_pairs={{0,1},{1,0},{2,3},{3,2},{4,5},{5,4},{6,7},{7,6},{8,9},{9,8},{10,11... | collective-permute-start | bytes 294920 | tf_op jit(solution)/shard_map/ppermute | solution.py:583
  4.9 1.9 %collective-permute-start.1 = (f32[16,8,128]{2,1,0:T(8,128)S(1)}, f32[16,8,128]{2,1,0:T(8,128)S(1)}, u32[]{:S(2)}, u32[]{:S(2)}) collective-permute-start(f32[16,8,128]{2,1,0:T(8,128)S(1)} %get-tuple-element.47), channel_id=1, source_target_pairs={{0,4},{1,2},{2,1},{3,7},{4,0},{5,6},{6,5},{7,3},{8,12},{9,10},{10,... | collective-permute-start | bytes 196616 | tf_op jit(solution)/shard_map/ppermute | solution.py:583
  7.4 6.3 %collective-permute-start.2 = (f32[14,24,128]{2,1,0:T(8,128)S(1)}, f32[14,24,128]{2,1,0:T(8,128)S(1)}, u32[]{:S(2)}, u32[]{:S(2)}) collective-permute-start(f32[14,24,128]{2,1,0:T(8,128)S(1)} %get-tuple-element.49), channel_id=1, source_target_pairs={{0,4},{1,5},{2,6},{3,7},{4,0},{5,1},{6,2},{7,3},{8,12},{9,13},{10,... | collective-permute-start | bytes 516104 | tf_op jit(solution)/shard_map/ppermute | solution.py:583
  8.7 5.1 %collective-permute-start.3 = (f32[14,24,128]{2,1,0:T(8,128)S(1)}, f32[14,24,128]{2,1,0:T(8,128)S(1)}, u32[]{:S(2)}, u32[]{:S(2)}) collective-permute-start(f32[14,24,128]{2,1,0:T(8,128)S(1)} %get-tuple-element.50), channel_id=1, source_target_pairs={{0,16},{1,17},{2,18},{3,19},{4,8},{5,9},{6,10},{7,11},{8,4},{9,5},... | collective-permute-start | bytes 516104 | tf_op jit(solution)/shard_map/ppermute | solution.py:583
  10.2 11.7 %collective-permute-start.8 = (f32[2,2,4,8,128]{4,3,2,1,0:T(8,128)S(1)}, f32[2,2,4,8,128]{4,3,2,1,0:T(8,128)S(1)}, u32[]{:S(2)}, u32[]{:S(2)}) collective-permute-start(f32[2,2,4,8,128]{4,3,2,1,0:T(8,128)S(1)} %pad_maximum_fusion.3), channel_id=1, source_target_pairs={{0,2},{1,3},{2,0},{3,1},{4,6},{5,7},{6,4},{7,5},{8,10},{9,11},{10,... | collective-permute-start | bytes 196616 | tf_op jit(solution)/shard_map/ppermute | solution.py:583
  15.4 3.5 %collective-permute-start.4 = (f32[1,4,8,128]{3,2,1,0:T(8,128)S(1)}, f32[1,4,8,128]{3,2,1,0:T(8,128)S(1)}, u32[]{:S(2)}, u32[]{:S(2)}) collective-permute-start(f32[1,4,8,128]{3,2,1,0:T(8,128)S(1)} %get-tuple-element.51), channel_id=1, source_target_pairs={{0,1},{1,0},{2,3},{3,2},{4,5},{5,4},{6,7},{7,6},{8,9},{9,8},{10,11... | collective-permute-start | bytes 49160 | tf_op jit(solution)/shard_map/ppermute | solution.py:583
  19.0 4.2 %collective-permute-start.5 = (f32[2,4,8,128]{3,2,1,0:T(8,128)S(1)}, f32[2,4,8,128]{3,2,1,0:T(8,128)S(1)}, u32[]{:S(2)}, u32[]{:S(2)}) collective-permute-start(f32[2,4,8,128]{3,2,1,0:T(8,128)S(1)} %get-tuple-element.80), channel_id=1, source_target_pairs={{0,2},{1,3},{2,0},{3,1},{4,6},{5,7},{6,4},{7,5},{8,10},{9,11},{10,... | collective-permute-start | bytes 98312 | tf_op jit(solution)/shard_map/ppermute | solution.py:583
  21.9 3.9 %collective-permute-start.9 = (f32[4,2,4,8,128]{4,3,2,1,0:T(8,128)S(1)}, f32[4,2,4,8,128]{4,3,2,1,0:T(8,128)S(1)}, u32[]{:S(2)}, u32[]{:S(2)}) collective-permute-start(f32[4,2,4,8,128]{4,3,2,1,0:T(8,128)S(1)} %pad_maximum_fusion), channel_id=1, source_target_pairs={{0,8},{1,9},{2,10},{3,11},{4,12},{5,13},{6,14},{7,15},{8,0},{9,1},... | collective-permute-start | bytes 393224 | tf_op jit(solution)/shard_map/ppermute | solution.py:583
  23.2 5.7 %collective-permute-start.6 = (f32[4,4,8,128]{3,2,1,0:T(8,128)S(1)}, f32[4,4,8,128]{3,2,1,0:T(8,128)S(1)}, u32[]{:S(2)}, u32[]{:S(2)}) collective-permute-start(f32[4,4,8,128]{3,2,1,0:T(8,128)S(1)} %pad_maximum_fusion.2), channel_id=1, source_target_pairs={{0,8},{1,9},{2,10},{3,11},{4,12},{5,13},{6,14},{7,15},{8,0},{9,1},... | collective-permute-start | bytes 196616 | tf_op jit(solution)/shard_map/ppermute | solution.py:583
  25.8 4.2 %collective-permute-start.10 = (f32[8,2,4,8,128]{4,3,2,1,0:T(8,128)S(1)}, f32[8,2,4,8,128]{4,3,2,1,0:T(8,128)S(1)}, u32[]{:S(2)}, u32[]{:S(2)}) collective-permute-start(f32[8,2,4,8,128]{4,3,2,1,0:T(8,128)S(1)} %constant_dynamic-update-slice_fusion.6.near), channel_id=1, source_target_pairs={{0,4},{1,5},{2,6},{3,7},{4,0},{5,1},{6,2},{7,3},{8,12},{9,13},{10,... | collective-permute-start | bytes 786440 | tf_op jit(solution)/shard_map/ppermute | solution.py:583
  28.9 3.0 %collective-permute-start.7 = (f32[8,4,8,128]{3,2,1,0:T(8,128)S(1)}, f32[8,4,8,128]{3,2,1,0:T(8,128)S(1)}, u32[]{:S(2)}, u32[]{:S(2)}) collective-permute-start(f32[8,4,8,128]{3,2,1,0:T(8,128)S(1)} %constant_dynamic-update-slice_fusion.2.near), channel_id=1, source_target_pairs={{0,4},{1,5},{2,6},{3,7},{4,0},{5,1},{6,2},{7,3},{8,12},{9,13},{10,... | collective-permute-start | bytes 393224 | tf_op jit(solution)/shard_map/ppermute | solution.py:583

commit v7 on v6

--- a/solution.py
+++ b/solution.py
@@ -428,7 +428,7 @@
         lv.u[i + 1] = u[i]
 
 
-def place(bits, ref, flip, x, y, ny, put):
+def place(bits, y_bits, ref, flip, x, y, ny, put):
     bx, by = ref.shape[-3], ref.shape[-2]
 
     def body(m, _):
@@ -436,7 +436,10 @@
         to_x = x ^ flip
         for k, bit in enumerate(bits[:-1]):
             to_x = to_x ^ (((b >> k) & 1) * bit)
-        row = pl.ds(pl.multiple_of((y ^ (m % ny)) * by, by), by)
+        to_y = y
+        for k, bit in enumerate(y_bits):
+            to_y = to_y ^ (((m >> k) & 1) * bit)
+        row = pl.ds(pl.multiple_of(to_y * by, by), by)
         for i in range(bx):
             put(m, i, to_x * bx + i, row)
         return 0
@@ -444,7 +447,7 @@
     loop(0, ref.shape[0], body, 0)
 
 
-def operators_kernel(bits, near, far, *refs):
+def operators_kernel(bits, y_bits, near, far, *refs):
     x, y, ny = lax.axis_index("gx"), lax.axis_index("gy"), lax.axis_size("gy")
     outs, scratch = refs[: 3 * OPERATOR], refs[3 * OPERATOR :]
     l1, l2, l3 = (
@@ -460,7 +463,7 @@
             l1.pot[at, row, :] = jnp.where(right, q, 0.0)
             l1.cap[at, row, :] = jnp.where(right, down(q, LANES // 2, 1), 0.0)
 
-        place(bits, ref, flip, x, y, ny, put)
+        place(bits, y_bits, ref, flip, x, y, ny, put)
     l1.assemble()
     l1.descend_fields(l2, tmp)
     l2.assemble()
@@ -468,7 +471,7 @@
     l3.assemble()
 
 
-def second_kernel(bits, near, far, kept, *refs):
+def second_kernel(bits, y_bits, near, far, kept, *refs):
     x, y, ny = lax.axis_index("gx"), lax.axis_index("gy"), lax.axis_size("gy")
     given, (out_p, out_n), scratch = refs[: 3 * OPERATOR], refs[3 * OPERATOR : 3 * OPERATOR + 2], refs[3 * OPERATOR + 2 :]
     l1, l2, l3 = (
@@ -481,7 +484,7 @@
         def put(m, i, at, row, ref=ref):
             l1.f[at, row, :] = ref[m, i]
 
-        place(bits, ref, flip, x, y, ny, put)
+        place(bits, y_bits, ref, flip, x, y, ny, put)
     for here, there in ((l1, l2), (l2, l3)):
         here.start()
         here.sweep(here.u, here.v)
@@ -635,11 +638,9 @@
 
     bits = [1 << k for k in reversed(range((nx - 1).bit_length()))]
 
-    def over_y(near, first):
-        bit = first
-        while bit < ny:
+    def over_y(near, line):
+        for bit in line:
             near = jnp.concatenate([near, permute(near, ("y", bit))])
-            bit *= 2
         return near
 
     def over_x(near):
@@ -648,13 +649,15 @@
         return near, permute(near, ("x", bits[-1]))
 
     halves = [fields_y, permute(fields_y, ("y", 2))]
-    pair = jnp.concatenate([block, permute(block, ("y", 1))])
+    y_bits = tuple(1 << k for k in range((ny - 1).bit_length()))
+    y_turn = (2, 1) + y_bits[2:]
+    pair = jnp.concatenate([block, permute(block, ("y", 2))])
     halves, _ = lax.optimization_barrier((halves, pair))
-    fields_y = over_y(jnp.concatenate(halves), 4)
+    fields_y = over_y(jnp.concatenate(halves), y_bits[2:])
     grids = [(bx * nx >> level, by * ny >> level) for level in range(3)]
     large = grids[0][0] * grids[0][1] > 1024
     operators = pl.pallas_call(
-        functools.partial(operators_kernel, tuple(bits)),
+        functools.partial(operators_kernel, tuple(bits), y_bits),
         out_shape=[shape(*s) for g in grids for s in Level.operator(*g)],
         in_specs=[VMEM] * 2,
         out_specs=[VMEM] * (3 * OPERATOR),
@@ -662,9 +665,9 @@
         + [pltpu.VMEM((grids[0][1], LANES), f32)],
         compiler_params=params(60 if large else 16),
     )(*over_x(fields_y))
-    near, far = over_x(over_y(pair, 2))
+    near, far = over_x(over_y(pair, y_turn[1:]))
     return pl.pallas_call(
-        functools.partial(second_kernel, tuple(bits)),
+        functools.partial(second_kernel, tuple(bits), y_turn),
         out_shape=[shape(planes, own, LANES)] * 2,
         in_specs=[VMEM] * (3 + 3 * OPERATOR),
         out_specs=[VMEM] * 2,

time: 36.2 us -> 35.9 us (level)
  transfers between devices with their start and end apart: 11 -> 11, of which waited for: 6 -> 5; matrix products, arithmetic and copies ran while one was open for 0% -> 0% of each run, Pallas kernels for 10% -> 10%
where the time goes in v7:
time: 35.9 us; the launch traced here: 35.7 us
  starting transfers between devices  20.3 us (57%)
  Pallas kernels  8.59 us (24%)
  waiting for transfers between devices  5.33 us (15%)
  other arithmetic  0.73 us (2%)
  between operations  0.7 us (2%)
    ppermute x11, starting transfers between devices, permute(): return lax.ppermute(v, ('groups', 'gx', 'gy'), send[name])  20.3 us
    ppermute x11, waiting for transfers between devices, permute(): return lax.ppermute(v, ('groups', 'gx', 'gy'), send[name])  5.33 us
    pallas_call x1, Pallas kernels, per_device(): pl.pallas_call(functools.partial(second_kernel, tuple(bits), y_turn), out...  3.8 us
    pallas_call x1, Pallas kernels, per_device(): pl.pallas_call(functools.partial(operators_kernel, tuple(bits), y_bits),...  1.87 us
    pallas_call x1, Pallas kernels, per_device(): pl.pallas_call(first_kernel, out_shape=[shape(KEPT, total, rows, LANES),...  1.61 us
    pallas_call x1, Pallas kernels, per_device(): pl.pallas_call(rim_y_kernel, out_shape=[shape(2 * planes, by, LANES), sha...  1.24 us
  transfers between devices with their start and end apart: 11, of which 5 were waited for; matrix products, arithmetic and copies ran while one was open for 0% of the time, Pallas kernels for 10%

profile of v7, /device:TPU:1, one launch (start us, length us, event | category | flops | bytes accessed | tf_op | source)
XLA Modules:
  0.0 35.7 jit_solution(3528700450089220390)
XLA Ops:
  0.6 0.7 %pad_maximum_fusion.4 = f32[3,6]{1,0:T(4,128)S(1)} fusion(f32[1,6]{1,0:T(1,128)} %bitcast.7, f32[1,6]{1,0:T(1,128)} %bitcast.8, f32[1,6]{1,0:T(1,128)} %bitcast.9), kind=kLoop, calls=%fused_computation.13 | loop fusion | flops 36 | bytes 144 | tf_op jit(solution)/shard_map/stack | solution.py:594
  1.3 0.1 broadcast_in_dim.2.table
  1.4 1.2 %shard_map.86 = (f32[16,8,128]{2,1,0:T(8,128)S(1)}, f32[16,8,128]{2,1,0:T(8,128)S(1)}, f32[1,2,4,8,128]{4,3,2,1,0:T(8,128)S(1)}, f32[8,16,128]{2,1,0:T(8,128)S(1...) custom-call(f32[3,6,128]{2,1,0:T(8,128)S(1)} %broadcast_in_dim.2.table, ...), custom_call_target="tpu_custom_call" | custom-call | tf_op jit(solution)/shard_map/pallas_call | solution.py:597
  2.7 2.2 %collective-permute-start = (f32[24,8,128]{2,1,0:T(8,128)S(1)}, f32[24,8,128]{2,1,0:T(8,128)S(1)}, u32[]{:S(2)}, u32[]{:S(2)}) collective-permute-start(f32[24,8,128]{2,1,0:T(8,128)S(1)} %pad_maximum_fusion.1), channel_id=1, source_target_pairs={{0,1},{1,0},{2,3},{3,2},{4,5},{5,4},{6,7},{7,6},{8,9},{9,8},{10,11... | collective-permute-start | bytes 294920 | tf_op jit(solution)/shard_map/ppermute | solution.py:586
  4.9 1.0 %collective-permute-start.1 = (f32[16,8,128]{2,1,0:T(8,128)S(1)}, f32[16,8,128]{2,1,0:T(8,128)S(1)}, u32[]{:S(2)}, u32[]{:S(2)}) collective-permute-start(f32[16,8,128]{2,1,0:T(8,128)S(1)} %get-tuple-element.47), channel_id=1, source_target_pairs={{0,4},{1,2},{2,1},{3,7},{4,0},{5,6},{6,5},{7,3},{8,12},{9,10},{10,... | collective-permute-start | bytes 196616 | tf_op jit(solution)/shard_map/ppermute | solution.py:586
  5.8 0.9 %collective-permute-done.1.in_b = f32[16,8,128]{2,1,0:T(8,128)S(1)} collective-permute-done((f32[16,8,128]{2,1,0:T(8,128)S(1)}, f32[16,8,128]{2,1,0:T(8,128)S(1)}, u32[]{:S(2)}, u32[]{:S(2)}) %collective-permute-start.1) | collective-permute-done | bytes 65568 | tf_op jit(solution)/shard_map/ppermute | solution.py:586
  6.7 0.7 %collective-permute-done.in_a = f32[24,8,128]{2,1,0:T(8,128)S(1)} collective-permute-done((f32[24,8,128]{2,1,0:T(8,128)S(1)}, f32[24,8,128]{2,1,0:T(8,128)S(1)}, u32[]{:S(2)}, u32[]{:S(2)}) %collective-permute-start) | collective-permute-done | bytes 98336 | tf_op jit(solution)/shard_map/ppermute | solution.py:586
  7.4 0.1 shard_map.87
  7.4 1.3 %collective-permute-start.2 = (f32[14,24,128]{2,1,0:T(8,128)S(1)}, f32[14,24,128]{2,1,0:T(8,128)S(1)}, u32[]{:S(2)}, u32[]{:S(2)}) collective-permute-start(f32[14,24,128]{2,1,0:T(8,128)S(1)} %get-tuple-element.49), channel_id=1, source_target_pairs={{0,4},{1,5},{2,6},{3,7},{4,0},{5,1},{6,2},{7,3},{8,12},{9,13},{10,... | collective-permute-start | bytes 516104 | tf_op jit(solution)/shard_map/ppermute | solution.py:586
  8.7 1.4 %collective-permute-start.3 = (f32[14,24,128]{2,1,0:T(8,128)S(1)}, f32[14,24,128]{2,1,0:T(8,128)S(1)}, u32[]{:S(2)}, u32[]{:S(2)}) collective-permute-start(f32[14,24,128]{2,1,0:T(8,128)S(1)} %get-tuple-element.50), channel_id=1, source_target_pairs={{0,16},{1,17},{2,18},{3,19},{4,8},{5,9},{6,10},{7,11},{8,4},{9,5},... | collective-permute-start | bytes 516104 | tf_op jit(solution)/shard_map/ppermute | solution.py:586
  10.2 3.6 %collective-permute-start.8 = (f32[2,2,4,8,128]{4,3,2,1,0:T(8,128)S(1)}, f32[2,2,4,8,128]{4,3,2,1,0:T(8,128)S(1)}, u32[]{:S(2)}, u32[]{:S(2)}) collective-permute-start(f32[2,2,4,8,128]{4,3,2,1,0:T(8,128)S(1)} %pad_maximum_fusion.3), channel_id=1, source_target_pairs={{0,2},{1,3},{2,0},{3,1},{4,6},{5,7},{6,4},{7,5},{8,10},{9,11},{10,... | collective-permute-start | bytes 196616 | tf_op jit(solution)/shard_map/ppermute | solution.py:586
  13.8 0.0 collective-permute-done.2.in_a
  13.8 0.0 collective-permute-done.3.in_b
  13.8 1.6 %shard_map.88 = (f32[15,16,24,128]{3,2,1,0:T(8,128)S(1)}, f32[1,4,8,128]{3,2,1,0:T(8,128)S(1)}) custom-call(f32[3,6,128]{2,1,0:T(8,128)S(1)} %broadcast_in_dim.2.table, f32[4,8,24,128]{3,2,1,0:T(8,128)S(1)} %get-tuple-element.48.mid, f32[14,24,128]{2,1,0:T(8,128)S(1)} %collective-permute-done.2.in_a, f32[14,24,128]{2,1,0:T(8,128)S(1)} %collective-permute-done.3.in_b), custom_call_target="tpu_custom_call" | custom-call | tf_op jit(solution)/shard_map/pallas_call | solution.py:627
  15.4 3.8 %collective-permute-start.4 = (f32[1,4,8,128]{3,2,1,0:T(8,128)S(1)}, f32[1,4,8,128]{3,2,1,0:T(8,128)S(1)}, u32[]{:S(2)}, u32[]{:S(2)}) collective-permute-start(f32[1,4,8,128]{3,2,1,0:T(8,128)S(1)} %get-tuple-element.51), channel_id=1, source_target_pairs={{0,2},{1,3},{2,0},{3,1},{4,6},{5,7},{6,4},{7,5},{8,10},{9,11},{10,... | collective-permute-start | bytes 49160 | tf_op jit(solution)/shard_map/ppermute | solution.py:586
  19.3 1.1 %collective-permute-done.4 = f32[1,4,8,128]{3,2,1,0:T(8,128)S(1)} collective-permute-done((f32[1,4,8,128]{3,2,1,0:T(8,128)S(1)}, f32[1,4,8,128]{3,2,1,0:T(8,128)S(1)}, u32[]{:S(2)}, u32[]{:S(2)}) %collective-permute-start.4) | collective-permute-done | bytes 16416 | tf_op jit(solution)/shard_map/ppermute | solution.py:586
  20.4 1.0 %collective-permute-start.5 = (f32[2,4,8,128]{3,2,1,0:T(8,128)S(1)}, f32[2,4,8,128]{3,2,1,0:T(8,128)S(1)}, u32[]{:S(2)}, u32[]{:S(2)}) collective-permute-start(f32[2,4,8,128]{3,2,1,0:T(8,128)S(1)} %get-tuple-element.80), channel_id=1, source_target_pairs={{0,1},{1,0},{2,3},{3,2},{4,5},{5,4},{6,7},{7,6},{8,9},{9,8},{10,11... | collective-permute-start | bytes 98312 | tf_op jit(solution)/shard_map/ppermute | solution.py:586
  21.4 0.0 collective-permute-done.8
  21.4 0.7 %collective-permute-start.9 = (f32[4,2,4,8,128]{4,3,2,1,0:T(8,128)S(1)}, f32[4,2,4,8,128]{4,3,2,1,0:T(8,128)S(1)}, u32[]{:S(2)}, u32[]{:S(2)}) collective-permute-start(f32[4,2,4,8,128]{4,3,2,1,0:T(8,128)S(1)} %pad_maximum_fusion), channel_id=1, source_target_pairs={{0,8},{1,9},{2,10},{3,11},{4,12},{5,13},{6,14},{7,15},{8,0},{9,1},... | collective-permute-start | bytes 393224 | tf_op jit(solution)/shard_map/ppermute | solution.py:586
  22.2 1.0 %collective-permute-done.5 = f32[2,4,8,128]{3,2,1,0:T(8,128)S(1)} collective-permute-done((f32[2,4,8,128]{3,2,1,0:T(8,128)S(1)}, f32[2,4,8,128]{3,2,1,0:T(8,128)S(1)}, u32[]{:S(2)}, u32[]{:S(2)}) %collective-permute-start.5) | collective-permute-done | bytes 32800 | tf_op jit(solution)/shard_map/ppermute | solution.py:586
  23.2 0.6 %collective-permute-start.6 = (f32[4,4,8,128]{3,2,1,0:T(8,128)S(1)}, f32[4,4,8,128]{3,2,1,0:T(8,128)S(1)}, u32[]{:S(2)}, u32[]{:S(2)}) collective-permute-start(f32[4,4,8,128]{3,2,1,0:T(8,128)S(1)} %pad_maximum_fusion.2), channel_id=1, source_target_pairs={{0,8},{1,9},{2,10},{3,11},{4,12},{5,13},{6,14},{7,15},{8,0},{9,1},... | collective-permute-start | bytes 196616 | tf_op jit(solution)/shard_map/ppermute | solution.py:586
  23.8 1.6 %collective-permute-done.9 = f32[4,2,4,8,128]{4,3,2,1,0:T(8,128)S(1)} collective-permute-done((f32[4,2,4,8,128]{4,3,2,1,0:T(8,128)S(1)}, f32[4,2,4,8,128]{4,3,2,1,0:T(8,128)S(1)}, u32[]{:S(2)}, u32[]{:S(2)}) %collective-permute-start.9) | collective-permute-done | bytes 131104 | tf_op jit(solution)/shard_map/ppermute | solution.py:586
  25.4 3.1 %collective-permute-start.10 = (f32[8,2,4,8,128]{4,3,2,1,0:T(8,128)S(1)}, f32[8,2,4,8,128]{4,3,2,1,0:T(8,128)S(1)}, u32[]{:S(2)}, u32[]{:S(2)}) collective-permute-start(f32[8,2,4,8,128]{4,3,2,1,0:T(8,128)S(1)} %constant_dynamic-update-slice_fusion.6.near), channel_id=1, source_target_pairs={{0,4},{1,5},{2,6},{3,7},{4,0},{5,1},{6,2},{7,3},{8,12},{9,13},{10,... | collective-permute-start | bytes 786440 | tf_op jit(solution)/shard_map/ppermute | solution.py:586
  28.5 0.0 collective-permute-done.6
  28.5 1.6 %collective-permute-start.7 = (f32[8,4,8,128]{3,2,1,0:T(8,128)S(1)}, f32[8,4,8,128]{3,2,1,0:T(8,128)S(1)}, u32[]{:S(2)}, u32[]{:S(2)}) collective-permute-start(f32[8,4,8,128]{3,2,1,0:T(8,128)S(1)} %constant_dynamic-update-slice_fusion.2.near), channel_id=1, source_target_pairs={{0,4},{1,5},{2,6},{3,7},{4,0},{5,1},{6,2},{7,3},{8,12},{9,13},{10,... | collective-permute-start | bytes 393224 | tf_op jit(solution)/shard_map/ppermute | solution.py:586
  30.0 0.0 collective-permute-done.10.far
  30.1 1.9 %shard_map.89 = (f32[17,32,128]{2,1,0:T(8,128)S(1)}, f32[17,32,128]{2,1,0:T(8,128)S(1)}, f32[16,32,128]{2,1,0:T(8,128)S(1)}, f32[16,32,128]{2,1,0:T(8,128)S(1)},...) custom-call(f32[8,2,4,8,128]{4,3,2,1,0:T(8,128)S(1)} %constant_dynam, ...), custom_call_target="tpu_custom_call" | custom-call | tf_op jit(solution)/shard_map/pallas_call | solution.py:659
  31.9 0.0 collective-permute-done.7.far
  31.9 3.8 %shard_map.90 = (f32[8,16,128]{2,1,0:T(8,128)}, f32[8,16,128]{2,1,0:T(8,128)}) custom-call(f32[8,4,8,128]{3,2,1,0:T(8,128)S(1)} %constant_dynamic-update-slice_fusion.2.near, f32[8,4,8,128]{3,2,1,0:T(8,128)S(1)} %collective-permute-done.7.far, f32[15,16,24,128]{3,2,1,0:T(8,128)S(1)} %get-tuple-element.52.kept, f32[17,32,128]{2,1,0:T(8,128)S(1)} %get-tuple-element.56.refs_0_, ...), custom_call_target="tpu_custom_call" | custom-call | tf_op jit(solution)/shard_map/pallas_call | solution.py:669
  (12 shorter events, 0.1 us)
Async XLA Ops:
  2.7 4.7 %collective-permute-start = (f32[24,8,128]{2,1,0:T(8,128)S(1)}, f32[24,8,128]{2,1,0:T(8,128)S(1)}, u32[]{:S(2)}, u32[]{:S(2)}) collective-permute-start(f32[24,8,128]{2,1,0:T(8,128)S(1)} %pad_maximum_fusion.1), channel_id=1, source_target_pairs={{0,1},{1,0},{2,3},{3,2},{4,5},{5,4},{6,7},{7,6},{8,9},{9,8},{10,11... | collective-permute-start | bytes 294920 | tf_op jit(solution)/shard_map/ppermute | solution.py:586
  4.9 1.9 %collective-permute-start.1 = (f32[16,8,128]{2,1,0:T(8,128)S(1)}, f32[16,8,128]{2,1,0:T(8,128)S(1)}, u32[]{:S(2)}, u32[]{:S(2)}) collective-permute-start(f32[16,8,128]{2,1,0:T(8,128)S(1)} %get-tuple-element.47), channel_id=1, source_target_pairs={{0,4},{1,2},{2,1},{3,7},{4,0},{5,6},{6,5},{7,3},{8,12},{9,10},{10,... | collective-permute-start | bytes 196616 | tf_op jit(solution)/shard_map/ppermute | solution.py:586
  7.4 6.3 %collective-permute-start.2 = (f32[14,24,128]{2,1,0:T(8,128)S(1)}, f32[14,24,128]{2,1,0:T(8,128)S(1)}, u32[]{:S(2)}, u32[]{:S(2)}) collective-permute-start(f32[14,24,128]{2,1,0:T(8,128)S(1)} %get-tuple-element.49), channel_id=1, source_target_pairs={{0,4},{1,5},{2,6},{3,7},{4,0},{5,1},{6,2},{7,3},{8,12},{9,13},{10,... | collective-permute-start | bytes 516104 | tf_op jit(solution)/shard_map/ppermute | solution.py:586
  8.7 5.1 %collective-permute-start.3 = (f32[14,24,128]{2,1,0:T(8,128)S(1)}, f32[14,24,128]{2,1,0:T(8,128)S(1)}, u32[]{:S(2)}, u32[]{:S(2)}) collective-permute-start(f32[14,24,128]{2,1,0:T(8,128)S(1)} %get-tuple-element.50), channel_id=1, source_target_pairs={{0,16},{1,17},{2,18},{3,19},{4,8},{5,9},{6,10},{7,11},{8,4},{9,5},... | collective-permute-start | bytes 516104 | tf_op jit(solution)/shard_map/ppermute | solution.py:586
  10.2 11.2 %collective-permute-start.8 = (f32[2,2,4,8,128]{4,3,2,1,0:T(8,128)S(1)}, f32[2,2,4,8,128]{4,3,2,1,0:T(8,128)S(1)}, u32[]{:S(2)}, u32[]{:S(2)}) collective-permute-start(f32[2,2,4,8,128]{4,3,2,1,0:T(8,128)S(1)} %pad_maximum_fusion.3), channel_id=1, source_target_pairs={{0,2},{1,3},{2,0},{3,1},{4,6},{5,7},{6,4},{7,5},{8,10},{9,11},{10,... | collective-permute-start | bytes 196616 | tf_op jit(solution)/shard_map/ppermute | solution.py:586
  15.4 5.0 %collective-permute-start.4 = (f32[1,4,8,128]{3,2,1,0:T(8,128)S(1)}, f32[1,4,8,128]{3,2,1,0:T(8,128)S(1)}, u32[]{:S(2)}, u32[]{:S(2)}) collective-permute-start(f32[1,4,8,128]{3,2,1,0:T(8,128)S(1)} %get-tuple-element.51), channel_id=1, source_target_pairs={{0,2},{1,3},{2,0},{3,1},{4,6},{5,7},{6,4},{7,5},{8,10},{9,11},{10,... | collective-permute-start | bytes 49160 | tf_op jit(solution)/shard_map/ppermute | solution.py:586
  20.4 2.8 %collective-permute-start.5 = (f32[2,4,8,128]{3,2,1,0:T(8,128)S(1)}, f32[2,4,8,128]{3,2,1,0:T(8,128)S(1)}, u32[]{:S(2)}, u32[]{:S(2)}) collective-permute-start(f32[2,4,8,128]{3,2,1,0:T(8,128)S(1)} %get-tuple-element.80), channel_id=1, source_target_pairs={{0,1},{1,0},{2,3},{3,2},{4,5},{5,4},{6,7},{7,6},{8,9},{9,8},{10,11... | collective-permute-start | bytes 98312 | tf_op jit(solution)/shard_map/ppermute | solution.py:586
  21.4 3.9 %collective-permute-start.9 = (f32[4,2,4,8,128]{4,3,2,1,0:T(8,128)S(1)}, f32[4,2,4,8,128]{4,3,2,1,0:T(8,128)S(1)}, u32[]{:S(2)}, u32[]{:S(2)}) collective-permute-start(f32[4,2,4,8,128]{4,3,2,1,0:T(8,128)S(1)} %pad_maximum_fusion), channel_id=1, source_target_pairs={{0,8},{1,9},{2,10},{3,11},{4,12},{5,13},{6,14},{7,15},{8,0},{9,1},... | collective-permute-start | bytes 393224 | tf_op jit(solution)/shard_map/ppermute | solution.py:586
  23.2 5.3 %collective-permute-start.6 = (f32[4,4,8,128]{3,2,1,0:T(8,128)S(1)}, f32[4,4,8,128]{3,2,1,0:T(8,128)S(1)}, u32[]{:S(2)}, u32[]{:S(2)}) collective-permute-start(f32[4,4,8,128]{3,2,1,0:T(8,128)S(1)} %pad_maximum_fusion.2), channel_id=1, source_target_pairs={{0,8},{1,9},{2,10},{3,11},{4,12},{5,13},{6,14},{7,15},{8,0},{9,1},... | collective-permute-start | bytes 196616 | tf_op jit(solution)/shard_map/ppermute | solution.py:586
  25.4 4.7 %collective-permute-start.10 = (f32[8,2,4,8,128]{4,3,2,1,0:T(8,128)S(1)}, f32[8,2,4,8,128]{4,3,2,1,0:T(8,128)S(1)}, u32[]{:S(2)}, u32[]{:S(2)}) collective-permute-start(f32[8,2,4,8,128]{4,3,2,1,0:T(8,128)S(1)} %constant_dynamic-update-slice_fusion.6.near), channel_id=1, source_target_pairs={{0,4},{1,5},{2,6},{3,7},{4,0},{5,1},{6,2},{7,3},{8,12},{9,13},{10,... | collective-permute-start | bytes 786440 | tf_op jit(solution)/shard_map/ppermute | solution.py:586
  28.5 3.4 %collective-permute-start.7 = (f32[8,4,8,128]{3,2,1,0:T(8,128)S(1)}, f32[8,4,8,128]{3,2,1,0:T(8,128)S(1)}, u32[]{:S(2)}, u32[]{:S(2)}) collective-permute-start(f32[8,4,8,128]{3,2,1,0:T(8,128)S(1)} %constant_dynamic-update-slice_fusion.2.near), channel_id=1, source_target_pairs={{0,4},{1,5},{2,6},{3,7},{4,0},{5,1},{6,2},{7,3},{8,12},{9,13},{10,... | collective-permute-start | bytes 393224 | tf_op jit(solution)/shard_map/ppermute | solution.py:586

commit v8 on v7

--- a/solution.py
+++ b/solution.py
@@ -35,8 +35,7 @@
     t = x * x
     series = (1.0 - 0.5 * x) + t * (1 / 12 - t * (1 / 720))
     near = t < 0.0625
-    guarded = jnp.where(near, 1.0, x)
-    return jnp.where(near, series, guarded / (jnp.exp(guarded) - 1.0))
+    return jnp.where(near, series, x / (jnp.exp(x) - 1.0))
 
 
 def iota(shape, dim):
@@ -222,8 +221,8 @@
         d_n = (kept[XM, i] + kept[XP, i - 1]) + (ym + down(yp, 1, 0)) + (zm + down(zp, 1, 1))
         d_n = d_n + jnp.where(ends, 0.5 * mob * bernoulli(pot), 0.0) + fld[CAP, i]
         inside = eps > 0.0
-        w_p = jnp.where(inside, OMEGA / jnp.where(inside, d_p, 1.0), 0.0)
-        w_n = jnp.where(inside, OMEGA / jnp.where(inside, d_n, 1.0), 0.0)
+        w_p = jnp.where(inside, OMEGA / d_p, 0.0)
+        w_n = jnp.where(inside, OMEGA / d_n, 0.0)
         kept[W_P, i], kept[W_N, i] = w_p, w_n
         kept[WF_P, i], kept[WF_N, i] = w_p * fld[F_P, i], w_n * fld[F_N, i]
         fld[D_P, i], fld[D_N, i] = d_p, d_n

time: 35.9 us -> 35.8 us (level)
  no operation moved by 1% of the time
where the time goes in v8:
time: 35.8 us; the launch traced here: 35.7 us
  starting transfers between devices  20.3 us (57%)
  Pallas kernels  8.51 us (24%)
  waiting for transfers between devices  5.33 us (15%)
  other arithmetic  0.73 us (2%)
  between operations  0.7 us (2%)
    ppermute x11, starting transfers between devices, permute(): return lax.ppermute(v, ('groups', 'gx', 'gy'), send[name])  20.3 us
    ppermute x11, waiting for transfers between devices, permute(): return lax.ppermute(v, ('groups', 'gx', 'gy'), send[name])  5.33 us
    pallas_call x1, Pallas kernels, per_device(): pl.pallas_call(functools.partial(second_kernel, tuple(bits), y_turn), out...  3.8 us
    pallas_call x1, Pallas kernels, per_device(): pl.pallas_call(functools.partial(operators_kernel, tuple(bits), y_bits),...  1.81 us
    pallas_call x1, Pallas kernels, per_device(): pl.pallas_call(first_kernel, out_shape=[shape(KEPT, total, rows, LANES),...  1.59 us
    pallas_call x1, Pallas kernels, per_device(): pl.pallas_call(rim_y_kernel, out_shape=[shape(2 * planes, by, LANES), sha...  1.24 us
  transfers between devices with their start and end apart: 11, of which 5 were waited for; matrix products, arithmetic and copies ran while one was open for 0% of the time, Pallas kernels for 10%

profile of v8, /device:TPU:1, one launch (start us, length us, event | category | flops | bytes accessed | tf_op | source)
XLA Modules:
  0.0 35.7 jit_solution(9116721554033033921)
XLA Ops:
  0.6 0.7 %pad_maximum_fusion.4 = f32[3,6]{1,0:T(4,128)S(1)} fusion(f32[1,6]{1,0:T(1,128)} %bitcast.7, f32[1,6]{1,0:T(1,128)} %bitcast.8, f32[1,6]{1,0:T(1,128)} %bitcast.9), kind=kLoop, calls=%fused_computation.13 | loop fusion | flops 36 | bytes 144 | tf_op jit(solution)/shard_map/stack | solution.py:593
  1.3 0.1 broadcast_in_dim.2.table
  1.4 1.2 %shard_map.86 = (f32[16,8,128]{2,1,0:T(8,128)S(1)}, f32[16,8,128]{2,1,0:T(8,128)S(1)}, f32[1,2,4,8,128]{4,3,2,1,0:T(8,128)S(1)}, f32[8,16,128]{2,1,0:T(8,128)S(1...) custom-call(f32[3,6,128]{2,1,0:T(8,128)S(1)} %broadcast_in_dim.2.table, ...), custom_call_target="tpu_custom_call" | custom-call | tf_op jit(solution)/shard_map/pallas_call | solution.py:596
  2.7 2.2 %collective-permute-start = (f32[24,8,128]{2,1,0:T(8,128)S(1)}, f32[24,8,128]{2,1,0:T(8,128)S(1)}, u32[]{:S(2)}, u32[]{:S(2)}) collective-permute-start(f32[24,8,128]{2,1,0:T(8,128)S(1)} %pad_maximum_fusion.1), channel_id=1, source_target_pairs={{0,1},{1,0},{2,3},{3,2},{4,5},{5,4},{6,7},{7,6},{8,9},{9,8},{10,11... | collective-permute-start | bytes 294920 | tf_op jit(solution)/shard_map/ppermute | solution.py:585
  4.9 1.0 %collective-permute-start.1 = (f32[16,8,128]{2,1,0:T(8,128)S(1)}, f32[16,8,128]{2,1,0:T(8,128)S(1)}, u32[]{:S(2)}, u32[]{:S(2)}) collective-permute-start(f32[16,8,128]{2,1,0:T(8,128)S(1)} %get-tuple-element.47), channel_id=1, source_target_pairs={{0,4},{1,2},{2,1},{3,7},{4,0},{5,6},{6,5},{7,3},{8,12},{9,10},{10,... | collective-permute-start | bytes 196616 | tf_op jit(solution)/shard_map/ppermute | solution.py:585
  5.8 0.9 %collective-permute-done.1.in_b = f32[16,8,128]{2,1,0:T(8,128)S(1)} collective-permute-done((f32[16,8,128]{2,1,0:T(8,128)S(1)}, f32[16,8,128]{2,1,0:T(8,128)S(1)}, u32[]{:S(2)}, u32[]{:S(2)}) %collective-permute-start.1) | collective-permute-done | bytes 65568 | tf_op jit(solution)/shard_map/ppermute | solution.py:585
  6.7 0.7 %collective-permute-done.in_a = f32[24,8,128]{2,1,0:T(8,128)S(1)} collective-permute-done((f32[24,8,128]{2,1,0:T(8,128)S(1)}, f32[24,8,128]{2,1,0:T(8,128)S(1)}, u32[]{:S(2)}, u32[]{:S(2)}) %collective-permute-start) | collective-permute-done | bytes 98336 | tf_op jit(solution)/shard_map/ppermute | solution.py:585
  7.4 0.1 shard_map.87
  7.4 1.3 %collective-permute-start.2 = (f32[14,24,128]{2,1,0:T(8,128)S(1)}, f32[14,24,128]{2,1,0:T(8,128)S(1)}, u32[]{:S(2)}, u32[]{:S(2)}) collective-permute-start(f32[14,24,128]{2,1,0:T(8,128)S(1)} %get-tuple-element.49), channel_id=1, source_target_pairs={{0,4},{1,5},{2,6},{3,7},{4,0},{5,1},{6,2},{7,3},{8,12},{9,13},{10,... | collective-permute-start | bytes 516104 | tf_op jit(solution)/shard_map/ppermute | solution.py:585
  8.7 1.4 %collective-permute-start.3 = (f32[14,24,128]{2,1,0:T(8,128)S(1)}, f32[14,24,128]{2,1,0:T(8,128)S(1)}, u32[]{:S(2)}, u32[]{:S(2)}) collective-permute-start(f32[14,24,128]{2,1,0:T(8,128)S(1)} %get-tuple-element.50), channel_id=1, source_target_pairs={{0,16},{1,17},{2,18},{3,19},{4,8},{5,9},{6,10},{7,11},{8,4},{9,5},... | collective-permute-start | bytes 516104 | tf_op jit(solution)/shard_map/ppermute | solution.py:585
  10.2 3.6 %collective-permute-start.8 = (f32[2,2,4,8,128]{4,3,2,1,0:T(8,128)S(1)}, f32[2,2,4,8,128]{4,3,2,1,0:T(8,128)S(1)}, u32[]{:S(2)}, u32[]{:S(2)}) collective-permute-start(f32[2,2,4,8,128]{4,3,2,1,0:T(8,128)S(1)} %pad_maximum_fusion.3), channel_id=1, source_target_pairs={{0,2},{1,3},{2,0},{3,1},{4,6},{5,7},{6,4},{7,5},{8,10},{9,11},{10,... | collective-permute-start | bytes 196616 | tf_op jit(solution)/shard_map/ppermute | solution.py:585
  13.8 0.0 collective-permute-done.2.in_a
  13.8 0.0 collective-permute-done.3.in_b
  13.8 1.6 %shard_map.88 = (f32[15,16,24,128]{3,2,1,0:T(8,128)S(1)}, f32[1,4,8,128]{3,2,1,0:T(8,128)S(1)}) custom-call(f32[3,6,128]{2,1,0:T(8,128)S(1)} %broadcast_in_dim.2.table, f32[4,8,24,128]{3,2,1,0:T(8,128)S(1)} %get-tuple-element.48.mid, f32[14,24,128]{2,1,0:T(8,128)S(1)} %collective-permute-done.2.in_a, f32[14,24,128]{2,1,0:T(8,128)S(1)} %collective-permute-done.3.in_b), custom_call_target="tpu_custom_call" | custom-call | tf_op jit(solution)/shard_map/pallas_call | solution.py:626
  15.4 3.8 %collective-permute-start.4 = (f32[1,4,8,128]{3,2,1,0:T(8,128)S(1)}, f32[1,4,8,128]{3,2,1,0:T(8,128)S(1)}, u32[]{:S(2)}, u32[]{:S(2)}) collective-permute-start(f32[1,4,8,128]{3,2,1,0:T(8,128)S(1)} %get-tuple-element.51), channel_id=1, source_target_pairs={{0,2},{1,3},{2,0},{3,1},{4,6},{5,7},{6,4},{7,5},{8,10},{9,11},{10,... | collective-permute-start | bytes 49160 | tf_op jit(solution)/shard_map/ppermute | solution.py:585
  19.3 1.1 %collective-permute-done.4 = f32[1,4,8,128]{3,2,1,0:T(8,128)S(1)} collective-permute-done((f32[1,4,8,128]{3,2,1,0:T(8,128)S(1)}, f32[1,4,8,128]{3,2,1,0:T(8,128)S(1)}, u32[]{:S(2)}, u32[]{:S(2)}) %collective-permute-start.4) | collective-permute-done | bytes 16416 | tf_op jit(solution)/shard_map/ppermute | solution.py:585
  20.4 1.0 %collective-permute-start.5 = (f32[2,4,8,128]{3,2,1,0:T(8,128)S(1)}, f32[2,4,8,128]{3,2,1,0:T(8,128)S(1)}, u32[]{:S(2)}, u32[]{:S(2)}) collective-permute-start(f32[2,4,8,128]{3,2,1,0:T(8,128)S(1)} %get-tuple-element.80), channel_id=1, source_target_pairs={{0,1},{1,0},{2,3},{3,2},{4,5},{5,4},{6,7},{7,6},{8,9},{9,8},{10,11... | collective-permute-start | bytes 98312 | tf_op jit(solution)/shard_map/ppermute | solution.py:585
  21.4 0.0 collective-permute-done.8
  21.4 0.7 %collective-permute-start.9 = (f32[4,2,4,8,128]{4,3,2,1,0:T(8,128)S(1)}, f32[4,2,4,8,128]{4,3,2,1,0:T(8,128)S(1)}, u32[]{:S(2)}, u32[]{:S(2)}) collective-permute-start(f32[4,2,4,8,128]{4,3,2,1,0:T(8,128)S(1)} %pad_maximum_fusion), channel_id=1, source_target_pairs={{0,8},{1,9},{2,10},{3,11},{4,12},{5,13},{6,14},{7,15},{8,0},{9,1},... | collective-permute-start | bytes 393224 | tf_op jit(solution)/shard_map/ppermute | solution.py:585
  22.1 1.0 %collective-permute-done.5 = f32[2,4,8,128]{3,2,1,0:T(8,128)S(1)} collective-permute-done((f32[2,4,8,128]{3,2,1,0:T(8,128)S(1)}, f32[2,4,8,128]{3,2,1,0:T(8,128)S(1)}, u32[]{:S(2)}, u32[]{:S(2)}) %collective-permute-start.5) | collective-permute-done | bytes 32800 | tf_op jit(solution)/shard_map/ppermute | solution.py:585
  23.2 0.6 %collective-permute-start.6 = (f32[4,4,8,128]{3,2,1,0:T(8,128)S(1)}, f32[4,4,8,128]{3,2,1,0:T(8,128)S(1)}, u32[]{:S(2)}, u32[]{:S(2)}) collective-permute-start(f32[4,4,8,128]{3,2,1,0:T(8,128)S(1)} %pad_maximum_fusion.2), channel_id=1, source_target_pairs={{0,8},{1,9},{2,10},{3,11},{4,12},{5,13},{6,14},{7,15},{8,0},{9,1},... | collective-permute-start | bytes 196616 | tf_op jit(solution)/shard_map/ppermute | solution.py:585
  23.8 1.6 %collective-permute-done.9 = f32[4,2,4,8,128]{4,3,2,1,0:T(8,128)S(1)} collective-permute-done((f32[4,2,4,8,128]{4,3,2,1,0:T(8,128)S(1)}, f32[4,2,4,8,128]{4,3,2,1,0:T(8,128)S(1)}, u32[]{:S(2)}, u32[]{:S(2)}) %collective-permute-start.9) | collective-permute-done | bytes 131104 | tf_op jit(solution)/shard_map/ppermute | solution.py:585
  25.4 3.1 %collective-permute-start.10 = (f32[8,2,4,8,128]{4,3,2,1,0:T(8,128)S(1)}, f32[8,2,4,8,128]{4,3,2,1,0:T(8,128)S(1)}, u32[]{:S(2)}, u32[]{:S(2)}) collective-permute-start(f32[8,2,4,8,128]{4,3,2,1,0:T(8,128)S(1)} %constant_dynamic-update-slice_fusion.6.near), channel_id=1, source_target_pairs={{0,4},{1,5},{2,6},{3,7},{4,0},{5,1},{6,2},{7,3},{8,12},{9,13},{10,... | collective-permute-start | bytes 786440 | tf_op jit(solution)/shard_map/ppermute | solution.py:585
  28.5 0.0 collective-permute-done.6
  28.5 1.6 %collective-permute-start.7 = (f32[8,4,8,128]{3,2,1,0:T(8,128)S(1)}, f32[8,4,8,128]{3,2,1,0:T(8,128)S(1)}, u32[]{:S(2)}, u32[]{:S(2)}) collective-permute-start(f32[8,4,8,128]{3,2,1,0:T(8,128)S(1)} %constant_dynamic-update-slice_fusion.2.near), channel_id=1, source_target_pairs={{0,4},{1,5},{2,6},{3,7},{4,0},{5,1},{6,2},{7,3},{8,12},{9,13},{10,... | collective-permute-start | bytes 393224 | tf_op jit(solution)/shard_map/ppermute | solution.py:585
  30.0 0.0 collective-permute-done.10.far
  30.0 1.8 %shard_map.89 = (f32[17,32,128]{2,1,0:T(8,128)S(1)}, f32[17,32,128]{2,1,0:T(8,128)S(1)}, f32[16,32,128]{2,1,0:T(8,128)S(1)}, f32[16,32,128]{2,1,0:T(8,128)S(1)},...) custom-call(f32[8,2,4,8,128]{4,3,2,1,0:T(8,128)S(1)} %constant_dynam, ...), custom_call_target="tpu_custom_call" | custom-call | tf_op jit(solution)/shard_map/pallas_call | solution.py:658
  31.9 0.0 collective-permute-done.7.far
  31.9 3.8 %shard_map.90 = (f32[8,16,128]{2,1,0:T(8,128)}, f32[8,16,128]{2,1,0:T(8,128)}) custom-call(f32[8,4,8,128]{3,2,1,0:T(8,128)S(1)} %constant_dynamic-update-slice_fusion.2.near, f32[8,4,8,128]{3,2,1,0:T(8,128)S(1)} %collective-permute-done.7.far, f32[15,16,24,128]{3,2,1,0:T(8,128)S(1)} %get-tuple-element.52.kept, f32[17,32,128]{2,1,0:T(8,128)S(1)} %get-tuple-element.56.refs_0_, ...), custom_call_target="tpu_custom_call" | custom-call | tf_op jit(solution)/shard_map/pallas_call | solution.py:668
  (12 shorter events, 0.1 us)
Async XLA Ops:
  2.7 4.7 %collective-permute-start = (f32[24,8,128]{2,1,0:T(8,128)S(1)}, f32[24,8,128]{2,1,0:T(8,128)S(1)}, u32[]{:S(2)}, u32[]{:S(2)}) collective-permute-start(f32[24,8,128]{2,1,0:T(8,128)S(1)} %pad_maximum_fusion.1), channel_id=1, source_target_pairs={{0,1},{1,0},{2,3},{3,2},{4,5},{5,4},{6,7},{7,6},{8,9},{9,8},{10,11... | collective-permute-start | bytes 294920 | tf_op jit(solution)/shard_map/ppermute | solution.py:585
  4.9 1.9 %collective-permute-start.1 = (f32[16,8,128]{2,1,0:T(8,128)S(1)}, f32[16,8,128]{2,1,0:T(8,128)S(1)}, u32[]{:S(2)}, u32[]{:S(2)}) collective-permute-start(f32[16,8,128]{2,1,0:T(8,128)S(1)} %get-tuple-element.47), channel_id=1, source_target_pairs={{0,4},{1,2},{2,1},{3,7},{4,0},{5,6},{6,5},{7,3},{8,12},{9,10},{10,... | collective-permute-start | bytes 196616 | tf_op jit(solution)/shard_map/ppermute | solution.py:585
  7.4 6.3 %collective-permute-start.2 = (f32[14,24,128]{2,1,0:T(8,128)S(1)}, f32[14,24,128]{2,1,0:T(8,128)S(1)}, u32[]{:S(2)}, u32[]{:S(2)}) collective-permute-start(f32[14,24,128]{2,1,0:T(8,128)S(1)} %get-tuple-element.49), channel_id=1, source_target_pairs={{0,4},{1,5},{2,6},{3,7},{4,0},{5,1},{6,2},{7,3},{8,12},{9,13},{10,... | collective-permute-start | bytes 516104 | tf_op jit(solution)/shard_map/ppermute | solution.py:585
  8.7 5.1 %collective-permute-start.3 = (f32[14,24,128]{2,1,0:T(8,128)S(1)}, f32[14,24,128]{2,1,0:T(8,128)S(1)}, u32[]{:S(2)}, u32[]{:S(2)}) collective-permute-start(f32[14,24,128]{2,1,0:T(8,128)S(1)} %get-tuple-element.50), channel_id=1, source_target_pairs={{0,16},{1,17},{2,18},{3,19},{4,8},{5,9},{6,10},{7,11},{8,4},{9,5},... | collective-permute-start | bytes 516104 | tf_op jit(solution)/shard_map/ppermute | solution.py:585
  10.2 11.2 %collective-permute-start.8 = (f32[2,2,4,8,128]{4,3,2,1,0:T(8,128)S(1)}, f32[2,2,4,8,128]{4,3,2,1,0:T(8,128)S(1)}, u32[]{:S(2)}, u32[]{:S(2)}) collective-permute-start(f32[2,2,4,8,128]{4,3,2,1,0:T(8,128)S(1)} %pad_maximum_fusion.3), channel_id=1, source_target_pairs={{0,2},{1,3},{2,0},{3,1},{4,6},{5,7},{6,4},{7,5},{8,10},{9,11},{10,... | collective-permute-start | bytes 196616 | tf_op jit(solution)/shard_map/ppermute | solution.py:585
  15.4 5.0 %collective-permute-start.4 = (f32[1,4,8,128]{3,2,1,0:T(8,128)S(1)}, f32[1,4,8,128]{3,2,1,0:T(8,128)S(1)}, u32[]{:S(2)}, u32[]{:S(2)}) collective-permute-start(f32[1,4,8,128]{3,2,1,0:T(8,128)S(1)} %get-tuple-element.51), channel_id=1, source_target_pairs={{0,2},{1,3},{2,0},{3,1},{4,6},{5,7},{6,4},{7,5},{8,10},{9,11},{10,... | collective-permute-start | bytes 49160 | tf_op jit(solution)/shard_map/ppermute | solution.py:585
  20.4 2.8 %collective-permute-start.5 = (f32[2,4,8,128]{3,2,1,0:T(8,128)S(1)}, f32[2,4,8,128]{3,2,1,0:T(8,128)S(1)}, u32[]{:S(2)}, u32[]{:S(2)}) collective-permute-start(f32[2,4,8,128]{3,2,1,0:T(8,128)S(1)} %get-tuple-element.80), channel_id=1, source_target_pairs={{0,1},{1,0},{2,3},{3,2},{4,5},{5,4},{6,7},{7,6},{8,9},{9,8},{10,11... | collective-permute-start | bytes 98312 | tf_op jit(solution)/shard_map/ppermute | solution.py:585
  21.4 3.9 %collective-permute-start.9 = (f32[4,2,4,8,128]{4,3,2,1,0:T(8,128)S(1)}, f32[4,2,4,8,128]{4,3,2,1,0:T(8,128)S(1)}, u32[]{:S(2)}, u32[]{:S(2)}) collective-permute-start(f32[4,2,4,8,128]{4,3,2,1,0:T(8,128)S(1)} %pad_maximum_fusion), channel_id=1, source_target_pairs={{0,8},{1,9},{2,10},{3,11},{4,12},{5,13},{6,14},{7,15},{8,0},{9,1},... | collective-permute-start | bytes 393224 | tf_op jit(solution)/shard_map/ppermute | solution.py:585
  23.2 5.3 %collective-permute-start.6 = (f32[4,4,8,128]{3,2,1,0:T(8,128)S(1)}, f32[4,4,8,128]{3,2,1,0:T(8,128)S(1)}, u32[]{:S(2)}, u32[]{:S(2)}) collective-permute-start(f32[4,4,8,128]{3,2,1,0:T(8,128)S(1)} %pad_maximum_fusion.2), channel_id=1, source_target_pairs={{0,8},{1,9},{2,10},{3,11},{4,12},{5,13},{6,14},{7,15},{8,0},{9,1},... | collective-permute-start | bytes 196616 | tf_op jit(solution)/shard_map/ppermute | solution.py:585
  25.4 4.7 %collective-permute-start.10 = (f32[8,2,4,8,128]{4,3,2,1,0:T(8,128)S(1)}, f32[8,2,4,8,128]{4,3,2,1,0:T(8,128)S(1)}, u32[]{:S(2)}, u32[]{:S(2)}) collective-permute-start(f32[8,2,4,8,128]{4,3,2,1,0:T(8,128)S(1)} %constant_dynamic-update-slice_fusion.6.near), channel_id=1, source_target_pairs={{0,4},{1,5},{2,6},{3,7},{4,0},{5,1},{6,2},{7,3},{8,12},{9,13},{10,... | collective-permute-start | bytes 786440 | tf_op jit(solution)/shard_map/ppermute | solution.py:585
  28.5 3.4 %collective-permute-start.7 = (f32[8,4,8,128]{3,2,1,0:T(8,128)S(1)}, f32[8,4,8,128]{3,2,1,0:T(8,128)S(1)}, u32[]{:S(2)}, u32[]{:S(2)}) collective-permute-start(f32[8,4,8,128]{3,2,1,0:T(8,128)S(1)} %constant_dynamic-update-slice_fusion.2.near), channel_id=1, source_target_pairs={{0,4},{1,5},{2,6},{3,7},{4,0},{5,1},{6,2},{7,3},{8,12},{9,13},{10,... | collective-permute-start | bytes 393224 | tf_op jit(solution)/shard_map/ppermute | solution.py:585

commit v9 on v7

--- a/solution.py
+++ b/solution.py
@@ -104,7 +104,7 @@
             block[0, f, i] = 0.125 * v
 
 
-def rim_x_kernel(cls, pot, fp, fn, in_a, in_b, out, out_a, out_b):
+def rim_x_kernel(cls, pot, fp, fn, in_a, in_b, out, out_a, out_a2, out_b):
     y, ny = lax.axis_index("gy"), lax.axis_size("gy")
     even_x, even_y = lax.axis_index("gx") % 2 == 0, y % 2 == 0
     planes, length = cls.shape[0], cls.shape[1]
@@ -126,7 +126,8 @@
             field = 2 * pair + slot
             at, n = RIM_PLANES[field]
             lo_x, hi_x = out[field, 0:n], out[field, planes - n : planes]
-            out_a[at : at + n] = jnp.where(even_x, hi_x, lo_x)
+            half, start = (out_a, at) if pair == 0 else (out_a2, at - 2 * RIM)
+            half[start : start + n] = jnp.where(even_x, hi_x, lo_x)
             out_b[at : at + n] = jnp.where(even_x, lo_x, hi_x)
 
 
@@ -614,16 +615,16 @@
     b = permute(b, "yb")
     a = permute(jnp.concatenate([a, fields.reshape(-1, by, LANES)]), "ya")
     fields_y = [fields, a[2 * planes :].reshape(fields.shape)]
-    mid, a, b = pl.pallas_call(
+    mid, a, a2, b = pl.pallas_call(
         rim_x_kernel,
-        out_shape=[shape(4, planes, rows, LANES)] + [shape(4 * RIM - 2, rows, LANES)] * 2,
+        out_shape=[shape(4, planes, rows, LANES)] + [shape(k, rows, LANES) for k in (2 * RIM, 2 * RIM - 2, 4 * RIM - 2)],
         in_specs=[VMEM] * 6,
-        out_specs=[VMEM] * 3,
+        out_specs=[VMEM] * 4,
         compiler_params=params(16),
     )(*raw, a, b)
     fields_y, _ = lax.optimization_barrier((jnp.concatenate(fields_y), mid))
     b = permute(b, "xb")
-    a = permute(a, "xa")
+    a = permute(jnp.concatenate([a, a2]), "xa")
     kept, block = pl.pallas_call(
         first_kernel,
         out_shape=[shape(KEPT, total, rows, LANES), shape(1, bx, by, LANES)],

time: 35.9 us -> 35.9 us (level)
  no operation moved by 1% of the time
where the time goes in v9:
time: 35.9 us; the launch traced here: 35.8 us
  starting transfers between devices  20.3 us (57%)
  Pallas kernels  8.59 us (24%)
  waiting for transfers between devices  5.33 us (15%)
  other arithmetic  0.74 us (2%)
  between operations  0.71 us (2%)
    ppermute x11, starting transfers between devices, permute(): return lax.ppermute(v, ('groups', 'gx', 'gy'), send[name])  20.3 us
    ppermute x11, waiting for transfers between devices, permute(): return lax.ppermute(v, ('groups', 'gx', 'gy'), send[name])  5.33 us
    pallas_call x1, Pallas kernels, per_device(): pl.pallas_call(functools.partial(second_kernel, tuple(bits), y_turn), out...  3.8 us
    pallas_call x1, Pallas kernels, per_device(): pl.pallas_call(functools.partial(operators_kernel, tuple(bits), y_bits),...  1.87 us
    pallas_call x1, Pallas kernels, per_device(): pl.pallas_call(first_kernel, out_shape=[shape(KEPT, total, rows, LANES),...  1.61 us
    pallas_call x1, Pallas kernels, per_device(): pl.pallas_call(rim_y_kernel, out_shape=[shape(2 * planes, by, LANES), sha...  1.24 us
  transfers between devices with their start and end apart: 11, of which 5 were waited for; matrix products, arithmetic and copies ran while one was open for 0% of the time, Pallas kernels for 10%

profile of v9, /device:TPU:1, one launch (start us, length us, event | category | flops | bytes accessed | tf_op | source)
XLA Modules:
  0.0 35.8 jit_solution(8058148030047390089)
XLA Ops:
  0.6 0.7 %pad_maximum_fusion.5 = f32[3,6]{1,0:T(4,128)S(1)} fusion(f32[1,6]{1,0:T(1,128)} %bitcast.7, f32[1,6]{1,0:T(1,128)} %bitcast.8, f32[1,6]{1,0:T(1,128)} %bitcast.9), kind=kLoop, calls=%fused_computation.14 | loop fusion | flops 36 | bytes 144 | tf_op jit(solution)/shard_map/stack | solution.py:595
  1.3 0.1 broadcast_in_dim.2.table
  1.4 1.2 %shard_map.86 = (f32[16,8,128]{2,1,0:T(8,128)S(1)}, f32[16,8,128]{2,1,0:T(8,128)S(1)}, f32[1,2,4,8,128]{4,3,2,1,0:T(8,128)S(1)}, f32[8,16,128]{2,1,0:T(8,128)S(1...) custom-call(f32[3,6,128]{2,1,0:T(8,128)S(1)} %broadcast_in_dim.2.table, ...), custom_call_target="tpu_custom_call" | custom-call | tf_op jit(solution)/shard_map/pallas_call | solution.py:598
  2.7 2.2 %collective-permute-start = (f32[24,8,128]{2,1,0:T(8,128)S(1)}, f32[24,8,128]{2,1,0:T(8,128)S(1)}, u32[]{:S(2)}, u32[]{:S(2)}) collective-permute-start(f32[24,8,128]{2,1,0:T(8,128)S(1)} %pad_maximum_fusion.2), channel_id=1, source_target_pairs={{0,1},{1,0},{2,3},{3,2},{4,5},{5,4},{6,7},{7,6},{8,9},{9,8},{10,11... | collective-permute-start | bytes 294920 | tf_op jit(solution)/shard_map/ppermute | solution.py:587
  4.9 1.0 %collective-permute-start.1 = (f32[16,8,128]{2,1,0:T(8,128)S(1)}, f32[16,8,128]{2,1,0:T(8,128)S(1)}, u32[]{:S(2)}, u32[]{:S(2)}) collective-permute-start(f32[16,8,128]{2,1,0:T(8,128)S(1)} %get-tuple-element.48), channel_id=1, source_target_pairs={{0,4},{1,2},{2,1},{3,7},{4,0},{5,6},{6,5},{7,3},{8,12},{9,10},{10,... | collective-permute-start | bytes 196616 | tf_op jit(solution)/shard_map/ppermute | solution.py:587
  5.8 0.9 %collective-permute-done.1.in_b = f32[16,8,128]{2,1,0:T(8,128)S(1)} collective-permute-done((f32[16,8,128]{2,1,0:T(8,128)S(1)}, f32[16,8,128]{2,1,0:T(8,128)S(1)}, u32[]{:S(2)}, u32[]{:S(2)}) %collective-permute-start.1) | collective-permute-done | bytes 65568 | tf_op jit(solution)/shard_map/ppermute | solution.py:587
  6.7 0.7 %collective-permute-done.in_a = f32[24,8,128]{2,1,0:T(8,128)S(1)} collective-permute-done((f32[24,8,128]{2,1,0:T(8,128)S(1)}, f32[24,8,128]{2,1,0:T(8,128)S(1)}, u32[]{:S(2)}, u32[]{:S(2)}) %collective-permute-start) | collective-permute-done | bytes 98336 | tf_op jit(solution)/shard_map/ppermute | solution.py:587
  7.4 0.1 shard_map.87
  7.5 1.3 %collective-permute-start.2 = (f32[14,24,128]{2,1,0:T(8,128)S(1)}, f32[14,24,128]{2,1,0:T(8,128)S(1)}, u32[]{:S(2)}, u32[]{:S(2)}) collective-permute-start(f32[14,24,128]{2,1,0:T(8,128)S(1)} %pad_maximum_fusion), channel_id=1, source_target_pairs={{0,4},{1,5},{2,6},{3,7},{4,0},{5,1},{6,2},{7,3},{8,12},{9,13},{10,... | collective-permute-start | bytes 516104 | tf_op jit(solution)/shard_map/ppermute | solution.py:587
  8.8 1.4 %collective-permute-start.3 = (f32[14,24,128]{2,1,0:T(8,128)S(1)}, f32[14,24,128]{2,1,0:T(8,128)S(1)}, u32[]{:S(2)}, u32[]{:S(2)}) collective-permute-start(f32[14,24,128]{2,1,0:T(8,128)S(1)} %get-tuple-element.52), channel_id=1, source_target_pairs={{0,16},{1,17},{2,18},{3,19},{4,8},{5,9},{6,10},{7,11},{8,4},{9,5},... | collective-permute-start | bytes 516104 | tf_op jit(solution)/shard_map/ppermute | solution.py:587
  10.2 3.6 %collective-permute-start.8 = (f32[2,2,4,8,128]{4,3,2,1,0:T(8,128)S(1)}, f32[2,2,4,8,128]{4,3,2,1,0:T(8,128)S(1)}, u32[]{:S(2)}, u32[]{:S(2)}) collective-permute-start(f32[2,2,4,8,128]{4,3,2,1,0:T(8,128)S(1)} %pad_maximum_fusion.4), channel_id=1, source_target_pairs={{0,2},{1,3},{2,0},{3,1},{4,6},{5,7},{6,4},{7,5},{8,10},{9,11},{10,... | collective-permute-start | bytes 196616 | tf_op jit(solution)/shard_map/ppermute | solution.py:587
  13.8 0.0 collective-permute-done.2.in_a
  13.8 0.0 collective-permute-done.3.in_b
  13.9 1.6 %shard_map.88 = (f32[15,16,24,128]{3,2,1,0:T(8,128)S(1)}, f32[1,4,8,128]{3,2,1,0:T(8,128)S(1)}) custom-call(f32[3,6,128]{2,1,0:T(8,128)S(1)} %broadcast_in_dim.2.table, f32[4,8,24,128]{3,2,1,0:T(8,128)S(1)} %get-tuple-element.49.mid, f32[14,24,128]{2,1,0:T(8,128)S(1)} %collective-permute-done.2.in_a, f32[14,24,128]{2,1,0:T(8,128)S(1)} %collective-permute-done.3.in_b), custom_call_target="tpu_custom_call" | custom-call | tf_op jit(solution)/shard_map/pallas_call | solution.py:628
  15.5 3.8 %collective-permute-start.4 = (f32[1,4,8,128]{3,2,1,0:T(8,128)S(1)}, f32[1,4,8,128]{3,2,1,0:T(8,128)S(1)}, u32[]{:S(2)}, u32[]{:S(2)}) collective-permute-start(f32[1,4,8,128]{3,2,1,0:T(8,128)S(1)} %get-tuple-element.53), channel_id=1, source_target_pairs={{0,2},{1,3},{2,0},{3,1},{4,6},{5,7},{6,4},{7,5},{8,10},{9,11},{10,... | collective-permute-start | bytes 49160 | tf_op jit(solution)/shard_map/ppermute | solution.py:587
  19.3 1.1 %collective-permute-done.4 = f32[1,4,8,128]{3,2,1,0:T(8,128)S(1)} collective-permute-done((f32[1,4,8,128]{3,2,1,0:T(8,128)S(1)}, f32[1,4,8,128]{3,2,1,0:T(8,128)S(1)}, u32[]{:S(2)}, u32[]{:S(2)}) %collective-permute-start.4) | collective-permute-done | bytes 16416 | tf_op jit(solution)/shard_map/ppermute | solution.py:587
  20.4 1.0 %collective-permute-start.5 = (f32[2,4,8,128]{3,2,1,0:T(8,128)S(1)}, f32[2,4,8,128]{3,2,1,0:T(8,128)S(1)}, u32[]{:S(2)}, u32[]{:S(2)}) collective-permute-start(f32[2,4,8,128]{3,2,1,0:T(8,128)S(1)} %get-tuple-element.82), channel_id=1, source_target_pairs={{0,1},{1,0},{2,3},{3,2},{4,5},{5,4},{6,7},{7,6},{8,9},{9,8},{10,11... | collective-permute-start | bytes 98312 | tf_op jit(solution)/shard_map/ppermute | solution.py:587
  21.4 0.0 collective-permute-done.8
  21.5 0.7 %collective-permute-start.9 = (f32[4,2,4,8,128]{4,3,2,1,0:T(8,128)S(1)}, f32[4,2,4,8,128]{4,3,2,1,0:T(8,128)S(1)}, u32[]{:S(2)}, u32[]{:S(2)}) collective-permute-start(f32[4,2,4,8,128]{4,3,2,1,0:T(8,128)S(1)} %pad_maximum_fusion.1), channel_id=1, source_target_pairs={{0,8},{1,9},{2,10},{3,11},{4,12},{5,13},{6,14},{7,15},{8,0},{9,1},... | collective-permute-start | bytes 393224 | tf_op jit(solution)/shard_map/ppermute | solution.py:587
  22.2 1.0 %collective-permute-done.5 = f32[2,4,8,128]{3,2,1,0:T(8,128)S(1)} collective-permute-done((f32[2,4,8,128]{3,2,1,0:T(8,128)S(1)}, f32[2,4,8,128]{3,2,1,0:T(8,128)S(1)}, u32[]{:S(2)}, u32[]{:S(2)}) %collective-permute-start.5) | collective-permute-done | bytes 32800 | tf_op jit(solution)/shard_map/ppermute | solution.py:587
  23.2 0.6 %collective-permute-start.6 = (f32[4,4,8,128]{3,2,1,0:T(8,128)S(1)}, f32[4,4,8,128]{3,2,1,0:T(8,128)S(1)}, u32[]{:S(2)}, u32[]{:S(2)}) collective-permute-start(f32[4,4,8,128]{3,2,1,0:T(8,128)S(1)} %pad_maximum_fusion.3), channel_id=1, source_target_pairs={{0,8},{1,9},{2,10},{3,11},{4,12},{5,13},{6,14},{7,15},{8,0},{9,1},... | collective-permute-start | bytes 196616 | tf_op jit(solution)/shard_map/ppermute | solution.py:587
  23.8 1.6 %collective-permute-done.9 = f32[4,2,4,8,128]{4,3,2,1,0:T(8,128)S(1)} collective-permute-done((f32[4,2,4,8,128]{4,3,2,1,0:T(8,128)S(1)}, f32[4,2,4,8,128]{4,3,2,1,0:T(8,128)S(1)}, u32[]{:S(2)}, u32[]{:S(2)}) %collective-permute-start.9) | collective-permute-done | bytes 131104 | tf_op jit(solution)/shard_map/ppermute | solution.py:587
  25.4 3.1 %collective-permute-start.10 = (f32[8,2,4,8,128]{4,3,2,1,0:T(8,128)S(1)}, f32[8,2,4,8,128]{4,3,2,1,0:T(8,128)S(1)}, u32[]{:S(2)}, u32[]{:S(2)}) collective-permute-start(f32[8,2,4,8,128]{4,3,2,1,0:T(8,128)S(1)} %constant_dynamic-update-slice_fusion.6.near), channel_id=1, source_target_pairs={{0,4},{1,5},{2,6},{3,7},{4,0},{5,1},{6,2},{7,3},{8,12},{9,13},{10,... | collective-permute-start | bytes 786440 | tf_op jit(solution)/shard_map/ppermute | solution.py:587
  28.5 0.0 collective-permute-done.6
  28.5 1.6 %collective-permute-start.7 = (f32[8,4,8,128]{3,2,1,0:T(8,128)S(1)}, f32[8,4,8,128]{3,2,1,0:T(8,128)S(1)}, u32[]{:S(2)}, u32[]{:S(2)}) collective-permute-start(f32[8,4,8,128]{3,2,1,0:T(8,128)S(1)} %constant_dynamic-update-slice_fusion.2.near), channel_id=1, source_target_pairs={{0,4},{1,5},{2,6},{3,7},{4,0},{5,1},{6,2},{7,3},{8,12},{9,13},{10,... | collective-permute-start | bytes 393224 | tf_op jit(solution)/shard_map/ppermute | solution.py:587
  30.1 0.0 collective-permute-done.10.far
  30.1 1.9 %shard_map.89 = (f32[17,32,128]{2,1,0:T(8,128)S(1)}, f32[17,32,128]{2,1,0:T(8,128)S(1)}, f32[16,32,128]{2,1,0:T(8,128)S(1)}, f32[16,32,128]{2,1,0:T(8,128)S(1)},...) custom-call(f32[8,2,4,8,128]{4,3,2,1,0:T(8,128)S(1)} %constant_dynam, ...), custom_call_target="tpu_custom_call" | custom-call | tf_op jit(solution)/shard_map/pallas_call | solution.py:660
  31.9 0.0 collective-permute-done.7.far
  32.0 3.8 %shard_map.90 = (f32[8,16,128]{2,1,0:T(8,128)}, f32[8,16,128]{2,1,0:T(8,128)}) custom-call(f32[8,4,8,128]{3,2,1,0:T(8,128)S(1)} %constant_dynamic-update-slice_fusion.2.near, f32[8,4,8,128]{3,2,1,0:T(8,128)S(1)} %collective-permute-done.7.far, f32[15,16,24,128]{3,2,1,0:T(8,128)S(1)} %get-tuple-element.54.kept, f32[17,32,128]{2,1,0:T(8,128)S(1)} %get-tuple-element.58.refs_0_, ...), custom_call_target="tpu_custom_call" | custom-call | tf_op jit(solution)/shard_map/pallas_call | solution.py:670
  (13 shorter events, 0.1 us)
Async XLA Ops:
  2.7 4.7 %collective-permute-start = (f32[24,8,128]{2,1,0:T(8,128)S(1)}, f32[24,8,128]{2,1,0:T(8,128)S(1)}, u32[]{:S(2)}, u32[]{:S(2)}) collective-permute-start(f32[24,8,128]{2,1,0:T(8,128)S(1)} %pad_maximum_fusion.2), channel_id=1, source_target_pairs={{0,1},{1,0},{2,3},{3,2},{4,5},{5,4},{6,7},{7,6},{8,9},{9,8},{10,11... | collective-permute-start | bytes 294920 | tf_op jit(solution)/shard_map/ppermute | solution.py:587
  4.9 1.9 %collective-permute-start.1 = (f32[16,8,128]{2,1,0:T(8,128)S(1)}, f32[16,8,128]{2,1,0:T(8,128)S(1)}, u32[]{:S(2)}, u32[]{:S(2)}) collective-permute-start(f32[16,8,128]{2,1,0:T(8,128)S(1)} %get-tuple-element.48), channel_id=1, source_target_pairs={{0,4},{1,2},{2,1},{3,7},{4,0},{5,6},{6,5},{7,3},{8,12},{9,10},{10,... | collective-permute-start | bytes 196616 | tf_op jit(solution)/shard_map/ppermute | solution.py:587
  7.5 6.3 %collective-permute-start.2 = (f32[14,24,128]{2,1,0:T(8,128)S(1)}, f32[14,24,128]{2,1,0:T(8,128)S(1)}, u32[]{:S(2)}, u32[]{:S(2)}) collective-permute-start(f32[14,24,128]{2,1,0:T(8,128)S(1)} %pad_maximum_fusion), channel_id=1, source_target_pairs={{0,4},{1,5},{2,6},{3,7},{4,0},{5,1},{6,2},{7,3},{8,12},{9,13},{10,... | collective-permute-start | bytes 516104 | tf_op jit(solution)/shard_map/ppermute | solution.py:587
  8.8 5.1 %collective-permute-start.3 = (f32[14,24,128]{2,1,0:T(8,128)S(1)}, f32[14,24,128]{2,1,0:T(8,128)S(1)}, u32[]{:S(2)}, u32[]{:S(2)}) collective-permute-start(f32[14,24,128]{2,1,0:T(8,128)S(1)} %get-tuple-element.52), channel_id=1, source_target_pairs={{0,16},{1,17},{2,18},{3,19},{4,8},{5,9},{6,10},{7,11},{8,4},{9,5},... | collective-permute-start | bytes 516104 | tf_op jit(solution)/shard_map/ppermute | solution.py:587
  10.2 11.2 %collective-permute-start.8 = (f32[2,2,4,8,128]{4,3,2,1,0:T(8,128)S(1)}, f32[2,2,4,8,128]{4,3,2,1,0:T(8,128)S(1)}, u32[]{:S(2)}, u32[]{:S(2)}) collective-permute-start(f32[2,2,4,8,128]{4,3,2,1,0:T(8,128)S(1)} %pad_maximum_fusion.4), channel_id=1, source_target_pairs={{0,2},{1,3},{2,0},{3,1},{4,6},{5,7},{6,4},{7,5},{8,10},{9,11},{10,... | collective-permute-start | bytes 196616 | tf_op jit(solution)/shard_map/ppermute | solution.py:587
  15.5 5.0 %collective-permute-start.4 = (f32[1,4,8,128]{3,2,1,0:T(8,128)S(1)}, f32[1,4,8,128]{3,2,1,0:T(8,128)S(1)}, u32[]{:S(2)}, u32[]{:S(2)}) collective-permute-start(f32[1,4,8,128]{3,2,1,0:T(8,128)S(1)} %get-tuple-element.53), channel_id=1, source_target_pairs={{0,2},{1,3},{2,0},{3,1},{4,6},{5,7},{6,4},{7,5},{8,10},{9,11},{10,... | collective-permute-start | bytes 49160 | tf_op jit(solution)/shard_map/ppermute | solution.py:587
  20.4 2.8 %collective-permute-start.5 = (f32[2,4,8,128]{3,2,1,0:T(8,128)S(1)}, f32[2,4,8,128]{3,2,1,0:T(8,128)S(1)}, u32[]{:S(2)}, u32[]{:S(2)}) collective-permute-start(f32[2,4,8,128]{3,2,1,0:T(8,128)S(1)} %get-tuple-element.82), channel_id=1, source_target_pairs={{0,1},{1,0},{2,3},{3,2},{4,5},{5,4},{6,7},{7,6},{8,9},{9,8},{10,11... | collective-permute-start | bytes 98312 | tf_op jit(solution)/shard_map/ppermute | solution.py:587
  21.5 3.9 %collective-permute-start.9 = (f32[4,2,4,8,128]{4,3,2,1,0:T(8,128)S(1)}, f32[4,2,4,8,128]{4,3,2,1,0:T(8,128)S(1)}, u32[]{:S(2)}, u32[]{:S(2)}) collective-permute-start(f32[4,2,4,8,128]{4,3,2,1,0:T(8,128)S(1)} %pad_maximum_fusion.1), channel_id=1, source_target_pairs={{0,8},{1,9},{2,10},{3,11},{4,12},{5,13},{6,14},{7,15},{8,0},{9,1},... | collective-permute-start | bytes 393224 | tf_op jit(solution)/shard_map/ppermute | solution.py:587
  23.2 5.3 %collective-permute-start.6 = (f32[4,4,8,128]{3,2,1,0:T(8,128)S(1)}, f32[4,4,8,128]{3,2,1,0:T(8,128)S(1)}, u32[]{:S(2)}, u32[]{:S(2)}) collective-permute-start(f32[4,4,8,128]{3,2,1,0:T(8,128)S(1)} %pad_maximum_fusion.3), channel_id=1, source_target_pairs={{0,8},{1,9},{2,10},{3,11},{4,12},{5,13},{6,14},{7,15},{8,0},{9,1},... | collective-permute-start | bytes 196616 | tf_op jit(solution)/shard_map/ppermute | solution.py:587
  25.4 4.7 %collective-permute-start.10 = (f32[8,2,4,8,128]{4,3,2,1,0:T(8,128)S(1)}, f32[8,2,4,8,128]{4,3,2,1,0:T(8,128)S(1)}, u32[]{:S(2)}, u32[]{:S(2)}) collective-permute-start(f32[8,2,4,8,128]{4,3,2,1,0:T(8,128)S(1)} %constant_dynamic-update-slice_fusion.6.near), channel_id=1, source_target_pairs={{0,4},{1,5},{2,6},{3,7},{4,0},{5,1},{6,2},{7,3},{8,12},{9,13},{10,... | collective-permute-start | bytes 786440 | tf_op jit(solution)/shard_map/ppermute | solution.py:587
  28.5 3.4 %collective-permute-start.7 = (f32[8,4,8,128]{3,2,1,0:T(8,128)S(1)}, f32[8,4,8,128]{3,2,1,0:T(8,128)S(1)}, u32[]{:S(2)}, u32[]{:S(2)}) collective-permute-start(f32[8,4,8,128]{3,2,1,0:T(8,128)S(1)} %constant_dynamic-update-slice_fusion.2.near), channel_id=1, source_target_pairs={{0,4},{1,5},{2,6},{3,7},{4,0},{5,1},{6,2},{7,3},{8,12},{9,13},{10,... | collective-permute-start | bytes 393224 | tf_op jit(solution)/shard_map/ppermute | solution.py:587
